TPU v7x, 32 devices: a whole 2x2x4 slice. The times are simulated.
32 devices in a mesh: groups: 2 (over y), stripe: 8 (over z, x), exp: 2 (over core).
Axes of the slice: x: 2, y: 2, z: 4, core: 2. Of those that a mesh axis runs over, the one named last changes fastest.
Arguments:
- template: float32 [256, 2048], P(('groups', 'stripe'), 'exp'), parts along dimension 0, may hold values from -6 to 6
- exposure: float32 [4, 128, 2048], P(('groups', 'exp'), 'stripe'), parts along dimension 0, may hold values from -30 to 30
- cosmic_mask: int32 [4, 128, 2048], P(('groups', 'exp'), 'stripe'), parts along dimension 0, may hold values 0 or 1
- stamp_blocks: int32 [16, 16], P(('groups', 'stripe')), parts along dimension 0, may hold values from 0 to 31, as said below
- row_filters: float32 [19, 19], replicated, may hold values from -1 to 2.5
- col_filters: float32 [19, 19], replicated, may hold values from -1 to 2.5
Outputs:
- filtered: float32 [4, 128, 2048], P(('groups', 'exp'), 'stripe'), parts along dimension 0
- coefficients: float32 [4, 64], P(('groups', 'exp')), parts along dimension 0
There are 2 independent parts, one for each index of `groups`. A program takes and returns all parts, laid end to end along the dimension named above; an argument that names none is the same for every part. Nothing has to cross between parts.
Inputs may be any that keep to these rules, and one draw needn't show every extreme that they name: `stamp_blocks`: each row lists the stamps of one stripe; stamp j lies in column block 2 j or 2 j + 1.
All inputs are finite; a program needn't handle non-finite values. No bound on the sum of `cosmic_mask` on one device may be relied on, other than what follows from the above.
Results may differ from a plain program's by a relative error of at most 0.0003.
Values sent between devices are 32-bit elements; how exact they have to be, the bound alone decides.
No kernel may reach another device: no remote copies, remote signals or barrier semaphores. Data moves between devices by JAX's collectives and lax.ppermute only.
A program may use at most 64 MiB of HBM per device.

v0:
```python
import functools

import jax
import jax.numpy as jnp
from jax import lax
from jax.experimental import pallas as pl
from jax.experimental.pallas import tpu as pltpu
from jax.sharding import PartitionSpec as P

HALF = 9
TAPS = 2 * HALF + 1
BASES = 19
STAMP_W = 64
LANES = 128
BASE_PAD = 24
BACK = 7
FIT_ROWS = 3 * BASE_PAD + BACK + 1
REACH = HALF + 1
GROUP = 32
GROUPS_TILE = LANES // GROUP
MAIN_TILES = 5
MAIN = MAIN_TILES * LANES
DEPTH = MAIN + LANES
EXTRA_ROWS = 80
F32 = jnp.float32
BF16 = jnp.bfloat16


def lane_id(rows):
    return lax.broadcasted_iota(jnp.int32, (rows, LANES), 1)


def row_id(rows):
    return lax.broadcasted_iota(jnp.int32, (rows, LANES), 0)


def split_two(values):
    high = values.astype(BF16)
    low = (values - high.astype(F32)).astype(BF16)
    return high, low


def position(index, total):
    return (2.0 * index.astype(F32) + 1.0) / total - 1.0


def even_stripe():
    return lax.rem(lax.axis_index("stripe"), 2) == 0


def edge_kernel(cores, *refs):
    pieces = refs[:cores]
    science_ref, good_ref, near_ref, far_ref, ext = refs[cores:]
    rows, half = pieces[0].shape
    wide = science_ref.shape[2]
    me = lax.axis_index("exp")
    for step in range(cores):
        start = lax.rem(me + step, cores) * half
        ext[:, pl.ds(pl.multiple_of(start, LANES), half)] = pieces[step][...]
    fold = wide // 2
    low_first = rows - 8

    def edge(first, extra, outer):
        parts = [ext[first : first + 8, :fold], ext[first : first + 8, fold:]]
        tail = []
        for line in (extra, extra + 1):
            tail += [ext[line : line + 1, :fold], ext[line : line + 1, fold:]]
        science = science_ref[0, outer : outer + 1, :]
        good = good_ref[0, outer : outer + 1, :].astype(F32)
        for line in (science, good):
            tail += [line[:, :fold], line[:, fold:]]
        return jnp.concatenate(parts + tail, axis=0)

    bottom = edge(low_first, rows - REACH, rows - 1)
    top = edge(0, 8, 0)
    even = even_stripe()
    near_ref[...] = jnp.where(even, bottom, top)
    far_ref[...] = jnp.where(even, top, bottom)


def weight_kernel(row_ref, col_ref, high_ref, low_ref, base_ref, pad):
    pad[...] = jnp.zeros_like(pad)
    pad[0, 0:BASES, 0:TAPS] = row_ref[...]
    pad[1, 0:BASES, 0:TAPS] = col_ref[...]
    row = pad[0]
    lane = lane_id(BASE_PAD)
    spot = lax.rem(lane, GROUP)
    group = lane // GROUP
    tiled = row
    for part in range(1, GROUPS_TILE):
        tiled = tiled + pltpu.roll(row, part * GROUP, 1)
    columns = [
        jnp.broadcast_to(pad[1, :, tap : tap + 1], (BASE_PAD, LANES)) for tap in range(TAPS)
    ]
    zero = jnp.zeros((BASE_PAD, LANES), F32)
    mains = []
    for tile in range(MAIN_TILES):
        spread = zero
        for part in range(GROUPS_TILE):
            tap = tile * GROUPS_TILE + part
            if tap < TAPS:
                spread = jnp.where(group == part, columns[tap], spread)
        mains.append(tiled * spread)
    spread = zero
    for tap in range(TAPS):
        spread = jnp.where(lane // 4 == tap, columns[tap], spread)
    corner = lax.rem(lane, 4)

    def tap_at(tap):
        return jnp.broadcast_to(pad[0, :, tap : tap + 1], (BASE_PAD, LANES))

    outer = jnp.where(
        corner == 0,
        tap_at(0),
        jnp.where(corner == 1, tap_at(1), jnp.where(corner == 2, tap_at(TAPS - 2), tap_at(TAPS - 1))),
    )
    inner = jnp.where(corner == 1, tap_at(0), jnp.where(corner == 2, tap_at(TAPS - 1), 0.0))
    outer = outer * spread
    inner = inner * spread
    for tile in range(MAIN_TILES):
        base_ref[:, tile * LANES : (tile + 1) * LANES] = mains[tile]
    base_ref[:, MAIN : MAIN + LANES] = outer
    base_ref[:, MAIN + LANES :] = inner
    rows = high_ref.shape[0] // BASE_PAD
    for line in range(rows):
        tap = spot - (line - 1)
        inside = (tap >= 0) & (tap < TAPS)
        tiles = [
            jnp.where(inside, pltpu.roll(main, (line - 1) % LANES, 1), 0.0) for main in mains
        ]
        if line == 0:
            tiles.append(jnp.where(corner < 2, inner, 0.0))
        elif line == rows - 1:
            tiles.append(jnp.where(corner >= 2, inner, 0.0))
        else:
            tiles.append(zero)
        high, low = split_two(jnp.concatenate(tiles, axis=1))
        where = pl.ds(line * BASE_PAD, BASE_PAD)
        high_ref[where, :] = high.astype(F32)
        low_ref[where, :] = low.astype(F32)


def fill_extended(ext, cores, pieces, near_ref, far_ref):
    rows, half = pieces[0].shape
    wide = half * cores
    fold = wide // 2
    ext[:, 0:LANES] = jnp.zeros((ext.shape[0], LANES), F32)
    ext[:, LANES + wide :] = jnp.zeros((ext.shape[0], LANES), F32)
    me = lax.axis_index("exp")
    for step in range(cores):
        start = lax.rem(me + step, cores) * half + LANES
        ext[8 : 8 + rows, pl.ds(pl.multiple_of(start, LANES), half)] = pieces[step][...]
    even = even_stripe()
    near = near_ref[...]
    far = far_ref[...]
    top = jnp.where(even, far, near)
    bottom = jnp.where(even, near, far)
    for side in range(2):
        where = pl.ds(LANES + side * fold, fold)
        ext[0:8, where] = top[8 * side : 8 * side + 8]
        ext[8 + rows : 16 + rows, where] = bottom[8 * side : 8 * side + 8]
        spare = [
            top[16 + side : 17 + side],
            top[18 + side : 19 + side],
            bottom[16 + side : 17 + side],
            bottom[18 + side : 19 + side],
        ]
        ext[16 + rows : 24 + rows, where] = jnp.concatenate(spare + spare, axis=0)
    return top, bottom


def spread_window(shifted, put):
    for tap in range(TAPS):
        put(tap * GROUP, shifted(tap, slice(0, GROUP)))
    extra = slice(GROUP, GROUP + 8)
    early = row_id(8) < 4
    for quad in range(MAIN_TILES):
        lines = [shifted(4 * quad + part, extra) for part in range(4)]
        put(
            MAIN + 16 * quad,
            jnp.concatenate(
                [jnp.where(early, lines[0], lines[1]), jnp.where(early, lines[2], lines[3])], axis=0
            ),
        )


def clear_spare(tile_refs, columns):
    for ref in tile_refs:
        ref[TAPS * GROUP : MAIN, columns] = jnp.zeros((MAIN - TAPS * GROUP, LANES), BF16)
        ref[MAIN + EXTRA_ROWS :, columns] = jnp.zeros((LANES - EXTRA_ROWS, LANES), BF16)


def back_profile(horiz):
    steady = jnp.ones_like(horiz)
    square = 0.5 * (3.0 * horiz * horiz - 1.0)
    return [steady, horiz, steady, horiz, square, steady, horiz]


def fit_kernel(cores, stripes, stamps_ref, *refs):
    pieces = refs[:cores]
    near_ref, far_ref, science_ref, good_ref, high_ref, low_ref, out_ref, ext, xhigh, xlow = refs[cores:]
    rows = pieces[0].shape[0]
    wide = science_ref.shape[2]
    pairs = wide // (4 * STAMP_W)
    fill_extended(ext, cores, pieces, near_ref, far_ref)
    lane = lane_id(1)
    lane_ext = lane_id(ext.shape[0])
    first_row = lax.axis_index("stripe") * rows

    def odd_of(stamp):
        return lax.rem(stamps_ref[0, stamp], 2)

    def window(stamp, offset):
        odd = odd_of(stamp)
        left = ext[:, stamp * LANES : (stamp + 1) * LANES]
        centre = ext[:, (stamp + 1) * LANES : (stamp + 2) * LANES]
        right = ext[:, (stamp + 2) * LANES : (stamp + 3) * LANES]
        taken = jnp.where(
            odd == 1,
            jnp.where(lane_ext < HALF, right, centre),
            jnp.where(lane_ext >= LANES - HALF, left, centre),
        )
        amount = jnp.where(odd == 1, HALF + STAMP_W, HALF) + offset
        return pltpu.roll(taken, lax.rem(amount, LANES), 1)

    def picked(values, stamp, offset):
        return pltpu.roll(values, odd_of(stamp) * STAMP_W + offset, 1)

    total = jnp.zeros((FIT_ROWS, FIT_ROWS), F32)
    chunk = 2
    for start in range(0, pairs, chunk):
        for pair in range(start, start + chunk):
            first = window(2 * pair, 0)
            second = window(2 * pair + 1, STAMP_W)
            columns = slice(pair * LANES, (pair + 1) * LANES)

            def shifted(tap, lines):
                back = (LANES - tap) % LANES
                a = first[lines]
                b = second[lines]
                if back:
                    a = pltpu.roll(a, back, 1)
                    b = pltpu.roll(b, back, 1)
                return jnp.where(lane_id(a.shape[0]) < STAMP_W, a, b)

            def put(place, values):
                high, low = split_two(values)
                xhigh[place : place + values.shape[0], columns] = high
                xlow[place : place + values.shape[0], columns] = low

            spread_window(shifted, put)
            clear_spare((xhigh, xlow), columns)
        span = slice(start * LANES, (start + chunk) * LANES)
        weights_high = high_ref[...].astype(BF16)
        weights_low = low_ref[...].astype(BF16)
        bases = (
            jnp.dot(weights_high, xhigh[:, span], preferred_element_type=F32)
            + jnp.dot(weights_low, xhigh[:, span], preferred_element_type=F32)
            + jnp.dot(weights_high, xlow[:, span], preferred_element_type=F32)
        )
        horiz_parts, science_parts, good_parts = [], [], []
        for pair in range(start, start + chunk):
            low_half = lane < STAMP_W
            block = jnp.where(low_half, stamps_ref[0, 2 * pair], stamps_ref[0, 2 * pair + 1] - 1)
            horiz_parts.append(position(block * STAMP_W + lane, wide))
            for source, parts in ((science_ref, science_parts), (good_ref, good_parts)):
                a = source[0, :, 2 * pair * LANES : (2 * pair + 1) * LANES].astype(F32)
                b = source[0, :, (2 * pair + 1) * LANES : (2 * pair + 2) * LANES].astype(F32)
                a = picked(a, 2 * pair, 0)
                b = picked(b, 2 * pair + 1, STAMP_W)
                parts.append(jnp.where(lane_id(rows) < STAMP_W, a, b))
        horiz = jnp.concatenate(horiz_parts, axis=1)
        good = jnp.concatenate(good_parts, axis=1)
        target = good * jnp.concatenate(science_parts, axis=1)
        profile = jnp.concatenate(back_profile(horiz), axis=0)
        for line in range(rows):
            keep = good[line : line + 1]
            own = bases[line * BASE_PAD : (line + 1) * BASE_PAD] * keep
            vert = position(jnp.full((1, chunk * LANES), first_row + line, jnp.int32), rows * stripes)
            square = 0.5 * (3.0 * vert * vert - 1.0)
            steady = jnp.ones_like(vert)
            scale = jnp.concatenate([steady, steady, vert, vert, steady, square, square], axis=0)
            ground = profile * scale * keep
            design = jnp.concatenate(
                [own, own * horiz, own * vert, ground, target[line : line + 1]], axis=0
            ).astype(BF16)
            total = total + lax.dot_general(
                design, design, (((1,), (1,)), ((), ())), preferred_element_type=F32
            )
    out_ref[...] = jnp.concatenate(
        [total, jnp.zeros((FIT_ROWS, LANES - FIT_ROWS), F32)], axis=1
    )


def pivots():
    return [t * BASE_PAD + b for t in range(3) for b in range(BASES)] + [
        3 * BASE_PAD + m for m in range(BACK)
    ]


def solve_rows(matrix):
    line = row_id(FIT_ROWS)
    lane = lane_id(FIT_ROWS)
    used = (line >= 3 * BASE_PAD) | (lax.rem(line, BASE_PAD) < BASES)
    matrix = jnp.where((line == lane) & ~used, 1.0, matrix)
    for pivot in pivots():
        column = jnp.broadcast_to(matrix[:, pivot : pivot + 1], (FIT_ROWS, LANES))
        row = matrix[pivot : pivot + 1] / column[pivot : pivot + 1]
        matrix = matrix - jnp.where(line == pivot, 0.0, column) * row
    right = jnp.broadcast_to(matrix[:, FIT_ROWS - 1 : FIT_ROWS], (FIT_ROWS, LANES))
    diagonal = jnp.sum(jnp.where(line == lane, matrix, 0.0), axis=1, keepdims=True)
    return right / jnp.broadcast_to(diagonal, (FIT_ROWS, LANES))


def model_kernel(cores, stripes, normal_ref, *refs):
    pieces = refs[:cores]
    near_ref, far_ref, science_ref, good_ref, base_ref, out_ref, coef_ref, ext, xhigh, xlow = refs[cores:]
    rows = pieces[0].shape[0]
    wide = science_ref.shape[2]
    fold = wide // 2
    top, bottom = fill_extended(ext, cores, pieces, near_ref, far_ref)
    tiles = wide // LANES
    lane_ext = lane_id(ext.shape[0])
    for tile in range(tiles):
        columns = slice(tile * LANES, (tile + 1) * LANES)
        left = ext[:, tile * LANES : (tile + 1) * LANES]
        centre = ext[:, (tile + 1) * LANES : (tile + 2) * LANES]
        right = ext[:, (tile + 2) * LANES : (tile + 3) * LANES]

        def shifted(tap, lines):
            move = HALF - tap
            middle = centre[lines]
            if move == 0:
                return middle
            where = lane_ext[lines]
            if move > 0:
                mixed = jnp.where(where >= LANES - move, left[lines], middle)
            else:
                mixed = jnp.where(where < -move, right[lines], middle)
            return pltpu.roll(mixed, move % LANES, 1)

        def put(place, values):
            high, low = split_two(values)
            xhigh[place : place + values.shape[0], columns] = high
            xlow[place : place + values.shape[0], columns] = low

        spread_window(shifted, put)
        clear_spare((xhigh, xlow), columns)

    coef = solve_rows(normal_ref[...])
    lane = lane_id(FIT_ROWS)
    home = jnp.where(
        lane < 3 * BASES, lax.rem(lane, 3) * BASE_PAD + lane // 3, lane + 3 * (BASE_PAD - BASES)
    )
    flat = jnp.sum(jnp.where(row_id(FIT_ROWS) == home, coef, 0.0), axis=0, keepdims=True)
    coef_ref[...] = flat[:, : coef_ref.shape[1]]

    line = row_id(BASE_PAD)
    lane = lane_id(BASE_PAD)
    spot = lax.rem(lane, GROUP)
    shift = jnp.where(line == rows + 1, -2, line - 1)
    tap = spot - shift
    inside = (tap >= 0) & (tap < TAPS)
    corner = lax.rem(lane, 4)
    blocks = []
    for term in range(3):
        share = coef[term * BASE_PAD : (term + 1) * BASE_PAD]
        parts = []
        for tile in range(MAIN_TILES + 2):
            mixed = base_ref[:, tile * LANES : (tile + 1) * LANES] * share
            parts.append(jnp.broadcast_to(jnp.sum(mixed, axis=0, keepdims=True), (BASE_PAD, LANES)))
        wanted = []
        for tile in range(MAIN_TILES):
            moved = jnp.concatenate(
                [
                    pltpu.roll(
                        pltpu.roll(parts[tile][:8], (start - 1) % LANES, 1), 0, 1, stride=1, stride_axis=0
                    )
                    for start in range(0, BASE_PAD, 8)
                ],
                axis=0,
            )
            moved = jnp.where(line == rows + 1, pltpu.roll(parts[tile], LANES - 2, 1), moved)
            wanted.append(jnp.where(inside, moved, 0.0))
        outer, inner = parts[MAIN_TILES], parts[MAIN_TILES + 1]
        spare = jnp.where((line == rows + 1) & (corner < 2), outer, 0.0)
        spare = jnp.where((line == 0) & (corner < 2), inner, spare)
        spare = jnp.where((line == rows - 1) & (corner >= 2), inner, spare)
        spare = jnp.where((line == rows) & (corner >= 2), outer, spare)
        wanted.append(spare)
        blocks.append(jnp.concatenate(wanted, axis=1))
    kernel_high, kernel_low = split_two(jnp.concatenate(blocks, axis=0))
    level = [coef[3 * BASE_PAD + m : 3 * BASE_PAD + m + 1, 0:1] for m in range(BACK)]
    first_row = lax.axis_index("stripe") * rows
    vert_line = jnp.where(line == rows + 1, -1, line)
    vert = position(first_row + vert_line, rows * stripes)[:, 0:1]
    vert_square = 0.5 * (3.0 * vert * vert - 1.0)
    chunk = min(4 * LANES, wide)
    outs = []
    for start in range(0, wide, chunk):
        span = slice(start, start + chunk)
        sums = (
            jnp.dot(kernel_high, xhigh[:, span], preferred_element_type=F32)
            + jnp.dot(kernel_low, xhigh[:, span], preferred_element_type=F32)
            + jnp.dot(kernel_high, xlow[:, span], preferred_element_type=F32)
        )
        horiz = position(start + lax.broadcasted_iota(jnp.int32, (1, chunk), 1), wide)
        horiz_square = 0.5 * (3.0 * horiz * horiz - 1.0)
        model = (
            sums[:BASE_PAD]
            + horiz * sums[BASE_PAD : 2 * BASE_PAD]
            + vert * sums[2 * BASE_PAD :]
            + (level[0] + level[1] * horiz + level[4] * horiz_square)
            + vert * (level[2] + level[3] * horiz)
            + vert_square * (level[5] + level[6] * horiz)
        )
        outs.append(model)
    model = jnp.concatenate(outs, axis=1)
    own = good_ref[0].astype(F32) * (science_ref[0] - model[:rows])

    def halo(edge, spot):
        science = jnp.concatenate([edge[20:21], edge[21:22]], axis=1)
        good = jnp.concatenate([edge[22:23], edge[23:24]], axis=1)
        return good * (science - model[spot : spot + 1])

    above_row = halo(top, rows + 1)
    below_row = halo(bottom, rows)
    lines = lax.broadcasted_iota(jnp.int32, (rows, wide), 0)
    spots = lax.broadcasted_iota(jnp.int32, (rows, wide), 1)
    above = jnp.where(lines == 0, above_row, pltpu.roll(own, 1, 0))
    below = jnp.where(lines == rows - 1, below_row, pltpu.roll(own, rows - 1, 0))
    before = jnp.where(spots == 0, 0.0, pltpu.roll(own, 1, 1))
    after = jnp.where(spots == wide - 1, 0.0, pltpu.roll(own, wide - 1, 1))
    out_ref[0] = 4.0 * own - (below + above + after + before)


def whole_vmem(count):
    return [pl.BlockSpec(memory_space=pltpu.VMEM)] * count


def summed(values, axis):
    count = lax.axis_size(axis)
    if count & (count - 1):
        return lax.psum(values, axis)
    step = 1
    while step < count:
        values = values + lax.ppermute(values, axis, [(i, i ^ step) for i in range(count)])
        step *= 2
    return values


def shards(template, exposure, cosmic_mask, stamp_blocks, row_filters, col_filters):
    rows, half = template.shape
    wide = exposure.shape[2]
    cores = lax.axis_size("exp")
    stripes = lax.axis_size("stripe")
    params = pltpu.CompilerParams(vmem_limit_bytes=48 * 1024 * 1024)
    pieces = [template] + [
        lax.ppermute(template, "exp", [((i + step) % cores, i) for i in range(cores)])
        for step in range(1, cores)
    ]
    edge_shape = jax.ShapeDtypeStruct((24, wide // 2), F32)
    near, far = pl.pallas_call(
        functools.partial(edge_kernel, cores),
        out_shape=(edge_shape, edge_shape),
        in_specs=whole_vmem(cores + 2),
        out_specs=tuple(whole_vmem(2)),
        scratch_shapes=[pltpu.VMEM((rows, wide), F32)],
        compiler_params=params,
        name="edges",
    )(*pieces, exposure, cosmic_mask)
    near_pairs = [(i, i + 1) for i in range(0, stripes - 1, 2)]
    far_pairs = [(i, i + 1) for i in range(1, stripes - 1, 2)]

    def swapped(values, couples):
        return lax.ppermute(values, "stripe", couples + [(b, a) for a, b in couples])

    near = swapped(near, near_pairs)
    far = swapped(far, far_pairs)
    weight_shape = jax.ShapeDtypeStruct((rows * BASE_PAD, DEPTH), F32)
    high, low, base = pl.pallas_call(
        weight_kernel,
        out_shape=(
            weight_shape,
            weight_shape,
            jax.ShapeDtypeStruct((BASE_PAD, DEPTH + LANES), F32),
        ),
        in_specs=whole_vmem(2),
        out_specs=tuple(whole_vmem(3)),
        scratch_shapes=[pltpu.VMEM((2, BASE_PAD, LANES), F32)],
        compiler_params=params,
        name="weights",
    )(row_filters, col_filters)
    ext_shape = pltpu.VMEM((rows + 24, wide + 2 * LANES), F32)
    normal = pl.pallas_call(
        functools.partial(fit_kernel, cores, stripes),
        out_shape=jax.ShapeDtypeStruct((FIT_ROWS, LANES), F32),
        in_specs=[pl.BlockSpec(memory_space=pltpu.SMEM)] + whole_vmem(cores + 6),
        out_specs=pl.BlockSpec(memory_space=pltpu.VMEM),
        scratch_shapes=[
            ext_shape,
            pltpu.VMEM((DEPTH, wide // 2), BF16),
            pltpu.VMEM((DEPTH, wide // 2), BF16),
        ],
        compiler_params=params,
        name="fit",
    )(stamp_blocks, *pieces, near, far, exposure, cosmic_mask, high, low)
    normal = summed(normal, "stripe")
    filtered, coef = pl.pallas_call(
        functools.partial(model_kernel, cores, stripes),
        out_shape=(
            jax.ShapeDtypeStruct(exposure.shape, F32),
            jax.ShapeDtypeStruct((1, 3 * BASES + BACK), F32),
        ),
        in_specs=whole_vmem(cores + 6),
        out_specs=tuple(whole_vmem(2)),
        scratch_shapes=[
            ext_shape,
            pltpu.VMEM((DEPTH, wide), BF16),
            pltpu.VMEM((DEPTH, wide), BF16),
        ],
        compiler_params=params,
        name="model",
    )(normal, *pieces, near, far, exposure, cosmic_mask, base)
    return filtered, coef


def solution(mesh):
    placed = (
        P(("groups", "stripe"), "exp"),
        P(("groups", "exp"), "stripe", None),
        P(("groups", "exp"), "stripe", None),
        P(("groups", "stripe"), None),
        P(),
        P(),
    )
    return jax.shard_map(
        shards,
        mesh=mesh,
        in_specs=placed,
        out_specs=(P(("groups", "exp"), "stripe", None), P(("groups", "exp"), None)),
        check_vma=False,
    )
```

profile of v0, /device:TPU:0, one launch (start us, length us, event | category | flops | bytes accessed | tf_op | source)
XLA Modules:
  0.0 42.4 jit_solution(7089990304949006334)
XLA Ops:
  0.6 0.5 %collective-permute-start = (f32[16,1024]{1,0:T(8,128)}, f32[16,1024]{1,0:T(8,128)S(1)}, u32[]{:S(2)}, u32[]{:S(2)}) collective-permute-start(f32[16,1024]{1,0:T(8,128)} %refs_0_.5), channel_id=1, source_target_pairs={{1,0},{0,1},{3,2},{2,3},{5,4},{4,5},{7,6},{6,7},{9,8},{8,9},{11,10... | collective-permute-start | bytes 196616 | tf_op jit(solution)/shard_map/ppermute | solution.py:459
  1.1 1.1 %collective-permute-done.refs_1_ = f32[16,1024]{1,0:T(8,128)S(1)} collective-permute-done((f32[16,1024]{1,0:T(8,128)}, f32[16,1024]{1,0:T(8,128)S(1)}, u32[]{:S(2)}, u32[]{:S(2)}) %collective-permute-start) | collective-permute-done | bytes 65568 | tf_op jit(solution)/shard_map/ppermute | solution.py:459
  2.3 0.0 copy-start
  2.3 0.9 %copy-done = f32[1,16,2048]{2,1,0:T(8,128)S(1)} copy-done((f32[1,16,2048]{2,1,0:T(8,128)S(1)}, f32[1,16,2048]{2,1,0:T(8,128)}, u32[]{:S(2)}) %copy-start) | copy-done | bytes 131096
  3.2 0.0 copy-start.1
  3.2 0.9 %copy-done.1 = s32[1,16,2048]{2,1,0:T(8,128)S(1)} copy-done((s32[1,16,2048]{2,1,0:T(8,128)S(1)}, s32[1,16,2048]{2,1,0:T(8,128)}, u32[]{:S(2)}) %copy-start.1) | copy-done | bytes 131096
  4.1 0.0 copy-start.2
  4.1 0.8 %copy-done.2 = f32[16,1024]{1,0:T(8,128)S(1)} copy-done((f32[16,1024]{1,0:T(8,128)S(1)}, f32[16,1024]{1,0:T(8,128)}, u32[]{:S(2)}) %copy-start.2) | copy-done | bytes 65560
  4.9 0.1 edges.1
  5.0 2.9 %collective-permute-start.1 = (f32[24,1024]{1,0:T(8,128)S(1)}, f32[24,1024]{1,0:T(8,128)S(1)}, u32[]{:S(2)}, u32[]{:S(2)}) collective-permute-start(f32[24,1024]{1,0:T(8,128)S(1)} %get-tuple-element.7), channel_id=1, source_target_pairs={{0,2},{4,6},{8,10},{12,14},{2,0},{6,4},{10,8},{14,12},{1,3},{5,7},... | collective-permute-start | bytes 294920 | tf_op jit(solution)/shard_map/ppermute | solution.py:476
  7.9 0.7 %collective-permute-start.2 = (f32[24,1024]{1,0:T(8,128)S(1)}, f32[24,1024]{1,0:T(8,128)S(1)}, u32[]{:S(2)}, u32[]{:S(2)}) collective-permute-start(f32[24,1024]{1,0:T(8,128)S(1)} %get-tuple-element.8), channel_id=1, source_target_pairs={{2,4},{6,8},{10,12},{4,2},{8,6},{12,10},{3,5},{7,9},{11,13},{5,3},... | collective-permute-start | bytes 294920 | tf_op jit(solution)/shard_map/ppermute | solution.py:476
  8.6 0.0 copy-start.4
  8.6 0.7 %copy-done.4 = f32[19,19]{1,0:T(8,128)S(1)} copy-done((f32[19,19]{1,0:T(8,128)S(1)}, f32[19,19]{1,0:T(8,128)}, u32[]{:S(2)}) %copy-start.4) | copy-done | bytes 1468
  9.3 0.0 copy-start.5
  9.3 0.7 %copy-done.5 = f32[19,19]{1,0:T(8,128)S(1)} copy-done((f32[19,19]{1,0:T(8,128)S(1)}, f32[19,19]{1,0:T(8,128)}, u32[]{:S(2)}) %copy-start.5) | copy-done | bytes 1468
  10.0 0.5 %weights.1 = (f32[384,768]{1,0:T(8,128)S(1)}, f32[384,768]{1,0:T(8,128)S(1)}, f32[24,896]{1,0:T(8,128)S(1)}) custom-call(f32[19,19]{1,0:T(8,128)S(1)} %copy-done.4, f32[19,19]{1,0:T(8,128)S(1)} %copy-done.5), custom_call_target="tpu_custom_call" | custom-call | tf_op jit(solution)/shard_map/weights/pallas_call | solution.py:481
  10.4 0.6 %collective-permute-done.1.refs_2_ = f32[24,1024]{1,0:T(8,128)S(1)} collective-permute-done((f32[24,1024]{1,0:T(8,128)S(1)}, f32[24,1024]{1,0:T(8,128)S(1)}, u32[]{:S(2)}, u32[]{:S(2)}) %collective-permute-start.1) | collective-permute-done | bytes 98336 | tf_op jit(solution)/shard_map/ppermute | solution.py:476
  11.0 0.0 collective-permute-done.2.refs_3_
  11.0 0.0 copy-start.3
  11.0 0.8 %copy-done.3 = f32[16,1024]{1,0:T(8,128)S(1)} copy-done((f32[16,1024]{1,0:T(8,128)S(1)}, f32[16,1024]{1,0:T(8,128)}, u32[]{:S(2)}) %copy-start.3) | copy-done | bytes 65560
  11.9 0.0 copy-start.6
  11.9 0.7 %copy-done.6 = s32[1,16]{1,0:T(1,128)S(1)} copy-done((s32[1,16]{1,0:T(1,128)S(1)}, s32[1,16]{1,0:T(1,128)}, u32[]{:S(2)}) %copy-start.6) | copy-done | bytes 88
  12.5 4.3 %fit.1 = f32[80,128]{1,0:T(8,128)S(1)} custom-call(s32[1,16]{1,0:T(1,128)S(1)} %copy-done.6, f32[16,1024]{1,0:T(8,128)S(1)} %copy-done.3, f32[16,1024]{1,0:T(8,128)S(1)} %collective-permute-done.refs_1_, f32[24,1024]{1,0:T(8,128)S(1)} %collective-permute-done.1.refs_2_, f32[24,1024]{1,0:T(8,128)S(1)} %collective-permute-done.2.refs_3_, ...), custom_call_target="tpu_custom_call" | custom-call | tf_op jit(solution)/shard_map/fit/pallas_call | solution.py:495
  16.8 4.7 %collective-permute-start.3 = (f32[80,128]{1,0:T(8,128)S(1)}, f32[80,128]{1,0:T(8,128)S(1)}, u32[]{:S(2)}, u32[]{:S(2)}) collective-permute-start(f32[80,128]{1,0:T(8,128)S(1)} %fit.1), channel_id=1, source_target_pairs={{0,2},{2,0},{4,6},{6,4},{8,10},{10,8},{12,14},{14,12},{1,3},{3,1},... | collective-permute-start | bytes 122888 | tf_op jit(solution)/shard_map/ppermute | solution.py:447
  21.6 2.0 %collective-permute-done.3 = f32[80,128]{1,0:T(8,128)S(1)} collective-permute-done((f32[80,128]{1,0:T(8,128)S(1)}, f32[80,128]{1,0:T(8,128)S(1)}, u32[]{:S(2)}, u32[]{:S(2)}) %collective-permute-start.3) | collective-permute-done | bytes 40992 | tf_op jit(solution)/shard_map/ppermute | solution.py:447
  23.5 3.2 %collective-permute-start.4 = (f32[80,128]{1,0:T(8,128)S(1)}, f32[80,128]{1,0:T(8,128)S(1)}, u32[]{:S(2)}, u32[]{:S(2)}) collective-permute-start(f32[80,128]{1,0:T(8,128)S(1)} %add.9), channel_id=1, source_target_pairs={{0,4},{2,6},{4,0},{6,2},{8,12},{10,14},{12,8},{14,10},{1,5},{3,7},... | collective-permute-start | bytes 122888 | tf_op jit(solution)/shard_map/ppermute | solution.py:447
  26.8 2.0 %collective-permute-done.4 = f32[80,128]{1,0:T(8,128)S(1)} collective-permute-done((f32[80,128]{1,0:T(8,128)S(1)}, f32[80,128]{1,0:T(8,128)S(1)}, u32[]{:S(2)}, u32[]{:S(2)}) %collective-permute-start.4) | collective-permute-done | bytes 40992 | tf_op jit(solution)/shard_map/ppermute | solution.py:447
  28.8 3.0 %collective-permute-start.5 = (f32[80,128]{1,0:T(8,128)S(1)}, f32[80,128]{1,0:T(8,128)S(1)}, u32[]{:S(2)}, u32[]{:S(2)}) collective-permute-start(f32[80,128]{1,0:T(8,128)S(1)} %add.10), channel_id=1, source_target_pairs={{0,8},{2,10},{4,12},{6,14},{8,0},{10,2},{12,4},{14,6},{1,9},{3,11}... | collective-permute-start | bytes 122888 | tf_op jit(solution)/shard_map/ppermute | solution.py:447
  31.8 2.0 %collective-permute-done.5 = f32[80,128]{1,0:T(8,128)S(1)} collective-permute-done((f32[80,128]{1,0:T(8,128)S(1)}, f32[80,128]{1,0:T(8,128)S(1)}, u32[]{:S(2)}, u32[]{:S(2)}) %collective-permute-start.5) | collective-permute-done | bytes 40992 | tf_op jit(solution)/shard_map/ppermute | solution.py:447
  33.8 8.7 %model.1 = (f32[1,16,2048]{2,1,0:T(8,128)}, f32[1,64]{1,0:T(1,128)}) custom-call(f32[80,128]{1,0:T(8,128)S(1)} %add.11.normal_ref, f32[16,1024]{1,0:T(8,128)S(1)} %copy-done.3, f32[16,1024]{1,0:T(8,128)S(1)} %collective-permute-done.refs_1_, f32[24,1024]{1,0:T(8,128)S(1)} %collective-permute-done.1.refs_2_, f32[24,1024]{1,0:T(8,128)S(1)} %collective-permute-done.2.refs_3_, ...), custom_call_target="tpu_custom_call" | custom-call | tf_op jit(solution)/shard_map/model/pallas_call | solution.py:509
  (3 shorter events, 0.0 us)
Async XLA Ops:
  0.6 1.6 %collective-permute-start = (f32[16,1024]{1,0:T(8,128)}, f32[16,1024]{1,0:T(8,128)S(1)}, u32[]{:S(2)}, u32[]{:S(2)}) collective-permute-start(f32[16,1024]{1,0:T(8,128)} %refs_0_.5), channel_id=1, source_target_pairs={{1,0},{0,1},{3,2},{2,3},{5,4},{4,5},{7,6},{6,7},{9,8},{8,9},{11,10... | collective-permute-start | bytes 196616 | tf_op jit(solution)/shard_map/ppermute | solution.py:459
  2.3 0.9 %copy-start = (f32[1,16,2048]{2,1,0:T(8,128)S(1)}, f32[1,16,2048]{2,1,0:T(8,128)}, u32[]{:S(2)}) copy-start(f32[1,16,2048]{2,1,0:T(8,128)} %refs_4_.3) | copy-start | bytes 393220
  3.2 0.9 %copy-start.1 = (s32[1,16,2048]{2,1,0:T(8,128)S(1)}, s32[1,16,2048]{2,1,0:T(8,128)}, u32[]{:S(2)}) copy-start(s32[1,16,2048]{2,1,0:T(8,128)} %refs_5_.3) | copy-start | bytes 393220
  4.1 0.8 %copy-start.2 = (f32[16,1024]{1,0:T(8,128)S(1)}, f32[16,1024]{1,0:T(8,128)}, u32[]{:S(2)}) copy-start(f32[16,1024]{1,0:T(8,128)} %refs_0_.5) | copy-start | bytes 196612
  5.0 6.0 %collective-permute-start.1 = (f32[24,1024]{1,0:T(8,128)S(1)}, f32[24,1024]{1,0:T(8,128)S(1)}, u32[]{:S(2)}, u32[]{:S(2)}) collective-permute-start(f32[24,1024]{1,0:T(8,128)S(1)} %get-tuple-element.7), channel_id=1, source_target_pairs={{0,2},{4,6},{8,10},{12,14},{2,0},{6,4},{10,8},{14,12},{1,3},{5,7},... | collective-permute-start | bytes 294920 | tf_op jit(solution)/shard_map/ppermute | solution.py:476
  7.9 3.1 %collective-permute-start.2 = (f32[24,1024]{1,0:T(8,128)S(1)}, f32[24,1024]{1,0:T(8,128)S(1)}, u32[]{:S(2)}, u32[]{:S(2)}) collective-permute-start(f32[24,1024]{1,0:T(8,128)S(1)} %get-tuple-element.8), channel_id=1, source_target_pairs={{2,4},{6,8},{10,12},{4,2},{8,6},{12,10},{3,5},{7,9},{11,13},{5,3},... | collective-permute-start | bytes 294920 | tf_op jit(solution)/shard_map/ppermute | solution.py:476
  8.6 0.7 %copy-start.4 = (f32[19,19]{1,0:T(8,128)S(1)}, f32[19,19]{1,0:T(8,128)}, u32[]{:S(2)}) copy-start(f32[19,19]{1,0:T(8,128)} %row_ref.1) | copy-start | bytes 4336
  9.3 0.7 %copy-start.5 = (f32[19,19]{1,0:T(8,128)S(1)}, f32[19,19]{1,0:T(8,128)}, u32[]{:S(2)}) copy-start(f32[19,19]{1,0:T(8,128)} %col_ref.1) | copy-start | bytes 4336
  11.0 0.8 %copy-start.3 = (f32[16,1024]{1,0:T(8,128)S(1)}, f32[16,1024]{1,0:T(8,128)}, u32[]{:S(2)}) copy-start(f32[16,1024]{1,0:T(8,128)} %refs_0_.5) | copy-start | bytes 196612
  11.9 0.7 %copy-start.6 = (s32[1,16]{1,0:T(1,128)S(1)}, s32[1,16]{1,0:T(1,128)}, u32[]{:S(2)}) copy-start(s32[1,16]{1,0:T(1,128)} %stamps_ref.1) | copy-start | bytes 196
  16.8 6.7 %collective-permute-start.3 = (f32[80,128]{1,0:T(8,128)S(1)}, f32[80,128]{1,0:T(8,128)S(1)}, u32[]{:S(2)}, u32[]{:S(2)}) collective-permute-start(f32[80,128]{1,0:T(8,128)S(1)} %fit.1), channel_id=1, source_target_pairs={{0,2},{2,0},{4,6},{6,4},{8,10},{10,8},{12,14},{14,12},{1,3},{3,1},... | collective-permute-start | bytes 122888 | tf_op jit(solution)/shard_map/ppermute | solution.py:447
  23.5 5.2 %collective-permute-start.4 = (f32[80,128]{1,0:T(8,128)S(1)}, f32[80,128]{1,0:T(8,128)S(1)}, u32[]{:S(2)}, u32[]{:S(2)}) collective-permute-start(f32[80,128]{1,0:T(8,128)S(1)} %add.9), channel_id=1, source_target_pairs={{0,4},{2,6},{4,0},{6,2},{8,12},{10,14},{12,8},{14,10},{1,5},{3,7},... | collective-permute-start | bytes 122888 | tf_op jit(solution)/shard_map/ppermute | solution.py:447
  28.8 5.0 %collective-permute-start.5 = (f32[80,128]{1,0:T(8,128)S(1)}, f32[80,128]{1,0:T(8,128)S(1)}, u32[]{:S(2)}, u32[]{:S(2)}) collective-permute-start(f32[80,128]{1,0:T(8,128)S(1)} %add.10), channel_id=1, source_target_pairs={{0,8},{2,10},{4,12},{6,14},{8,0},{10,2},{12,4},{14,6},{1,9},{3,11}... | collective-permute-start | bytes 122888 | tf_op jit(solution)/shard_map/ppermute | solution.py:447
where the time goes:
time: 42.8 us; the launch traced here: 42.4 us
  starting transfers between devices  15.1 us (35%)
  Pallas kernels  13.5 us (32%)
  waiting for transfers between devices  7.61 us (18%)
  local copies, waits for them, and re-layouts  5.55 us (13%)
  between operations  0.68 us (2%)
    ppermute x3, starting transfers between devices, summed(): lax.ppermute(values, axis, [(i, i ^ step) for i in range(count)])  11 us
    pallas_call x1, Pallas kernels, shards(): pl.pallas_call(functools.partial(model_kernel, cores, stripes), out_shape...  8.66 us
    ppermute x3, waiting for transfers between devices, summed(): lax.ppermute(values, axis, [(i, i ^ step) for i in range(count)])  5.94 us
    unnamed x14, local copies, waits for them, and re-layouts  5.55 us
    pallas_call x1, Pallas kernels, shards(): pl.pallas_call(functools.partial(fit_kernel, cores, stripes), out_shape=j...  4.33 us
    ppermute x2, starting transfers between devices, swapped(): lax.ppermute(values, 'stripe', couples + [(b, a) for a, b in couples])  3.56 us
    ppermute x1, waiting for transfers between devices, shards(): lax.ppermute(template, 'exp', [((i + step) % cores, i) for i in range(cor...  1.11 us
  transfers between devices with their start and end apart: 6, of which 5 were waited for; matrix products, arithmetic and copies ran while one was open for 0% of the time, Pallas kernels for 1%

commit v1 on v0

--- a/solution.py
+++ b/solution.py
@@ -66,7 +66,7 @@
         for line in (extra, extra + 1):
             tail += [ext[line : line + 1, :fold], ext[line : line + 1, fold:]]
         science = science_ref[0, outer : outer + 1, :]
-        good = good_ref[0, outer : outer + 1, :].astype(F32)
+        good = good_ref[0, outer : outer + 1, :]
         for line in (science, good):
             tail += [line[:, :fold], line[:, fold:]]
         return jnp.concatenate(parts + tail, axis=0)
@@ -78,8 +78,53 @@
     far_ref[...] = jnp.where(even, top, bottom)
 
 
-def weight_kernel(row_ref, col_ref, high_ref, low_ref, base_ref, pad):
+def load_kernel(
+    template_hbm,
+    science_hbm,
+    good_hbm,
+    stamps_hbm,
+    row_hbm,
+    col_hbm,
+    template_ref,
+    science_ref,
+    good_ref,
+    odd_ref,
+    high_ref,
+    low_ref,
+    base_ref,
+    pad,
+    row_ref,
+    col_ref,
+    mask_ref,
+    stamps_ref,
+    sems,
+):
+    moves = [
+        pltpu.make_async_copy(source, target, sems.at[spot])
+        for spot, (source, target) in enumerate(
+            [
+                (row_hbm, row_ref),
+                (col_hbm, col_ref),
+                (template_hbm, template_ref),
+                (stamps_hbm, stamps_ref),
+                (good_hbm, mask_ref),
+                (science_hbm, science_ref),
+            ]
+        )
+    ]
+    for move in moves:
+        move.start()
     pad[...] = jnp.zeros_like(pad)
+    for move in moves:
+        move.wait()
+    good_ref[...] = mask_ref[...].astype(F32)
+    odd_ref[...] = jnp.concatenate(
+        [
+            jnp.full((1, LANES), lax.rem(stamps_ref[0, stamp], 2), jnp.int32)
+            for stamp in range(odd_ref.shape[0])
+        ],
+        axis=0,
+    )
     pad[0, 0:BASES, 0:TAPS] = row_ref[...]
     pad[1, 0:BASES, 0:TAPS] = col_ref[...]
     row = pad[0]
@@ -122,7 +167,8 @@
     base_ref[:, MAIN : MAIN + LANES] = outer
     base_ref[:, MAIN + LANES :] = inner
     rows = high_ref.shape[0] // BASE_PAD
-    for line in range(rows):
+
+    def line_weights(line):
         tap = spot - (line - 1)
         inside = (tap >= 0) & (tap < TAPS)
         tiles = [
@@ -134,13 +180,24 @@
             tiles.append(jnp.where(corner >= 2, inner, 0.0))
         else:
             tiles.append(zero)
-        high, low = split_two(jnp.concatenate(tiles, axis=1))
-        where = pl.ds(line * BASE_PAD, BASE_PAD)
-        high_ref[where, :] = high.astype(F32)
-        low_ref[where, :] = low.astype(F32)
-
-
-def fill_extended(ext, cores, pieces, near_ref, far_ref):
+        return jnp.concatenate(tiles, axis=1)
+
+    for line in range(0, rows, 2):
+        both = jnp.concatenate([line_weights(line), line_weights(line + 1)], axis=0)
+        high, low = split_two(both)
+        where = pl.ds(line * BASE_PAD, 2 * BASE_PAD)
+        high_ref[where, :] = high
+        low_ref[where, :] = low
+
+
+def edges_of(near_ref, far_ref):
+    even = even_stripe()
+    near = near_ref[...]
+    far = far_ref[...]
+    return jnp.where(even, far, near), jnp.where(even, near, far)
+
+
+def fill_extended(ext, highs, lows, cores, pieces, near_ref, far_ref):
     rows, half = pieces[0].shape
     wide = half * cores
     fold = wide // 2
@@ -150,11 +207,7 @@
     for step in range(cores):
         start = lax.rem(me + step, cores) * half + LANES
         ext[8 : 8 + rows, pl.ds(pl.multiple_of(start, LANES), half)] = pieces[step][...]
-    even = even_stripe()
-    near = near_ref[...]
-    far = far_ref[...]
-    top = jnp.where(even, far, near)
-    bottom = jnp.where(even, near, far)
+    top, bottom = edges_of(near_ref, far_ref)
     for side in range(2):
         where = pl.ds(LANES + side * fold, fold)
         ext[0:8, where] = top[8 * side : 8 * side + 8]
@@ -166,28 +219,30 @@
             bottom[18 + side : 19 + side],
         ]
         ext[16 + rows : 24 + rows, where] = jnp.concatenate(spare + spare, axis=0)
-    return top, bottom
+    main = slice(0, GROUP)
+    highs[main], lows[main] = split_two(ext[main])
+    extra = ext[GROUP : GROUP + 8]
+    span = extra.shape[1]
+    early = lax.broadcasted_iota(jnp.int32, extra.shape, 0) < 4
+    ahead = [extra] + [pltpu.roll(extra, span - part, 1) for part in range(1, 4)]
+    lines = jnp.concatenate(
+        [jnp.where(early, ahead[0], ahead[1]), jnp.where(early, ahead[2], ahead[3])], axis=0
+    )
+    highs[GROUP:], lows[GROUP:] = split_two(lines)
 
 
 def spread_window(shifted, put):
     for tap in range(TAPS):
         put(tap * GROUP, shifted(tap, slice(0, GROUP)))
-    extra = slice(GROUP, GROUP + 8)
-    early = row_id(8) < 4
     for quad in range(MAIN_TILES):
-        lines = [shifted(4 * quad + part, extra) for part in range(4)]
-        put(
-            MAIN + 16 * quad,
-            jnp.concatenate(
-                [jnp.where(early, lines[0], lines[1]), jnp.where(early, lines[2], lines[3])], axis=0
-            ),
-        )
-
-
-def clear_spare(tile_refs, columns):
-    for ref in tile_refs:
-        ref[TAPS * GROUP : MAIN, columns] = jnp.zeros((MAIN - TAPS * GROUP, LANES), BF16)
-        ref[MAIN + EXTRA_ROWS :, columns] = jnp.zeros((LANES - EXTRA_ROWS, LANES), BF16)
+        put(MAIN + 16 * quad, shifted(4 * quad, slice(GROUP, GROUP + 16)))
+
+
+def clear_spare(refs):
+    for ref in refs:
+        wide = ref.shape[1]
+        ref[TAPS * GROUP : MAIN] = jnp.zeros((MAIN - TAPS * GROUP, wide), BF16)
+        ref[MAIN + EXTRA_ROWS :] = jnp.zeros((LANES - EXTRA_ROWS, wide), BF16)
 
 
 def back_profile(horiz):
@@ -196,63 +251,73 @@
     return [steady, horiz, steady, horiz, square, steady, horiz]
 
 
-def fit_kernel(cores, stripes, stamps_ref, *refs):
+def fit_kernel(cores, stripes, *refs):
     pieces = refs[:cores]
-    near_ref, far_ref, science_ref, good_ref, high_ref, low_ref, out_ref, ext, xhigh, xlow = refs[cores:]
+    (
+        near_ref,
+        far_ref,
+        science_ref,
+        good_ref,
+        odd_ref,
+        high_ref,
+        low_ref,
+        out_ref,
+        ext,
+        highs,
+        lows,
+        xhigh,
+        xlow,
+    ) = refs[cores:]
     rows = pieces[0].shape[0]
     wide = science_ref.shape[2]
     pairs = wide // (4 * STAMP_W)
-    fill_extended(ext, cores, pieces, near_ref, far_ref)
+    fill_extended(ext, highs, lows, cores, pieces, near_ref, far_ref)
+    clear_spare((xhigh, xlow))
     lane = lane_id(1)
-    lane_ext = lane_id(ext.shape[0])
+    lane_ext = lane_id(highs.shape[0])
     first_row = lax.axis_index("stripe") * rows
 
-    def odd_of(stamp):
-        return lax.rem(stamps_ref[0, stamp], 2)
-
-    def window(stamp, offset):
-        odd = odd_of(stamp)
-        left = ext[:, stamp * LANES : (stamp + 1) * LANES]
-        centre = ext[:, (stamp + 1) * LANES : (stamp + 2) * LANES]
-        right = ext[:, (stamp + 2) * LANES : (stamp + 3) * LANES]
-        taken = jnp.where(
-            odd == 1,
-            jnp.where(lane_ext < HALF, right, centre),
-            jnp.where(lane_ext >= LANES - HALF, left, centre),
-        )
-        amount = jnp.where(odd == 1, HALF + STAMP_W, HALF) + offset
-        return pltpu.roll(taken, lax.rem(amount, LANES), 1)
-
-    def picked(values, stamp, offset):
-        return pltpu.roll(values, odd_of(stamp) * STAMP_W + offset, 1)
+    def odd_of(stamp, height):
+        return jnp.broadcast_to(odd_ref[stamp : stamp + 1, :] == 1, (height, LANES))
+
+    def window(source, stamp, offset):
+        left = source[:, stamp * LANES : (stamp + 1) * LANES]
+        centre = source[:, (stamp + 1) * LANES : (stamp + 2) * LANES]
+        right = source[:, (stamp + 2) * LANES : (stamp + 3) * LANES]
+        odd = jnp.where(lane_ext < HALF, right, centre)
+        even = jnp.where(lane_ext >= LANES - HALF, left, centre)
+        odd = pltpu.roll(odd, (HALF + STAMP_W + offset) % LANES, 1)
+        even = pltpu.roll(even, HALF + offset, 1)
+        return jnp.where(odd_of(stamp, source.shape[0]), odd, even)
+
+    def picked(values, stamp, upper):
+        moved = pltpu.roll(values, STAMP_W, 1)
+        odd = odd_of(stamp, values.shape[0])
+        return jnp.where(odd, values, moved) if upper else jnp.where(odd, moved, values)
 
     total = jnp.zeros((FIT_ROWS, FIT_ROWS), F32)
     chunk = 2
     for start in range(0, pairs, chunk):
         for pair in range(start, start + chunk):
-            first = window(2 * pair, 0)
-            second = window(2 * pair + 1, STAMP_W)
             columns = slice(pair * LANES, (pair + 1) * LANES)
-
-            def shifted(tap, lines):
-                back = (LANES - tap) % LANES
-                a = first[lines]
-                b = second[lines]
-                if back:
-                    a = pltpu.roll(a, back, 1)
-                    b = pltpu.roll(b, back, 1)
-                return jnp.where(lane_id(a.shape[0]) < STAMP_W, a, b)
-
-            def put(place, values):
-                high, low = split_two(values)
-                xhigh[place : place + values.shape[0], columns] = high
-                xlow[place : place + values.shape[0], columns] = low
-
-            spread_window(shifted, put)
-            clear_spare((xhigh, xlow), columns)
+            for source, target in ((highs, xhigh), (lows, xlow)):
+                first = window(source, 2 * pair, 0)
+                second = window(source, 2 * pair + 1, STAMP_W)
+
+                def shifted(tap, lines):
+                    a, b = first[lines], second[lines]
+                    if tap:
+                        a = pltpu.roll(a, LANES - tap, 1)
+                        b = pltpu.roll(b, LANES - tap, 1)
+                    return jnp.where(lane_id(a.shape[0]) < STAMP_W, a, b)
+
+                def put(place, values):
+                    target[place : place + values.shape[0], columns] = values
+
+                spread_window(shifted, put)
         span = slice(start * LANES, (start + chunk) * LANES)
-        weights_high = high_ref[...].astype(BF16)
-        weights_low = low_ref[...].astype(BF16)
+        weights_high = high_ref[...]
+        weights_low = low_ref[...]
         bases = (
             jnp.dot(weights_high, xhigh[:, span], preferred_element_type=F32)
             + jnp.dot(weights_low, xhigh[:, span], preferred_element_type=F32)
@@ -261,13 +326,15 @@
         horiz_parts, science_parts, good_parts = [], [], []
         for pair in range(start, start + chunk):
             low_half = lane < STAMP_W
-            block = jnp.where(low_half, stamps_ref[0, 2 * pair], stamps_ref[0, 2 * pair + 1] - 1)
-            horiz_parts.append(position(block * STAMP_W + lane, wide))
+            odd = jnp.where(
+                low_half, odd_ref[2 * pair : 2 * pair + 1], odd_ref[2 * pair + 1 : 2 * pair + 2] + 1
+            )
+            horiz_parts.append(position(4 * pair * STAMP_W + odd * STAMP_W + lane, wide))
             for source, parts in ((science_ref, science_parts), (good_ref, good_parts)):
-                a = source[0, :, 2 * pair * LANES : (2 * pair + 1) * LANES].astype(F32)
-                b = source[0, :, (2 * pair + 1) * LANES : (2 * pair + 2) * LANES].astype(F32)
-                a = picked(a, 2 * pair, 0)
-                b = picked(b, 2 * pair + 1, STAMP_W)
+                a = source[0, :, 2 * pair * LANES : (2 * pair + 1) * LANES]
+                b = source[0, :, (2 * pair + 1) * LANES : (2 * pair + 2) * LANES]
+                a = picked(a, 2 * pair, False)
+                b = picked(b, 2 * pair + 1, True)
                 parts.append(jnp.where(lane_id(rows) < STAMP_W, a, b))
         horiz = jnp.concatenate(horiz_parts, axis=1)
         good = jnp.concatenate(good_parts, axis=1)
@@ -292,61 +359,86 @@
     )
 
 
-def pivots():
-    return [t * BASE_PAD + b for t in range(3) for b in range(BASES)] + [
-        3 * BASE_PAD + m for m in range(BACK)
-    ]
+def panels():
+    out = []
+    for term in range(3):
+        start = term * BASE_PAD
+        out += [(start, 8), (start + 8, 8), (start + 16, BASES - 16)]
+    return out + [(3 * BASE_PAD, BACK)]
 
 
 def solve_rows(matrix):
+    sub = row_id(8)
+    tiles = [matrix[start : start + 8] for start in range(0, FIT_ROWS, 8)]
+
+    def spread(tile, spot):
+        return jnp.broadcast_to(tile[spot : spot + 1], (8, LANES))
+
+    for start, size in panels():
+        home = start // 8
+        columns = [
+            [jnp.broadcast_to(tile[:, start + j : start + j + 1], (8, LANES)) for tile in tiles]
+            for j in range(size)
+        ]
+        corner = [column[home] for column in columns]
+        rows = tiles[home]
+        for spot in range(size):
+            keep = sub == spot
+            inverse = 1.0 / spread(corner[spot], spot)
+            others = jnp.where(keep, 0.0, corner[spot])
+            scaled = spread(rows, spot) * inverse
+            rows = jnp.where(keep, scaled, rows - others * scaled)
+            for j in range(spot + 1, size):
+                scaled = spread(corner[j], spot) * inverse
+                corner[j] = jnp.where(keep, scaled, corner[j] - others * scaled)
+        for place in range(len(tiles)):
+            if place == home:
+                tiles[place] = rows
+                continue
+            change = columns[0][place] * spread(rows, 0)
+            for j in range(1, size):
+                change = change + columns[j][place] * spread(rows, j)
+            tiles[place] = tiles[place] - change
     line = row_id(FIT_ROWS)
-    lane = lane_id(FIT_ROWS)
     used = (line >= 3 * BASE_PAD) | (lax.rem(line, BASE_PAD) < BASES)
-    matrix = jnp.where((line == lane) & ~used, 1.0, matrix)
-    for pivot in pivots():
-        column = jnp.broadcast_to(matrix[:, pivot : pivot + 1], (FIT_ROWS, LANES))
-        row = matrix[pivot : pivot + 1] / column[pivot : pivot + 1]
-        matrix = matrix - jnp.where(line == pivot, 0.0, column) * row
-    right = jnp.broadcast_to(matrix[:, FIT_ROWS - 1 : FIT_ROWS], (FIT_ROWS, LANES))
-    diagonal = jnp.sum(jnp.where(line == lane, matrix, 0.0), axis=1, keepdims=True)
-    return right / jnp.broadcast_to(diagonal, (FIT_ROWS, LANES))
-
-
-def model_kernel(cores, stripes, normal_ref, *refs):
+    right = jnp.concatenate(tiles, axis=0)[:, FIT_ROWS - 1 : FIT_ROWS]
+    return jnp.where(used, jnp.broadcast_to(right, (FIT_ROWS, LANES)), 0.0)
+
+
+def spread_kernel(cores, *refs):
     pieces = refs[:cores]
-    near_ref, far_ref, science_ref, good_ref, base_ref, out_ref, coef_ref, ext, xhigh, xlow = refs[cores:]
-    rows = pieces[0].shape[0]
+    near_ref, far_ref, after_ref, xhigh, xlow, ext, highs, lows = refs[cores:]
+    wide = xhigh.shape[1]
+    fill_extended(ext, highs, lows, cores, pieces, near_ref, far_ref)
+    clear_spare((xhigh, xlow))
+    for source, target in ((highs, xhigh), (lows, xlow)):
+
+        def shifted(tap, lines):
+            start = LANES - HALF + tap
+            return source[lines, start : start + wide]
+
+        def put(place, values):
+            target[place : place + values.shape[0]] = values
+
+        spread_window(shifted, put)
+
+
+def model_kernel(
+    stripes,
+    normal_ref,
+    xhigh,
+    xlow,
+    near_ref,
+    far_ref,
+    science_ref,
+    good_ref,
+    base_ref,
+    out_ref,
+    coef_ref,
+):
+    rows = science_ref.shape[1]
     wide = science_ref.shape[2]
-    fold = wide // 2
-    top, bottom = fill_extended(ext, cores, pieces, near_ref, far_ref)
-    tiles = wide // LANES
-    lane_ext = lane_id(ext.shape[0])
-    for tile in range(tiles):
-        columns = slice(tile * LANES, (tile + 1) * LANES)
-        left = ext[:, tile * LANES : (tile + 1) * LANES]
-        centre = ext[:, (tile + 1) * LANES : (tile + 2) * LANES]
-        right = ext[:, (tile + 2) * LANES : (tile + 3) * LANES]
-
-        def shifted(tap, lines):
-            move = HALF - tap
-            middle = centre[lines]
-            if move == 0:
-                return middle
-            where = lane_ext[lines]
-            if move > 0:
-                mixed = jnp.where(where >= LANES - move, left[lines], middle)
-            else:
-                mixed = jnp.where(where < -move, right[lines], middle)
-            return pltpu.roll(mixed, move % LANES, 1)
-
-        def put(place, values):
-            high, low = split_two(values)
-            xhigh[place : place + values.shape[0], columns] = high
-            xlow[place : place + values.shape[0], columns] = low
-
-        spread_window(shifted, put)
-        clear_spare((xhigh, xlow), columns)
-
+    top, bottom = edges_of(near_ref, far_ref)
     coef = solve_rows(normal_ref[...])
     lane = lane_id(FIT_ROWS)
     home = jnp.where(
@@ -389,7 +481,10 @@
         spare = jnp.where((line == rows) & (corner >= 2), outer, spare)
         wanted.append(spare)
         blocks.append(jnp.concatenate(wanted, axis=1))
+    blocks.append(jnp.zeros((8, DEPTH), F32))
     kernel_high, kernel_low = split_two(jnp.concatenate(blocks, axis=0))
+    kernel_gap = kernel_high.shape[0]
+    kernel_both = jnp.concatenate([kernel_high, kernel_low], axis=0)
     level = [coef[3 * BASE_PAD + m : 3 * BASE_PAD + m + 1, 0:1] for m in range(BACK)]
     first_row = lax.axis_index("stripe") * rows
     vert_line = jnp.where(line == rows + 1, -1, line)
@@ -399,11 +494,9 @@
     outs = []
     for start in range(0, wide, chunk):
         span = slice(start, start + chunk)
-        sums = (
-            jnp.dot(kernel_high, xhigh[:, span], preferred_element_type=F32)
-            + jnp.dot(kernel_low, xhigh[:, span], preferred_element_type=F32)
-            + jnp.dot(kernel_high, xlow[:, span], preferred_element_type=F32)
-        )
+        both = jnp.dot(kernel_both, xhigh[:, span], preferred_element_type=F32)
+        lower = jnp.dot(kernel_high, xlow[:, span], preferred_element_type=F32)
+        sums = both[: 3 * BASE_PAD] + (both[kernel_gap : kernel_gap + 3 * BASE_PAD] + lower[: 3 * BASE_PAD])
         horiz = position(start + lax.broadcasted_iota(jnp.int32, (1, chunk), 1), wide)
         horiz_square = 0.5 * (3.0 * horiz * horiz - 1.0)
         model = (
@@ -416,7 +509,7 @@
         )
         outs.append(model)
     model = jnp.concatenate(outs, axis=1)
-    own = good_ref[0].astype(F32) * (science_ref[0] - model[:rows])
+    own = good_ref[0] * (science_ref[0] - model[:rows])
 
     def halo(edge, spot):
         science = jnp.concatenate([edge[20:21], edge[21:22]], axis=1)
@@ -450,15 +543,43 @@
 
 
 def shards(template, exposure, cosmic_mask, stamp_blocks, row_filters, col_filters):
+    arguments = (template, exposure, cosmic_mask, stamp_blocks, row_filters, col_filters)
     rows, half = template.shape
     wide = exposure.shape[2]
     cores = lax.axis_size("exp")
     stripes = lax.axis_size("stripe")
-    params = pltpu.CompilerParams(vmem_limit_bytes=48 * 1024 * 1024)
+    params = pltpu.CompilerParams(vmem_limit_bytes=24 * 1024 * 1024)
     pieces = [template] + [
         lax.ppermute(template, "exp", [((i + step) % cores, i) for i in range(cores)])
         for step in range(1, cores)
     ]
+    weight_shape = jax.ShapeDtypeStruct((rows * BASE_PAD, DEPTH), BF16)
+    stamps = stamp_blocks.shape[1]
+    template_in, science, good, odd, high, low, base = pl.pallas_call(
+        load_kernel,
+        out_shape=(
+            jax.ShapeDtypeStruct(template.shape, F32),
+            jax.ShapeDtypeStruct(exposure.shape, F32),
+            jax.ShapeDtypeStruct(exposure.shape, F32),
+            jax.ShapeDtypeStruct((stamps, LANES), jnp.int32),
+            weight_shape,
+            weight_shape,
+            jax.ShapeDtypeStruct((BASE_PAD, DEPTH + LANES), F32),
+        ),
+        in_specs=[pl.BlockSpec(memory_space=pltpu.HBM)] * 6,
+        out_specs=tuple(whole_vmem(7)),
+        scratch_shapes=[
+            pltpu.VMEM((2, BASE_PAD, LANES), F32),
+            pltpu.VMEM(row_filters.shape, F32),
+            pltpu.VMEM(col_filters.shape, F32),
+            pltpu.VMEM(cosmic_mask.shape, jnp.int32),
+            pltpu.SMEM(stamp_blocks.shape, jnp.int32),
+            pltpu.SemaphoreType.DMA((6,)),
+        ],
+        compiler_params=params,
+        name="load",
+    )(*[pltpu.with_memory_space_constraint(array, pltpu.HBM) for array in arguments])
+    pieces = [template_in] + pieces[1:]
     edge_shape = jax.ShapeDtypeStruct((24, wide // 2), F32)
     near, far = pl.pallas_call(
         functools.partial(edge_kernel, cores),
@@ -468,60 +589,55 @@
         scratch_shapes=[pltpu.VMEM((rows, wide), F32)],
         compiler_params=params,
         name="edges",
-    )(*pieces, exposure, cosmic_mask)
+    )(*pieces, science, good)
     near_pairs = [(i, i + 1) for i in range(0, stripes - 1, 2)]
     far_pairs = [(i, i + 1) for i in range(1, stripes - 1, 2)]
 
     def swapped(values, couples):
         return lax.ppermute(values, "stripe", couples + [(b, a) for a, b in couples])
 
+    far = swapped(far, far_pairs)
     near = swapped(near, near_pairs)
-    far = swapped(far, far_pairs)
-    weight_shape = jax.ShapeDtypeStruct((rows * BASE_PAD, DEPTH), F32)
-    high, low, base = pl.pallas_call(
-        weight_kernel,
-        out_shape=(
-            weight_shape,
-            weight_shape,
-            jax.ShapeDtypeStruct((BASE_PAD, DEPTH + LANES), F32),
-        ),
-        in_specs=whole_vmem(2),
-        out_specs=tuple(whole_vmem(3)),
-        scratch_shapes=[pltpu.VMEM((2, BASE_PAD, LANES), F32)],
-        compiler_params=params,
-        name="weights",
-    )(row_filters, col_filters)
-    ext_shape = pltpu.VMEM((rows + 24, wide + 2 * LANES), F32)
+    ext_shapes = [
+        pltpu.VMEM((rows + 24, wide + 2 * LANES), F32),
+        pltpu.VMEM((GROUP + 16, wide + 2 * LANES), BF16),
+        pltpu.VMEM((GROUP + 16, wide + 2 * LANES), BF16),
+    ]
     normal = pl.pallas_call(
         functools.partial(fit_kernel, cores, stripes),
         out_shape=jax.ShapeDtypeStruct((FIT_ROWS, LANES), F32),
-        in_specs=[pl.BlockSpec(memory_space=pltpu.SMEM)] + whole_vmem(cores + 6),
+        in_specs=whole_vmem(cores + 7),
         out_specs=pl.BlockSpec(memory_space=pltpu.VMEM),
-        scratch_shapes=[
-            ext_shape,
+        scratch_shapes=ext_shapes
+        + [
             pltpu.VMEM((DEPTH, wide // 2), BF16),
             pltpu.VMEM((DEPTH, wide // 2), BF16),
         ],
         compiler_params=params,
         name="fit",
-    )(stamp_blocks, *pieces, near, far, exposure, cosmic_mask, high, low)
+    )(*pieces, near, far, science, good, odd, high, low)
+    wide_shape = jax.ShapeDtypeStruct((DEPTH, wide), BF16)
+    xhigh, xlow = pl.pallas_call(
+        functools.partial(spread_kernel, cores),
+        out_shape=(wide_shape, wide_shape),
+        in_specs=whole_vmem(cores + 3),
+        out_specs=tuple(whole_vmem(2)),
+        scratch_shapes=ext_shapes,
+        compiler_params=params,
+        name="spread",
+    )(*pieces, near, far, normal)
     normal = summed(normal, "stripe")
     filtered, coef = pl.pallas_call(
-        functools.partial(model_kernel, cores, stripes),
+        functools.partial(model_kernel, stripes),
         out_shape=(
             jax.ShapeDtypeStruct(exposure.shape, F32),
             jax.ShapeDtypeStruct((1, 3 * BASES + BACK), F32),
         ),
-        in_specs=whole_vmem(cores + 6),
+        in_specs=whole_vmem(8),
         out_specs=tuple(whole_vmem(2)),
-        scratch_shapes=[
-            ext_shape,
-            pltpu.VMEM((DEPTH, wide), BF16),
-            pltpu.VMEM((DEPTH, wide), BF16),
-        ],
         compiler_params=params,
         name="model",
-    )(normal, *pieces, near, far, exposure, cosmic_mask, base)
+    )(normal, xhigh, xlow, near, far, science, good, base)
     return filtered, coef
 
 

time: 42.8 us -> 35.2 us (0.82)
  local copies, waits for them, and re-layouts: 5.55 us -> 0 us
  Pallas kernels: 13.5 us -> 12.2 us
  waiting for transfers between devices: 7.61 us -> 7 us
    unnamed x14 -> x0, local copies, waits for them, and re-layouts: 5.55 us -> none
    ppermute x2, waiting for transfers between devices: 0.56 us -> 2.79 us  [swapped(): lax.ppermute(values, 'stripe', couples + [(b, a) for a, b in couples])]
    ppermute x3, waiting for transfers between devices: 5.94 us -> 4.2 us  [summed(): lax.ppermute(values, axis, [(i, i ^ step) for i in range(count)])]
    ppermute x1, waiting for transfers between devices: 1.11 us -> 0.01 us  [shards(): lax.ppermute(template, 'exp', [((i + step) % cores, i) for i in range(cor...]
    pallas_call x2 -> x3, Pallas kernels: 9.13 us -> 8.46 us  [the longest x1 5.16 us: shards(): pl.pallas_call(functools.partial(model_kernel, stripes), out_shape=(jax.S...]
    pallas_call x1, Pallas kernels: 4.33 us -> 3.72 us  [shards(): pl.pallas_call(functools.partial(fit_kernel, cores, stripes), out_shape=j...]
  transfers between devices with their start and end apart: 6 -> 6, of which waited for: 5 -> 4; matrix products, arithmetic and copies ran while one was open for 0% -> 0% of each run, Pallas kernels for 1% -> 9%
where the time goes in v1:
time: 35.2 us; the launch traced here: 35 us
  starting transfers between devices  15.1 us (43%)
  Pallas kernels  12.2 us (35%)
  waiting for transfers between devices  7 us (20%)
  between operations  0.68 us (2%)
    ppermute x3, starting transfers between devices, summed(): lax.ppermute(values, axis, [(i, i ^ step) for i in range(count)])  11.3 us
    pallas_call x1, Pallas kernels, shards(): pl.pallas_call(functools.partial(model_kernel, stripes), out_shape=(jax.S...  5.16 us
    ppermute x3, waiting for transfers between devices, summed(): lax.ppermute(values, axis, [(i, i ^ step) for i in range(count)])  4.2 us
    pallas_call x1, Pallas kernels, shards(): pl.pallas_call(functools.partial(fit_kernel, cores, stripes), out_shape=j...  3.72 us
    ppermute x2, starting transfers between devices, swapped(): lax.ppermute(values, 'stripe', couples + [(b, a) for a, b in couples])  3.22 us
    ppermute x2, waiting for transfers between devices, swapped(): lax.ppermute(values, 'stripe', couples + [(b, a) for a, b in couples])  2.79 us
    pallas_call x1, Pallas kernels, shards(): pl.pallas_call(functools.partial(spread_kernel, cores), out_shape=(wide_s...  1.74 us
    pallas_call x1, Pallas kernels, shards(): pl.pallas_call(load_kernel, out_shape=(jax.ShapeDtypeStruct(template.shap...  1.57 us
  transfers between devices with their start and end apart: 6, of which 4 were waited for; matrix products, arithmetic and copies ran while one was open for 0% of the time, Pallas kernels for 9%

profile of v1, /device:TPU:0, one launch (start us, length us, event | category | flops | bytes accessed | tf_op | source)
XLA Modules:
  0.0 35.0 jit_solution(4590543035220050462)
XLA Ops:
  0.6 0.5 %collective-permute-start = (f32[16,1024]{1,0:T(8,128)}, f32[16,1024]{1,0:T(8,128)S(1)}, u32[]{:S(2)}, u32[]{:S(2)}) collective-permute-start(f32[16,1024]{1,0:T(8,128)} %template_hbm.1), channel_id=1, source_target_pairs={{1,0},{0,1},{3,2},{2,3},{5,4},{4,5},{7,6},{6,7},{9,8},{8,9},{11,10... | collective-permute-start | bytes 196616 | tf_op jit(solution)/shard_map/ppermute | solution.py:553
  1.1 1.6 %load.1 = (f32[16,1024]{1,0:T(8,128)S(1)}, f32[1,16,2048]{2,1,0:T(8,128)S(1)}, f32[1,16,2048]{2,1,0:T(8,128)S(1)}, s32[16,128]{1,0:T(8,128)S(1)}, bf16[384,768]{...) custom-call(f32[16,1024]{1,0:T(8,128)} %template_hbm.1, f32[1,16,2048]{2,1,0:T(8,128)} %science_hbm.1, ...), custom_call_target="tpu_custom_call" | custom-call | tf_op jit(solution)/shard_map/load/pallas_call | solution.py:558
  2.7 0.0 collective-permute-done.refs_1_
  2.7 0.1 edges.1
  2.8 2.6 %collective-permute-start.1 = (f32[24,1024]{1,0:T(8,128)S(1)}, f32[24,1024]{1,0:T(8,128)S(1)}, u32[]{:S(2)}, u32[]{:S(2)}) collective-permute-start(f32[24,1024]{1,0:T(8,128)S(1)} %get-tuple-element.16), channel_id=1, source_target_pairs={{0,2},{4,6},{8,10},{12,14},{2,0},{6,4},{10,8},{14,12},{1,3},{5,7},... | collective-permute-start | bytes 294920 | tf_op jit(solution)/shard_map/ppermute | solution.py:597
  5.4 0.7 %collective-permute-start.2 = (f32[24,1024]{1,0:T(8,128)S(1)}, f32[24,1024]{1,0:T(8,128)S(1)}, u32[]{:S(2)}, u32[]{:S(2)}) collective-permute-start(f32[24,1024]{1,0:T(8,128)S(1)} %get-tuple-element.17), channel_id=1, source_target_pairs={{2,4},{6,8},{10,12},{4,2},{8,6},{12,10},{3,5},{7,9},{11,13},{5,3},... | collective-permute-start | bytes 294920 | tf_op jit(solution)/shard_map/ppermute | solution.py:597
  6.0 2.8 %collective-permute-done.1.refs_2_.near_ref = f32[24,1024]{1,0:T(8,128)S(1)} collective-permute-done((f32[24,1024]{1,0:T(8,128)S(1)}, f32[24,1024]{1,0:T(8,128)S(1)}, u32[]{:S(2)}, u32[]{:S(2)}) %collective-permute-start.1) | collective-permute-done | bytes 98336 | tf_op jit(solution)/shard_map/ppermute | solution.py:597
  8.8 0.0 collective-permute-done.2.refs_3_.far_ref
  8.8 3.7 %fit.1.refs_4_ = f32[80,128]{1,0:T(8,128)S(1)} custom-call(f32[16,1024]{1,0:T(8,128)S(1)} %get-tuple-element.13.refs_0_, f32[16,1024]{1,0:T(8,128)S(1)} %collective-permute-done.refs_1_, f32[24,1024]{1,0:T(8,128)S(1)} %collective-permute-done.1.refs_2_.near_ref, f32[24,1024]{1,0:T(8,128)S(1)} %collective-permute-done.2.refs_3_.far_ref, ...), custom_call_target="tpu_custom_call" | custom-call | tf_op jit(solution)/shard_map/fit/pallas_call | solution.py:606
  12.6 4.7 %collective-permute-start.3 = (f32[80,128]{1,0:T(8,128)S(1)}, f32[80,128]{1,0:T(8,128)S(1)}, u32[]{:S(2)}, u32[]{:S(2)}) collective-permute-start(f32[80,128]{1,0:T(8,128)S(1)} %fit.1.refs_4_), channel_id=1, source_target_pairs={{0,2},{2,0},{4,6},{6,4},{8,10},{10,8},{12,14},{14,12},{1,3},{3,1},... | collective-permute-start | bytes 122888 | tf_op jit(solution)/shard_map/ppermute | solution.py:540
  17.3 2.0 %collective-permute-done.3 = f32[80,128]{1,0:T(8,128)S(1)} collective-permute-done((f32[80,128]{1,0:T(8,128)S(1)}, f32[80,128]{1,0:T(8,128)S(1)}, u32[]{:S(2)}, u32[]{:S(2)}) %collective-permute-start.3) | collective-permute-done | bytes 40992 | tf_op jit(solution)/shard_map/ppermute | solution.py:540
  19.3 3.2 %collective-permute-start.4 = (f32[80,128]{1,0:T(8,128)S(1)}, f32[80,128]{1,0:T(8,128)S(1)}, u32[]{:S(2)}, u32[]{:S(2)}) collective-permute-start(f32[80,128]{1,0:T(8,128)S(1)} %add.9), channel_id=1, source_target_pairs={{0,4},{2,6},{4,0},{6,2},{8,12},{10,14},{12,8},{14,10},{1,5},{3,7},... | collective-permute-start | bytes 122888 | tf_op jit(solution)/shard_map/ppermute | solution.py:540
  22.4 2.0 %collective-permute-done.4 = f32[80,128]{1,0:T(8,128)S(1)} collective-permute-done((f32[80,128]{1,0:T(8,128)S(1)}, f32[80,128]{1,0:T(8,128)S(1)}, u32[]{:S(2)}, u32[]{:S(2)}) %collective-permute-start.4) | collective-permute-done | bytes 40992 | tf_op jit(solution)/shard_map/ppermute | solution.py:540
  24.4 3.4 %collective-permute-start.5 = (f32[80,128]{1,0:T(8,128)S(1)}, f32[80,128]{1,0:T(8,128)S(1)}, u32[]{:S(2)}, u32[]{:S(2)}) collective-permute-start(f32[80,128]{1,0:T(8,128)S(1)} %add.10), channel_id=1, source_target_pairs={{0,8},{2,10},{4,12},{6,14},{8,0},{10,2},{12,4},{14,6},{1,9},{3,11}... | collective-permute-start | bytes 122888 | tf_op jit(solution)/shard_map/ppermute | solution.py:540
  27.9 1.7 %spread.1 = (bf16[768,2048]{1,0:T(8,128)(2,1)S(1)}, bf16[768,2048]{1,0:T(8,128)(2,1)S(1)}) custom-call(f32[16,1024]{1,0:T(8,128)S(1)} %get-tuple-element.13.refs_0_, f32[16,1024]{1,0:T(8,128)S(1)} %collective-permute-done.refs_1_, f32[24,1024]{1,0:T(8,128)S(1)} %collective-permute-done.1.refs_2_.near_ref, ...), custom_call_target="tpu_custom_call" | custom-call | tf_op jit(solution)/shard_map/spread/pallas_call | solution.py:620
  29.6 0.2 collective-permute-done.5
  29.9 5.2 %model.1 = (f32[1,16,2048]{2,1,0:T(8,128)}, f32[1,64]{1,0:T(1,128)}) custom-call(f32[80,128]{1,0:T(8,128)S(1)} %add.11.normal_ref, bf16[768,2048]{1,0:T(8,128)(2,1)S(1)} %get-tuple-element.21.xhigh, bf16[768,2048]{1,0:T(8,128)(2,1)S(1)} %get-tuple-element.22.xlow, f32[24,1024]{1,0:T(8,128)S(1)} %collective-permute-done.1.refs_2_.near_ref, ...), custom_call_target="tpu_custom_call" | custom-call | tf_op jit(solution)/shard_map/model/pallas_call | solution.py:630
  (3 shorter events, 0.0 us)
Async XLA Ops:
  0.6 2.1 %collective-permute-start = (f32[16,1024]{1,0:T(8,128)}, f32[16,1024]{1,0:T(8,128)S(1)}, u32[]{:S(2)}, u32[]{:S(2)}) collective-permute-start(f32[16,1024]{1,0:T(8,128)} %template_hbm.1), channel_id=1, source_target_pairs={{1,0},{0,1},{3,2},{2,3},{5,4},{4,5},{7,6},{6,7},{9,8},{8,9},{11,10... | collective-permute-start | bytes 196616 | tf_op jit(solution)/shard_map/ppermute | solution.py:553
  2.8 6.0 %collective-permute-start.1 = (f32[24,1024]{1,0:T(8,128)S(1)}, f32[24,1024]{1,0:T(8,128)S(1)}, u32[]{:S(2)}, u32[]{:S(2)}) collective-permute-start(f32[24,1024]{1,0:T(8,128)S(1)} %get-tuple-element.16), channel_id=1, source_target_pairs={{0,2},{4,6},{8,10},{12,14},{2,0},{6,4},{10,8},{14,12},{1,3},{5,7},... | collective-permute-start | bytes 294920 | tf_op jit(solution)/shard_map/ppermute | solution.py:597
  5.4 3.5 %collective-permute-start.2 = (f32[24,1024]{1,0:T(8,128)S(1)}, f32[24,1024]{1,0:T(8,128)S(1)}, u32[]{:S(2)}, u32[]{:S(2)}) collective-permute-start(f32[24,1024]{1,0:T(8,128)S(1)} %get-tuple-element.17), channel_id=1, source_target_pairs={{2,4},{6,8},{10,12},{4,2},{8,6},{12,10},{3,5},{7,9},{11,13},{5,3},... | collective-permute-start | bytes 294920 | tf_op jit(solution)/shard_map/ppermute | solution.py:597
  12.6 6.7 %collective-permute-start.3 = (f32[80,128]{1,0:T(8,128)S(1)}, f32[80,128]{1,0:T(8,128)S(1)}, u32[]{:S(2)}, u32[]{:S(2)}) collective-permute-start(f32[80,128]{1,0:T(8,128)S(1)} %fit.1.refs_4_), channel_id=1, source_target_pairs={{0,2},{2,0},{4,6},{6,4},{8,10},{10,8},{12,14},{14,12},{1,3},{3,1},... | collective-permute-start | bytes 122888 | tf_op jit(solution)/shard_map/ppermute | solution.py:540
  19.3 5.2 %collective-permute-start.4 = (f32[80,128]{1,0:T(8,128)S(1)}, f32[80,128]{1,0:T(8,128)S(1)}, u32[]{:S(2)}, u32[]{:S(2)}) collective-permute-start(f32[80,128]{1,0:T(8,128)S(1)} %add.9), channel_id=1, source_target_pairs={{0,4},{2,6},{4,0},{6,2},{8,12},{10,14},{12,8},{14,10},{1,5},{3,7},... | collective-permute-start | bytes 122888 | tf_op jit(solution)/shard_map/ppermute | solution.py:540
  24.4 5.4 %collective-permute-start.5 = (f32[80,128]{1,0:T(8,128)S(1)}, f32[80,128]{1,0:T(8,128)S(1)}, u32[]{:S(2)}, u32[]{:S(2)}) collective-permute-start(f32[80,128]{1,0:T(8,128)S(1)} %add.10), channel_id=1, source_target_pairs={{0,8},{2,10},{4,12},{6,14},{8,0},{10,2},{12,4},{14,6},{1,9},{3,11}... | collective-permute-start | bytes 122888 | tf_op jit(solution)/shard_map/ppermute | solution.py:540

commit v2 on v1

--- a/solution.py
+++ b/solution.py
@@ -22,6 +22,12 @@
 MAIN = MAIN_TILES * LANES
 DEPTH = MAIN + LANES
 EXTRA_ROWS = 80
+NEAR_AT = TAPS * 16
+NEAR_EXTRA_AT = NEAR_AT + 160
+EARLY = NEAR_EXTRA_AT + 48
+FAR_EXTRA_AT = 160
+LATE = 2 * LANES
+LATE_ROWS = -(-HALF * BASE_PAD // 16) * 16
 F32 = jnp.float32
 BF16 = jnp.bfloat16
 
@@ -48,9 +54,10 @@
     return lax.rem(lax.axis_index("stripe"), 2) == 0
 
 
-def edge_kernel(cores, *refs):
+def edge_kernel(cores, toward_near, *refs):
     pieces = refs[:cores]
-    science_ref, good_ref, near_ref, far_ref, ext = refs[cores:]
+    science_ref, good_ref = refs[cores : cores + 2]
+    edge_ref, ext = refs[-2:]
     rows, half = pieces[0].shape
     wide = science_ref.shape[2]
     me = lax.axis_index("exp")
@@ -73,28 +80,22 @@
 
     bottom = edge(low_first, rows - REACH, rows - 1)
     top = edge(0, 8, 0)
-    even = even_stripe()
-    near_ref[...] = jnp.where(even, bottom, top)
-    far_ref[...] = jnp.where(even, top, bottom)
+    edge_ref[...] = jnp.where(even_stripe() == toward_near, bottom, top)
 
 
 def load_kernel(
     template_hbm,
     science_hbm,
     good_hbm,
-    stamps_hbm,
     row_hbm,
     col_hbm,
+    stamps_hbm,
     template_ref,
     science_ref,
     good_ref,
-    odd_ref,
-    high_ref,
-    low_ref,
-    base_ref,
-    pad,
     row_ref,
     col_ref,
+    odd_ref,
     mask_ref,
     stamps_ref,
     sems,
@@ -103,18 +104,17 @@
         pltpu.make_async_copy(source, target, sems.at[spot])
         for spot, (source, target) in enumerate(
             [
+                (science_hbm, science_ref),
+                (good_hbm, mask_ref),
+                (template_hbm, template_ref),
                 (row_hbm, row_ref),
                 (col_hbm, col_ref),
-                (template_hbm, template_ref),
                 (stamps_hbm, stamps_ref),
-                (good_hbm, mask_ref),
-                (science_hbm, science_ref),
             ]
         )
     ]
     for move in moves:
         move.start()
-    pad[...] = jnp.zeros_like(pad)
     for move in moves:
         move.wait()
     good_ref[...] = mask_ref[...].astype(F32)
@@ -125,11 +125,16 @@
         ],
         axis=0,
     )
+
+
+def weight_kernel(
+    row_ref, col_ref, high_ref, low_ref, late_high_ref, late_low_ref, base_ref, pad
+):
+    pad[...] = jnp.zeros_like(pad)
     pad[0, 0:BASES, 0:TAPS] = row_ref[...]
     pad[1, 0:BASES, 0:TAPS] = col_ref[...]
     row = pad[0]
     lane = lane_id(BASE_PAD)
-    spot = lax.rem(lane, GROUP)
     group = lane // GROUP
     tiled = row
     for part in range(1, GROUPS_TILE):
@@ -167,27 +172,104 @@
     base_ref[:, MAIN : MAIN + LANES] = outer
     base_ref[:, MAIN + LANES :] = inner
     rows = high_ref.shape[0] // BASE_PAD
-
-    def line_weights(line):
-        tap = spot - (line - 1)
-        inside = (tap >= 0) & (tap < TAPS)
+    even = even_stripe()
+    first_tap, last_tap = tap_at(0), tap_at(TAPS - 1)
+
+    def column_tile(tap_of):
+        spread = zero
+        begin = 0
+        for end in range(1, LANES + 1):
+            if end < LANES and tap_of(end) == tap_of(begin):
+                continue
+            if tap_of(begin) < TAPS:
+                spread = jnp.where((lane >= begin) & (lane < end), columns[tap_of(begin)], spread)
+            begin = end
+        return spread
+
+    def early_tap(place):
+        if place < NEAR_AT:
+            return place // 16
+        return (place - NEAR_AT) // 8 if place < NEAR_EXTRA_AT else (place - NEAR_EXTRA_AT) // 2
+
+    def late_tap(place):
+        return place // 8 if place < FAR_EXTRA_AT else (place - FAR_EXTRA_AT) // 2
+
+    early_tiles = [
+        column_tile(lambda spot, tile=tile: early_tap(tile * LANES + spot))
+        for tile in range(EARLY // LANES)
+    ]
+    late_tiles = [
+        column_tile(lambda spot, tile=tile: late_tap(tile * LANES + spot))
+        for tile in range(LATE // LANES)
+    ]
+
+    def repeats(period):
+        blocks = []
+        for start in range(0, TAPS, period):
+            block = pltpu.roll(row, (LANES - start) % LANES, 1) if start else row
+            block = jnp.where(lane < period, block, 0.0)
+            size = period
+            while size < LANES:
+                block = block + pltpu.roll(block, size, 1)
+                size *= 2
+            blocks.append(block)
+        return blocks
+
+    def window(blocks, period, first):
+        block, move = first // period, first % period
+        here = blocks[block] if 0 <= block < len(blocks) else None
+        beyond = blocks[block + 1] if 0 <= block + 1 < len(blocks) else None
+        if move == 0:
+            return zero if here is None else here
+        ready = lax.rem(lane, period) < period - move
+        parts = [zero if part is None else pltpu.roll(part, LANES - move, 1) for part in (here, beyond)]
+        return jnp.where(ready, parts[0], parts[1])
+
+    by_sixteen, by_eight = repeats(16), repeats(8)
+    own_rows = [window(by_sixteen, 16, HALF - line) for line in range(rows)]
+    top_rows = [window(by_eight, 8, 1 - line) for line in range(rows)]
+    bottom_rows = [window(by_eight, 8, rows + HALF - line) for line in range(rows)]
+
+    parity = lax.rem(lane, 2)
+
+    def corner_taps(upper, lower, is_upper):
+        top = jnp.where(parity == 1, first_tap, 0.0) if upper else zero
+        bottom = jnp.where(parity == 0, last_tap, 0.0) if lower else zero
+        return jnp.where(is_upper, top, bottom)
+
+    near_is_top = ~even
+    early_rows, late_rows = [], []
+    for spot in range(rows):
+        odd_line = spot + rows - HALF if spot < HALF else spot - HALF
+        own = jnp.where(even, own_rows[spot], own_rows[odd_line])
+        side = jnp.where(even, bottom_rows[spot], top_rows[odd_line])
+        extra = zero
+        if spot >= HALF:
+            extra = corner_taps(spot == HALF, spot == rows - 1, near_is_top)
         tiles = [
-            jnp.where(inside, pltpu.roll(main, (line - 1) % LANES, 1), 0.0) for main in mains
+            own,
+            own,
+            jnp.where(lane < NEAR_AT - 2 * LANES, own, side),
+            jnp.where(lane < NEAR_EXTRA_AT - 3 * LANES, side, extra),
         ]
-        if line == 0:
-            tiles.append(jnp.where(corner < 2, inner, 0.0))
-        elif line == rows - 1:
-            tiles.append(jnp.where(corner >= 2, inner, 0.0))
-        else:
-            tiles.append(zero)
-        return jnp.concatenate(tiles, axis=1)
-
-    for line in range(0, rows, 2):
-        both = jnp.concatenate([line_weights(line), line_weights(line + 1)], axis=0)
-        high, low = split_two(both)
-        where = pl.ds(line * BASE_PAD, 2 * BASE_PAD)
-        high_ref[where, :] = high
-        low_ref[where, :] = low
+        early_rows.append(
+            jnp.concatenate([mine * tile for mine, tile in zip(tiles, early_tiles)], axis=1)
+        )
+        if spot < HALF:
+            side = jnp.where(even, top_rows[spot], bottom_rows[odd_line])
+            extra = corner_taps(spot == 0, spot == HALF - 1, even)
+            tiles = [side, jnp.where(lane < FAR_EXTRA_AT - LANES, side, extra)]
+            late_rows.append(
+                jnp.concatenate([mine * tile for mine, tile in zip(tiles, late_tiles)], axis=1)
+            )
+    for spot in range(0, rows, 2):
+        where = pl.ds(spot * BASE_PAD, 2 * BASE_PAD)
+        high_ref[where, :], low_ref[where, :] = split_two(
+            jnp.concatenate(early_rows[spot : spot + 2], axis=0)
+        )
+    spare = late_high_ref.shape[0] - HALF * BASE_PAD
+    late_rows.append(jnp.zeros((spare, LATE), F32))
+    late_high_ref[...], late_low_ref[...] = split_two(jnp.concatenate(late_rows, axis=0))
 
 
 def edges_of(near_ref, far_ref):
@@ -251,112 +333,234 @@
     return [steady, horiz, steady, horiz, square, steady, horiz]
 
 
-def fit_kernel(cores, stripes, *refs):
+def put_halves(target, edge_ref, rows, first):
+    fold = edge_ref.shape[1]
+    for side in range(2):
+        where = pl.ds(LANES + side * fold, fold)
+        target[first : first + 8, where] = edge_ref[8 * side : 8 * side + 8]
+        for line in range(2):
+            spot = 16 + 2 * line + side
+            target[rows + line : rows + line + 1, where] = edge_ref[spot : spot + 1]
+
+
+def paired(values):
+    span = values.shape[1]
+    return jnp.concatenate([values, pltpu.roll(values, span - 1, 1)], axis=0)
+
+
+def corner_block(lines):
+    span = lines.shape[1]
+    parts = [lines] + [pltpu.roll(lines, span - move, 1) for move in range(1, 8)]
+    return jnp.concatenate(parts, axis=0)
+
+
+def odd_rows(odd_ref, stamp, height):
+    return jnp.broadcast_to(odd_ref[stamp : stamp + 1, :] == 1, (height, LANES))
+
+
+def stamp_window(source, odd_ref, stamp, offset):
+    height = source.shape[0]
+    lane = lane_id(height)
+    left = source[:, stamp * LANES : (stamp + 1) * LANES]
+    centre = source[:, (stamp + 1) * LANES : (stamp + 2) * LANES]
+    right = source[:, (stamp + 2) * LANES : (stamp + 3) * LANES]
+    odd = jnp.where(lane < LANES // 4, right, centre)
+    even = jnp.where(lane >= LANES - HALF, left, centre)
+    odd = pltpu.roll(odd, (HALF + STAMP_W + offset) % LANES, 1)
+    even = pltpu.roll(even, HALF + offset, 1)
+    return jnp.where(odd_rows(odd_ref, stamp, height), odd, even)
+
+
+def stamp_shifts(sources, targets, odd_ref, pair, moves):
+    columns = slice(pair * LANES, (pair + 1) * LANES)
+    for source, target in zip(sources, targets):
+        first = stamp_window(source, odd_ref, 2 * pair, 0)
+        second = stamp_window(source, odd_ref, 2 * pair + 1, STAMP_W)
+        for spot, (tile, move) in enumerate(moves):
+            a, b = first[16 * tile : 16 * tile + 16], second[16 * tile : 16 * tile + 16]
+            if move:
+                a = pltpu.roll(a, LANES - move, 1)
+                b = pltpu.roll(b, LANES - move, 1)
+            target[16 * spot : 16 * spot + 16, columns] = jnp.where(
+                lane_id(16) < STAMP_W, a, b
+            )
+
+
+def three_products(high, low, xhigh, xlow):
+    return (
+        jnp.dot(high, xhigh, preferred_element_type=F32)
+        + jnp.dot(low, xhigh, preferred_element_type=F32)
+        + jnp.dot(high, xlow, preferred_element_type=F32)
+    )
+
+
+def design_line(bases, keep, target, horiz, profile, row, region_rows):
+    own = bases * keep
+    vert = position(jnp.full(horiz.shape, row, jnp.int32), region_rows)
+    square = 0.5 * (3.0 * vert * vert - 1.0)
+    steady = jnp.ones_like(vert)
+    scale = jnp.concatenate([steady, steady, vert, vert, steady, square, square], axis=0)
+    return jnp.concatenate(
+        [own, own * horiz, own * vert, profile * scale * keep, target], axis=0
+    ).astype(BF16)
+
+
+def gram(design):
+    return lax.dot_general(design, design, (((1,), (1,)), ((), ())), preferred_element_type=F32)
+
+
+def early_kernel(cores, stripes, *refs):
     pieces = refs[:cores]
     (
         near_ref,
-        far_ref,
         science_ref,
         good_ref,
         odd_ref,
         high_ref,
         low_ref,
+        total_ref,
+        late_ref,
+        aux_ref,
+        ext,
+        highs,
+        lows,
+        xhigh,
+        xlow,
+        bases,
+    ) = refs[cores:]
+    rows, half = pieces[0].shape
+    wide = science_ref.shape[2]
+    pairs = wide // (4 * STAMP_W)
+    me = lax.axis_index("exp")
+    ext[:, 0:LANES] = jnp.zeros((ext.shape[0], LANES), F32)
+    ext[:, LANES + wide :] = jnp.zeros((ext.shape[0], LANES), F32)
+    for step in range(cores):
+        start = lax.rem(me + step, cores) * half + LANES
+        ext[0:rows, pl.ds(pl.multiple_of(start, LANES), half)] = pieces[step][...]
+    put_halves(ext, near_ref, rows + 8, rows)
+    lines = jnp.concatenate(
+        [ext[0:rows], paired(ext[rows : rows + 8]), corner_block(ext[rows + 8 : rows + 10])], axis=0
+    )
+    highs[...], lows[...] = split_two(lines)
+    moves = [(0, tap) for tap in range(TAPS)]
+    moves += [(1, 2 * step) for step in range(10)]
+    moves += [(2, 8 * step) for step in range(3)]
+    lane = lane_id(1)
+    for pair in range(pairs):
+        columns = slice(pair * LANES, (pair + 1) * LANES)
+        stamp_shifts((highs, lows), (xhigh, xlow), odd_ref, pair, moves)
+        odd = jnp.where(
+            lane < STAMP_W,
+            odd_ref[2 * pair : 2 * pair + 1],
+            odd_ref[2 * pair + 1 : 2 * pair + 2] + 1,
+        )
+        horiz = position(4 * pair * STAMP_W + odd * STAMP_W + lane, wide)
+        aux_ref[2 * rows : 2 * rows + 8, columns] = jnp.broadcast_to(horiz, (8, LANES))
+        picked = []
+        for source in (good_ref, science_ref):
+            lower = source[0, :, 2 * pair * LANES : (2 * pair + 1) * LANES]
+            upper = source[0, :, (2 * pair + 1) * LANES : (2 * pair + 2) * LANES]
+            lower = jnp.where(
+                odd_rows(odd_ref, 2 * pair, rows), pltpu.roll(lower, STAMP_W, 1), lower
+            )
+            upper = jnp.where(
+                odd_rows(odd_ref, 2 * pair + 1, rows), upper, pltpu.roll(upper, STAMP_W, 1)
+            )
+            picked.append(jnp.where(lane_id(rows) < STAMP_W, lower, upper))
+        aux_ref[0:rows, columns] = picked[0]
+        aux_ref[rows : 2 * rows, columns] = picked[0] * picked[1]
+    split = HALF * BASE_PAD
+    chunk = 2 * LANES
+    for start in range(0, wide // 2, chunk):
+        span = slice(start, start + chunk)
+        values = three_products(high_ref[...], low_ref[...], xhigh[:, span], xlow[:, span])
+        late_ref[:, span] = values[:split]
+        bases[:, span] = values[split:]
+    horiz = aux_ref[2 * rows : 2 * rows + 1]
+    profile = jnp.concatenate(back_profile(horiz), axis=0)
+    first_line = jnp.where(even_stripe(), HALF, 0)
+    first_row = lax.axis_index("stripe") * rows
+    total = jnp.zeros((FIT_ROWS, FIT_ROWS), F32)
+    for spot in range(rows - HALF):
+        line = first_line + spot
+        design = design_line(
+            bases[spot * BASE_PAD : (spot + 1) * BASE_PAD],
+            aux_ref[pl.ds(line, 1), :],
+            aux_ref[pl.ds(rows + line, 1), :],
+            horiz,
+            profile,
+            first_row + line,
+            rows * stripes,
+        )
+        total = total + gram(design)
+    total_ref[...] = jnp.concatenate(
+        [total, jnp.zeros((FIT_ROWS, LANES - FIT_ROWS), F32)], axis=1
+    )
+
+
+def late_kernel(stripes, rows, *refs):
+    (
+        far_ref,
+        odd_ref,
+        high_ref,
+        low_ref,
+        total_ref,
+        early_ref,
+        aux_ref,
         out_ref,
         ext,
         highs,
         lows,
         xhigh,
         xlow,
-    ) = refs[cores:]
-    rows = pieces[0].shape[0]
-    wide = science_ref.shape[2]
-    pairs = wide // (4 * STAMP_W)
-    fill_extended(ext, highs, lows, cores, pieces, near_ref, far_ref)
-    clear_spare((xhigh, xlow))
-    lane = lane_id(1)
-    lane_ext = lane_id(highs.shape[0])
+        bases,
+    ) = refs
+    width = early_ref.shape[1]
+    pairs = width // LANES
+    ext[:, 0:LANES] = jnp.zeros((ext.shape[0], LANES), F32)
+    ext[:, ext.shape[1] - LANES :] = jnp.zeros((ext.shape[0], LANES), F32)
+    put_halves(ext, far_ref, 8, 0)
+    lines = jnp.concatenate([paired(ext[0:8]), corner_block(ext[8:10])], axis=0)
+    highs[...], lows[...] = split_two(lines)
+    moves = [(0, 2 * step) for step in range(10)] + [(1, 8 * step) for step in range(3)]
+    used = 16 * len(moves)
+    for ref in (xhigh, xlow):
+        ref[used:] = jnp.zeros((LATE - used, width), BF16)
+    split = HALF * BASE_PAD
+    chunk = 2 * LANES
+    for start in range(0, width, chunk):
+        span = slice(start, start + chunk)
+        for pair in range(start // LANES, (start + chunk) // LANES):
+            stamp_shifts((highs, lows), (xhigh, xlow), odd_ref, pair, moves)
+        values = three_products(high_ref[...], low_ref[...], xhigh[:, span], xlow[:, span])
+        bases[:, span] = early_ref[:, span] + values[:split]
+    horiz = aux_ref[2 * rows : 2 * rows + 1]
+    profile = jnp.concatenate(back_profile(horiz), axis=0)
+    first_line = jnp.where(even_stripe(), 0, rows - HALF)
     first_row = lax.axis_index("stripe") * rows
-
-    def odd_of(stamp, height):
-        return jnp.broadcast_to(odd_ref[stamp : stamp + 1, :] == 1, (height, LANES))
-
-    def window(source, stamp, offset):
-        left = source[:, stamp * LANES : (stamp + 1) * LANES]
-        centre = source[:, (stamp + 1) * LANES : (stamp + 2) * LANES]
-        right = source[:, (stamp + 2) * LANES : (stamp + 3) * LANES]
-        odd = jnp.where(lane_ext < HALF, right, centre)
-        even = jnp.where(lane_ext >= LANES - HALF, left, centre)
-        odd = pltpu.roll(odd, (HALF + STAMP_W + offset) % LANES, 1)
-        even = pltpu.roll(even, HALF + offset, 1)
-        return jnp.where(odd_of(stamp, source.shape[0]), odd, even)
-
-    def picked(values, stamp, upper):
-        moved = pltpu.roll(values, STAMP_W, 1)
-        odd = odd_of(stamp, values.shape[0])
-        return jnp.where(odd, values, moved) if upper else jnp.where(odd, moved, values)
-
-    total = jnp.zeros((FIT_ROWS, FIT_ROWS), F32)
-    chunk = 2
-    for start in range(0, pairs, chunk):
-        for pair in range(start, start + chunk):
-            columns = slice(pair * LANES, (pair + 1) * LANES)
-            for source, target in ((highs, xhigh), (lows, xlow)):
-                first = window(source, 2 * pair, 0)
-                second = window(source, 2 * pair + 1, STAMP_W)
-
-                def shifted(tap, lines):
-                    a, b = first[lines], second[lines]
-                    if tap:
-                        a = pltpu.roll(a, LANES - tap, 1)
-                        b = pltpu.roll(b, LANES - tap, 1)
-                    return jnp.where(lane_id(a.shape[0]) < STAMP_W, a, b)
-
-                def put(place, values):
-                    target[place : place + values.shape[0], columns] = values
-
-                spread_window(shifted, put)
-        span = slice(start * LANES, (start + chunk) * LANES)
-        weights_high = high_ref[...]
-        weights_low = low_ref[...]
-        bases = (
-            jnp.dot(weights_high, xhigh[:, span], preferred_element_type=F32)
-            + jnp.dot(weights_low, xhigh[:, span], preferred_element_type=F32)
-            + jnp.dot(weights_high, xlow[:, span], preferred_element_type=F32)
-        )
-        horiz_parts, science_parts, good_parts = [], [], []
-        for pair in range(start, start + chunk):
-            low_half = lane < STAMP_W
-            odd = jnp.where(
-                low_half, odd_ref[2 * pair : 2 * pair + 1], odd_ref[2 * pair + 1 : 2 * pair + 2] + 1
+    stack = 3
+    total = jnp.zeros((stack * FIT_ROWS, stack * FIT_ROWS), F32)
+    for begin in range(0, HALF, stack):
+        designs = []
+        for spot in range(begin, begin + stack):
+            line = first_line + spot
+            designs.append(
+                design_line(
+                    bases[spot * BASE_PAD : (spot + 1) * BASE_PAD],
+                    aux_ref[pl.ds(line, 1), :],
+                    aux_ref[pl.ds(rows + line, 1), :],
+                    horiz,
+                    profile,
+                    first_row + line,
+                    rows * stripes,
+                )
             )
-            horiz_parts.append(position(4 * pair * STAMP_W + odd * STAMP_W + lane, wide))
-            for source, parts in ((science_ref, science_parts), (good_ref, good_parts)):
-                a = source[0, :, 2 * pair * LANES : (2 * pair + 1) * LANES]
-                b = source[0, :, (2 * pair + 1) * LANES : (2 * pair + 2) * LANES]
-                a = picked(a, 2 * pair, False)
-                b = picked(b, 2 * pair + 1, True)
-                parts.append(jnp.where(lane_id(rows) < STAMP_W, a, b))
-        horiz = jnp.concatenate(horiz_parts, axis=1)
-        good = jnp.concatenate(good_parts, axis=1)
-        target = good * jnp.concatenate(science_parts, axis=1)
-        profile = jnp.concatenate(back_profile(horiz), axis=0)
-        for line in range(rows):
-            keep = good[line : line + 1]
-            own = bases[line * BASE_PAD : (line + 1) * BASE_PAD] * keep
-            vert = position(jnp.full((1, chunk * LANES), first_row + line, jnp.int32), rows * stripes)
-            square = 0.5 * (3.0 * vert * vert - 1.0)
-            steady = jnp.ones_like(vert)
-            scale = jnp.concatenate([steady, steady, vert, vert, steady, square, square], axis=0)
-            ground = profile * scale * keep
-            design = jnp.concatenate(
-                [own, own * horiz, own * vert, ground, target[line : line + 1]], axis=0
-            ).astype(BF16)
-            total = total + lax.dot_general(
-                design, design, (((1,), (1,)), ((), ())), preferred_element_type=F32
-            )
-    out_ref[...] = jnp.concatenate(
-        [total, jnp.zeros((FIT_ROWS, LANES - FIT_ROWS), F32)], axis=1
-    )
+        total = total + gram(jnp.concatenate(designs, axis=0))
+    own = total_ref[:, :FIT_ROWS]
+    for spot in range(stack):
+        where = slice(spot * FIT_ROWS, (spot + 1) * FIT_ROWS)
+        own = own + total[where, where]
+    out_ref[...] = jnp.concatenate([own, jnp.zeros((FIT_ROWS, LANES - FIT_ROWS), F32)], axis=1)
 
 
 def panels():
@@ -407,7 +611,7 @@
 
 def spread_kernel(cores, *refs):
     pieces = refs[:cores]
-    near_ref, far_ref, after_ref, xhigh, xlow, ext, highs, lows = refs[cores:]
+    far_ref, near_ref, after_ref, xhigh, xlow, ext, highs, lows = refs[cores:]
     wide = xhigh.shape[1]
     fill_extended(ext, highs, lows, cores, pieces, near_ref, far_ref)
     clear_spare((xhigh, xlow))
@@ -428,8 +632,8 @@
     normal_ref,
     xhigh,
     xlow,
+    far_ref,
     near_ref,
-    far_ref,
     science_ref,
     good_ref,
     base_ref,
@@ -543,7 +747,7 @@
 
 
 def shards(template, exposure, cosmic_mask, stamp_blocks, row_filters, col_filters):
-    arguments = (template, exposure, cosmic_mask, stamp_blocks, row_filters, col_filters)
+    arguments = (template, exposure, cosmic_mask, row_filters, col_filters, stamp_blocks)
     rows, half = template.shape
     wide = exposure.shape[2]
     cores = lax.axis_size("exp")
@@ -553,25 +757,20 @@
         lax.ppermute(template, "exp", [((i + step) % cores, i) for i in range(cores)])
         for step in range(1, cores)
     ]
-    weight_shape = jax.ShapeDtypeStruct((rows * BASE_PAD, DEPTH), BF16)
     stamps = stamp_blocks.shape[1]
-    template_in, science, good, odd, high, low, base = pl.pallas_call(
+    template_in, science, good, row_in, col_in, odd = pl.pallas_call(
         load_kernel,
         out_shape=(
             jax.ShapeDtypeStruct(template.shape, F32),
             jax.ShapeDtypeStruct(exposure.shape, F32),
             jax.ShapeDtypeStruct(exposure.shape, F32),
+            jax.ShapeDtypeStruct(row_filters.shape, F32),
+            jax.ShapeDtypeStruct(col_filters.shape, F32),
             jax.ShapeDtypeStruct((stamps, LANES), jnp.int32),
-            weight_shape,
-            weight_shape,
-            jax.ShapeDtypeStruct((BASE_PAD, DEPTH + LANES), F32),
         ),
         in_specs=[pl.BlockSpec(memory_space=pltpu.HBM)] * 6,
-        out_specs=tuple(whole_vmem(7)),
+        out_specs=tuple(whole_vmem(6)),
         scratch_shapes=[
-            pltpu.VMEM((2, BASE_PAD, LANES), F32),
-            pltpu.VMEM(row_filters.shape, F32),
-            pltpu.VMEM(col_filters.shape, F32),
             pltpu.VMEM(cosmic_mask.shape, jnp.int32),
             pltpu.SMEM(stamp_blocks.shape, jnp.int32),
             pltpu.SemaphoreType.DMA((6,)),
@@ -581,15 +780,20 @@
     )(*[pltpu.with_memory_space_constraint(array, pltpu.HBM) for array in arguments])
     pieces = [template_in] + pieces[1:]
     edge_shape = jax.ShapeDtypeStruct((24, wide // 2), F32)
-    near, far = pl.pallas_call(
-        functools.partial(edge_kernel, cores),
-        out_shape=(edge_shape, edge_shape),
-        in_specs=whole_vmem(cores + 2),
-        out_specs=tuple(whole_vmem(2)),
-        scratch_shapes=[pltpu.VMEM((rows, wide), F32)],
-        compiler_params=params,
-        name="edges",
-    )(*pieces, science, good)
+
+    def edge(toward_near, *others):
+        return pl.pallas_call(
+            functools.partial(edge_kernel, cores, toward_near),
+            out_shape=edge_shape,
+            in_specs=whole_vmem(cores + 2 + len(others)),
+            out_specs=pl.BlockSpec(memory_space=pltpu.VMEM),
+            scratch_shapes=[pltpu.VMEM((rows, wide), F32)],
+            compiler_params=params,
+            name="edges",
+        )(*pieces, science, good, *others)
+
+    far = edge(False)
+    near = edge(True)
     near_pairs = [(i, i + 1) for i in range(0, stripes - 1, 2)]
     far_pairs = [(i, i + 1) for i in range(1, stripes - 1, 2)]
 
@@ -598,24 +802,67 @@
 
     far = swapped(far, far_pairs)
     near = swapped(near, near_pairs)
+    early_shape = jax.ShapeDtypeStruct((rows * BASE_PAD, EARLY), BF16)
+    late_shape = jax.ShapeDtypeStruct((LATE_ROWS, LATE), BF16)
+    high, low, late_high, late_low, base = pl.pallas_call(
+        weight_kernel,
+        out_shape=(
+            early_shape,
+            early_shape,
+            late_shape,
+            late_shape,
+            jax.ShapeDtypeStruct((BASE_PAD, DEPTH + LANES), F32),
+        ),
+        in_specs=whole_vmem(2),
+        out_specs=tuple(whole_vmem(5)),
+        scratch_shapes=[pltpu.VMEM((2, BASE_PAD, LANES), F32)],
+        compiler_params=params,
+        name="weights",
+    )(row_in, col_in)
+    width = wide // 2
+    reach = wide + 2 * LANES
+    normal_shape = jax.ShapeDtypeStruct((FIT_ROWS, LANES), F32)
+    part, kept, aux = pl.pallas_call(
+        functools.partial(early_kernel, cores, stripes),
+        out_shape=(
+            normal_shape,
+            jax.ShapeDtypeStruct((HALF * BASE_PAD, width), F32),
+            jax.ShapeDtypeStruct((2 * rows + 8, width), F32),
+        ),
+        in_specs=whole_vmem(cores + 6),
+        out_specs=tuple(whole_vmem(3)),
+        scratch_shapes=[
+            pltpu.VMEM((rows + 16, reach), F32),
+            pltpu.VMEM((rows + 32, reach), BF16),
+            pltpu.VMEM((rows + 32, reach), BF16),
+            pltpu.VMEM((EARLY, width), BF16),
+            pltpu.VMEM((EARLY, width), BF16),
+            pltpu.VMEM(((rows - HALF) * BASE_PAD, width), F32),
+        ],
+        compiler_params=params,
+        name="early",
+    )(*pieces, near, science, good, odd, high, low)
+    normal = pl.pallas_call(
+        functools.partial(late_kernel, stripes, rows),
+        out_shape=normal_shape,
+        in_specs=whole_vmem(7),
+        out_specs=pl.BlockSpec(memory_space=pltpu.VMEM),
+        scratch_shapes=[
+            pltpu.VMEM((16, reach), F32),
+            pltpu.VMEM((32, reach), BF16),
+            pltpu.VMEM((32, reach), BF16),
+            pltpu.VMEM((LATE, width), BF16),
+            pltpu.VMEM((LATE, width), BF16),
+            pltpu.VMEM((HALF * BASE_PAD, width), F32),
+        ],
+        compiler_params=params,
+        name="late",
+    )(far, odd, late_high, late_low, part, kept, aux)
     ext_shapes = [
         pltpu.VMEM((rows + 24, wide + 2 * LANES), F32),
         pltpu.VMEM((GROUP + 16, wide + 2 * LANES), BF16),
         pltpu.VMEM((GROUP + 16, wide + 2 * LANES), BF16),
     ]
-    normal = pl.pallas_call(
-        functools.partial(fit_kernel, cores, stripes),
-        out_shape=jax.ShapeDtypeStruct((FIT_ROWS, LANES), F32),
-        in_specs=whole_vmem(cores + 7),
-        out_specs=pl.BlockSpec(memory_space=pltpu.VMEM),
-        scratch_shapes=ext_shapes
-        + [
-            pltpu.VMEM((DEPTH, wide // 2), BF16),
-            pltpu.VMEM((DEPTH, wide // 2), BF16),
-        ],
-        compiler_params=params,
-        name="fit",
-    )(*pieces, near, far, science, good, odd, high, low)
     wide_shape = jax.ShapeDtypeStruct((DEPTH, wide), BF16)
     xhigh, xlow = pl.pallas_call(
         functools.partial(spread_kernel, cores),
@@ -625,7 +872,7 @@
         scratch_shapes=ext_shapes,
         compiler_params=params,
         name="spread",
-    )(*pieces, near, far, normal)
+    )(*pieces, far, near, normal)
     normal = summed(normal, "stripe")
     filtered, coef = pl.pallas_call(
         functools.partial(model_kernel, stripes),
@@ -637,7 +884,7 @@
         out_specs=tuple(whole_vmem(2)),
         compiler_params=params,
         name="model",
-    )(normal, xhigh, xlow, near, far, science, good, base)
+    )(normal, xhigh, xlow, far, near, science, good, base)
     return filtered, coef
 
 

time: 35.2 us -> 33.1 us (0.940)
  starting transfers between devices: 15.1 us -> 12.3 us
  Pallas kernels: 12.2 us -> 14.1 us
  waiting for transfers between devices: 7 us -> 5.83 us
    ppermute x3, starting transfers between devices: 11.3 us -> 8.16 us  [summed(): lax.ppermute(values, axis, [(i, i ^ step) for i in range(count)])]
    pallas_call x2 -> x5, Pallas kernels: 3.79 us -> 6.17 us  [the longest x1 3.21 us: shards(): pl.pallas_call(functools.partial(early_kernel, cores, stripes), out_shape...]
    ppermute x2, waiting for transfers between devices: 2.79 us -> 1.57 us  [swapped(): lax.ppermute(values, 'stripe', couples + [(b, a) for a, b in couples])]
    pallas_call x1, Pallas kernels: 1.57 us -> 1.07 us  [shards(): pl.pallas_call(load_kernel, out_shape=(jax.ShapeDtypeStruct(template.shap...]
  transfers between devices with their start and end apart: 6 -> 6, of which waited for: 4 -> 4; matrix products, arithmetic and copies ran while one was open for 0% -> 0% of each run, Pallas kernels for 9% -> 21%
where the time goes in v2:
time: 33.1 us; the launch traced here: 32.9 us
  Pallas kernels  14.1 us (43%)
  starting transfers between devices  12.3 us (37%)
  waiting for transfers between devices  5.83 us (18%)
  between operations  0.7 us (2%)
    ppermute x3, starting transfers between devices, summed(): lax.ppermute(values, axis, [(i, i ^ step) for i in range(count)])  8.16 us
    pallas_call x1, Pallas kernels, shards(): pl.pallas_call(functools.partial(model_kernel, stripes), out_shape=(jax.S...  5.14 us
    ppermute x3, waiting for transfers between devices, summed(): lax.ppermute(values, axis, [(i, i ^ step) for i in range(count)])  4.22 us
    ppermute x2, starting transfers between devices, swapped(): lax.ppermute(values, 'stripe', couples + [(b, a) for a, b in couples])  3.57 us
    pallas_call x1, Pallas kernels, shards(): pl.pallas_call(functools.partial(early_kernel, cores, stripes), out_shape...  3.21 us
    pallas_call x1, Pallas kernels, shards(): pl.pallas_call(functools.partial(late_kernel, stripes, rows), out_shape=n...  2.04 us
    pallas_call x1, Pallas kernels, shards(): pl.pallas_call(functools.partial(spread_kernel, cores), out_shape=(wide_s...  1.73 us
    ppermute x2, waiting for transfers between devices, swapped(): lax.ppermute(values, 'stripe', couples + [(b, a) for a, b in couples])  1.57 us
  transfers between devices with their start and end apart: 6, of which 4 were waited for; matrix products, arithmetic and copies ran while one was open for 0% of the time, Pallas kernels for 21%

profile of v2, /device:TPU:0, one launch (start us, length us, event | category | flops | bytes accessed | tf_op | source)
XLA Modules:
  0.0 32.9 jit_solution(15280053408775174328)
XLA Ops:
  0.6 0.5 %collective-permute-start = (f32[16,1024]{1,0:T(8,128)}, f32[16,1024]{1,0:T(8,128)S(1)}, u32[]{:S(2)}, u32[]{:S(2)}) collective-permute-start(f32[16,1024]{1,0:T(8,128)} %template_hbm.1), channel_id=1, source_target_pairs={{1,0},{0,1},{3,2},{2,3},{5,4},{4,5},{7,6},{6,7},{9,8},{8,9},{11,10... | collective-permute-start | bytes 196616 | tf_op jit(solution)/shard_map/ppermute | solution.py:757
  1.1 1.1 %load.1 = (f32[16,1024]{1,0:T(8,128)S(1)}, f32[1,16,2048]{2,1,0:T(8,128)S(1)}, f32[1,16,2048]{2,1,0:T(8,128)S(1)}, f32[19,19]{1,0:T(8,128)S(1)}, f32[19,19]{1,0:T(8,128)S(1)}, /*index=5*/s32[16,128]{1,0:T(8,128)S(1)}) custom-call(f32[16,1024]{1,0:T(8,128)} %template_hbm.1, f32[1,16,2048]{2,1,0:T(8,128)} %science_hbm.1, s32[1,16,2048]{2,1,0:T(8,128)} %good_hbm.1, ...), custom_call_target="tpu_custom_call" | custom-call | tf_op jit(solution)/shard_map/load/pallas_call | solution.py:761
  2.2 0.0 collective-permute-done.refs_1_
  2.3 0.1 edges.3
  2.3 2.9 %collective-permute-start.2 = (f32[24,1024]{1,0:T(8,128)S(1)}, f32[24,1024]{1,0:T(8,128)S(1)}, u32[]{:S(2)}, u32[]{:S(2)}) collective-permute-start(f32[24,1024]{1,0:T(8,128)S(1)} %edges.3), channel_id=1, source_target_pairs={{0,2},{4,6},{8,10},{12,14},{2,0},{6,4},{10,8},{14,12},{1,3},{5,7},... | collective-permute-start | bytes 294920 | tf_op jit(solution)/shard_map/ppermute | solution.py:801
  5.2 0.1 edges.2
  5.3 0.7 %collective-permute-start.1 = (f32[24,1024]{1,0:T(8,128)S(1)}, f32[24,1024]{1,0:T(8,128)S(1)}, u32[]{:S(2)}, u32[]{:S(2)}) collective-permute-start(f32[24,1024]{1,0:T(8,128)S(1)} %edges.2), channel_id=1, source_target_pairs={{2,4},{6,8},{10,12},{4,2},{8,6},{12,10},{3,5},{7,9},{11,13},{5,3},... | collective-permute-start | bytes 294920 | tf_op jit(solution)/shard_map/ppermute | solution.py:801
  6.0 0.8 %weights.1 = (bf16[384,512]{1,0:T(8,128)(2,1)S(1)}, bf16[384,512]{1,0:T(8,128)(2,1)S(1)}, bf16[224,256]{1,0:T(8,128)(2,1)S(1)}, bf16[224,256]{1,0:T(8,128)(2,1)S(1)}, f32[24,896]{1,0:T(8,128)S(1)}) custom-call(f32[19,19]{1,0:T(8,128)S(1)} %get-tuple-element.22.row_ref, f32[19,19]{1,0:T(8,128)S(1)} %get-tuple-element.23.col_ref), custom_call_target="tpu_custom_call" | custom-call | tf_op jit(solution)/shard_map/weights/pallas_call | solution.py:807
  6.8 1.6 %collective-permute-done.2.refs_2_.refs_3_.near_ref = f32[24,1024]{1,0:T(8,128)S(1)} collective-permute-done((f32[24,1024]{1,0:T(8,128)S(1)}, f32[24,1024]{1,0:T(8,128)S(1)}, u32[]{:S(2)}, u32[]{:S(2)}) %collective-permute-start.2) | collective-permute-done | bytes 98336 | tf_op jit(solution)/shard_map/ppermute | solution.py:801
  8.4 3.2 %early.1 = (f32[80,128]{1,0:T(8,128)S(1)}, f32[216,1024]{1,0:T(8,128)S(1)}, f32[40,1024]{1,0:T(8,128)S(1)}) custom-call(f32[16,1024]{1,0:T(8,128)S(1)} %get-tuple-element.18.refs_0_, f32[16,1024]{1,0:T(8,128)S(1)} %collective-permute-done.refs_1_, f32[24,1024]{1,0:T(8,128)S(1)} %collective-permute-done.2.refs_2_.refs_3_.near_ref, ...), custom_call_target="tpu_custom_call" | custom-call | tf_op jit(solution)/shard_map/early/pallas_call | solution.py:825
  11.6 0.0 collective-permute-done.1.refs_0_.refs_2_.far_ref
  11.6 2.0 %late.1.refs_4_ = f32[80,128]{1,0:T(8,128)S(1)} custom-call(f32[24,1024]{1,0:T(8,128)S(1)} %collective-permute-done.1.refs_0_.refs_2_.far_ref, s32[16,128]{1,0:T(8,128)S(1)} %get-tuple-element.21.refs_5_.refs_1_, bf16[224,256]{1,0:T(8,128)(2,1)S(1)} %get-tuple-element.24.refs_2_, bf16[224,256]{1,0:T(8,128)(2,1)S(1)} %get-tuple-element.25.refs_3_, ...), custom_call_target="tpu_custom_call" | custom-call | tf_op jit(solution)/shard_map/late/pallas_call | solution.py:845
  13.6 2.8 %collective-permute-start.3 = (f32[80,128]{1,0:T(8,128)S(1)}, f32[80,128]{1,0:T(8,128)S(1)}, u32[]{:S(2)}, u32[]{:S(2)}) collective-permute-start(f32[80,128]{1,0:T(8,128)S(1)} %late.1.refs_4_), channel_id=1, source_target_pairs={{0,2},{2,0},{4,6},{6,4},{8,10},{10,8},{12,14},{14,12},{1,3},{3,1},... | collective-permute-start | bytes 122888 | tf_op jit(solution)/shard_map/ppermute | solution.py:744
  16.4 2.0 %collective-permute-done.3 = f32[80,128]{1,0:T(8,128)S(1)} collective-permute-done((f32[80,128]{1,0:T(8,128)S(1)}, f32[80,128]{1,0:T(8,128)S(1)}, u32[]{:S(2)}, u32[]{:S(2)}) %collective-permute-start.3) | collective-permute-done | bytes 40992 | tf_op jit(solution)/shard_map/ppermute | solution.py:744
  18.4 2.0 %collective-permute-start.4 = (f32[80,128]{1,0:T(8,128)S(1)}, f32[80,128]{1,0:T(8,128)S(1)}, u32[]{:S(2)}, u32[]{:S(2)}) collective-permute-start(f32[80,128]{1,0:T(8,128)S(1)} %add.9), channel_id=1, source_target_pairs={{0,4},{2,6},{4,0},{6,2},{8,12},{10,14},{12,8},{14,10},{1,5},{3,7},... | collective-permute-start | bytes 122888 | tf_op jit(solution)/shard_map/ppermute | solution.py:744
  20.4 2.0 %collective-permute-done.4 = f32[80,128]{1,0:T(8,128)S(1)} collective-permute-done((f32[80,128]{1,0:T(8,128)S(1)}, f32[80,128]{1,0:T(8,128)S(1)}, u32[]{:S(2)}, u32[]{:S(2)}) %collective-permute-start.4) | collective-permute-done | bytes 40992 | tf_op jit(solution)/shard_map/ppermute | solution.py:744
  22.4 3.4 %collective-permute-start.5 = (f32[80,128]{1,0:T(8,128)S(1)}, f32[80,128]{1,0:T(8,128)S(1)}, u32[]{:S(2)}, u32[]{:S(2)}) collective-permute-start(f32[80,128]{1,0:T(8,128)S(1)} %add.10), channel_id=1, source_target_pairs={{0,8},{2,10},{4,12},{6,14},{8,0},{10,2},{12,4},{14,6},{1,9},{3,11}... | collective-permute-start | bytes 122888 | tf_op jit(solution)/shard_map/ppermute | solution.py:744
  25.8 1.7 %spread.1 = (bf16[768,2048]{1,0:T(8,128)(2,1)S(1)}, bf16[768,2048]{1,0:T(8,128)(2,1)S(1)}) custom-call(f32[16,1024]{1,0:T(8,128)S(1)} %get-tuple-element.18.refs_0_, f32[16,1024]{1,0:T(8,128)S(1)} %collective-permute-done.refs_1_, f32[24,1024]{1,0:T(8,128)S(1)} %collective-permute-done.1.refs_0_.refs_2_.far_ref, ...), custom_call_target="tpu_custom_call" | custom-call | tf_op jit(solution)/shard_map/spread/pallas_call | solution.py:867
  27.5 0.2 collective-permute-done.5
  27.8 5.1 %model.1 = (f32[1,16,2048]{2,1,0:T(8,128)}, f32[1,64]{1,0:T(1,128)}) custom-call(f32[80,128]{1,0:T(8,128)S(1)} %add.11.normal_ref, bf16[768,2048]{1,0:T(8,128)(2,1)S(1)} %get-tuple-element.31.xhigh, bf16[768,2048]{1,0:T(8,128)(2,1)S(1)} %get-tuple-element.32.xlow, f32[24,1024]{1,0:T(8,128)S(1)} %collective-permute-done.1.refs_0_.refs_2_.far_ref, ...), custom_call_target="tpu_custom_call" | custom-call | tf_op jit(solution)/shard_map/model/pallas_call | solution.py:877
  (3 shorter events, 0.0 us)
Async XLA Ops:
  0.6 1.6 %collective-permute-start = (f32[16,1024]{1,0:T(8,128)}, f32[16,1024]{1,0:T(8,128)S(1)}, u32[]{:S(2)}, u32[]{:S(2)}) collective-permute-start(f32[16,1024]{1,0:T(8,128)} %template_hbm.1), channel_id=1, source_target_pairs={{1,0},{0,1},{3,2},{2,3},{5,4},{4,5},{7,6},{6,7},{9,8},{8,9},{11,10... | collective-permute-start | bytes 196616 | tf_op jit(solution)/shard_map/ppermute | solution.py:757
  2.3 6.0 %collective-permute-start.2 = (f32[24,1024]{1,0:T(8,128)S(1)}, f32[24,1024]{1,0:T(8,128)S(1)}, u32[]{:S(2)}, u32[]{:S(2)}) collective-permute-start(f32[24,1024]{1,0:T(8,128)S(1)} %edges.3), channel_id=1, source_target_pairs={{0,2},{4,6},{8,10},{12,14},{2,0},{6,4},{10,8},{14,12},{1,3},{5,7},... | collective-permute-start | bytes 294920 | tf_op jit(solution)/shard_map/ppermute | solution.py:801
  5.3 6.3 %collective-permute-start.1 = (f32[24,1024]{1,0:T(8,128)S(1)}, f32[24,1024]{1,0:T(8,128)S(1)}, u32[]{:S(2)}, u32[]{:S(2)}) collective-permute-start(f32[24,1024]{1,0:T(8,128)S(1)} %edges.2), channel_id=1, source_target_pairs={{2,4},{6,8},{10,12},{4,2},{8,6},{12,10},{3,5},{7,9},{11,13},{5,3},... | collective-permute-start | bytes 294920 | tf_op jit(solution)/shard_map/ppermute | solution.py:801
  13.6 4.8 %collective-permute-start.3 = (f32[80,128]{1,0:T(8,128)S(1)}, f32[80,128]{1,0:T(8,128)S(1)}, u32[]{:S(2)}, u32[]{:S(2)}) collective-permute-start(f32[80,128]{1,0:T(8,128)S(1)} %late.1.refs_4_), channel_id=1, source_target_pairs={{0,2},{2,0},{4,6},{6,4},{8,10},{10,8},{12,14},{14,12},{1,3},{3,1},... | collective-permute-start | bytes 122888 | tf_op jit(solution)/shard_map/ppermute | solution.py:744
  18.4 4.0 %collective-permute-start.4 = (f32[80,128]{1,0:T(8,128)S(1)}, f32[80,128]{1,0:T(8,128)S(1)}, u32[]{:S(2)}, u32[]{:S(2)}) collective-permute-start(f32[80,128]{1,0:T(8,128)S(1)} %add.9), channel_id=1, source_target_pairs={{0,4},{2,6},{4,0},{6,2},{8,12},{10,14},{12,8},{14,10},{1,5},{3,7},... | collective-permute-start | bytes 122888 | tf_op jit(solution)/shard_map/ppermute | solution.py:744
  22.4 5.4 %collective-permute-start.5 = (f32[80,128]{1,0:T(8,128)S(1)}, f32[80,128]{1,0:T(8,128)S(1)}, u32[]{:S(2)}, u32[]{:S(2)}) collective-permute-start(f32[80,128]{1,0:T(8,128)S(1)} %add.10), channel_id=1, source_target_pairs={{0,8},{2,10},{4,12},{6,14},{8,0},{10,2},{12,4},{14,6},{1,9},{3,11}... | collective-permute-start | bytes 122888 | tf_op jit(solution)/shard_map/ppermute | solution.py:744

commit v3 on v2

--- a/solution.py
+++ b/solution.py
@@ -609,37 +609,103 @@
     return jnp.where(used, jnp.broadcast_to(right, (FIT_ROWS, LANES)), 0.0)
 
 
-def spread_kernel(cores, *refs):
+def region_weights(base_ref, high_ref, low_ref, rows):
+    lane = lane_id(8)
+    spot = lax.rem(lane, GROUP)
+    corner = lax.rem(lane, 4)
+    line = row_id(8)
+    mains = [base_ref[:, tile * LANES : (tile + 1) * LANES] for tile in range(MAIN_TILES)]
+    outer = base_ref[:, MAIN : MAIN + LANES]
+    inner = base_ref[:, MAIN + LANES :]
+    blocks = [[] for _ in range(BASES)]
+    for start in range(0, rows, 8):
+        tap = spot - (start + line - 1)
+        inside = (tap >= 0) & (tap < TAPS)
+        moved = [pltpu.roll(main, (start - 1) % LANES, 1) for main in mains]
+        extra = zero_row = jnp.zeros((8, LANES), F32)
+        for b in range(BASES):
+            tiles = []
+            for main in moved:
+                wide = jnp.broadcast_to(main[b : b + 1], (8, LANES))
+                tiles.append(
+                    jnp.where(inside, pltpu.roll(wide, 0, 1, stride=1, stride_axis=0), 0.0)
+                )
+            extra = zero_row
+            mine = jnp.broadcast_to(inner[b : b + 1], (8, LANES))
+            if start == 0:
+                extra = jnp.where((line == 0) & (corner < 2), mine, extra)
+            if start == rows - 8:
+                extra = jnp.where((line == 7) & (corner >= 2), mine, extra)
+            blocks[b].append(jnp.concatenate(tiles + [extra], axis=1))
+    for b in range(BASES):
+        where = pl.ds(b * rows, rows)
+        high_ref[where, :], low_ref[where, :] = split_two(jnp.concatenate(blocks[b], axis=0))
+    lane = lane_id(BASE_PAD)
+    spot = lax.rem(lane, GROUP)
+    corner = lax.rem(lane, 4)
+    halos = []
+    for shift, extra in ((rows - 1, corner >= 2), (-2, corner < 2)):
+        tap = spot - shift
+        inside = (tap >= 0) & (tap < TAPS)
+        tiles = [jnp.where(inside, pltpu.roll(main, shift % LANES, 1), 0.0) for main in mains]
+        halos.append(jnp.concatenate(tiles + [jnp.where(extra, outer, 0.0)], axis=1))
+    where = pl.ds(BASES * rows, 2 * BASE_PAD)
+    high_ref[where, :], low_ref[where, :] = split_two(jnp.concatenate(halos, axis=0))
+
+
+def region_bases(highs, lows, high_ref, low_ref, first, out_ref, xhigh, xlow):
+    clear_spare((xhigh, xlow))
+    wide = out_ref.shape[1]
+    chunk = 2 * LANES
+    for start in range(0, wide, chunk):
+        span = slice(start, start + chunk)
+        for source, target in ((highs, xhigh), (lows, xlow)):
+
+            def shifted(tap, lines):
+                begin = first + start + LANES - HALF + tap
+                return source[lines, begin : begin + chunk]
+
+            def put(place, values):
+                target[place : place + values.shape[0], span] = values
+
+            spread_window(shifted, put)
+        out_ref[:, span] = three_products(
+            high_ref[...], low_ref[...], xhigh[:, span], xlow[:, span]
+        )
+
+
+def first_bases_kernel(cores, *refs):
     pieces = refs[:cores]
-    far_ref, near_ref, after_ref, xhigh, xlow, ext, highs, lows = refs[cores:]
-    wide = xhigh.shape[1]
+    (
+        far_ref,
+        near_ref,
+        base_ref,
+        after_ref,
+        high_ref,
+        low_ref,
+        highs,
+        lows,
+        out_ref,
+        ext,
+        xhigh,
+        xlow,
+    ) = refs[cores:]
+    region_weights(base_ref, high_ref, low_ref, pieces[0].shape[0])
     fill_extended(ext, highs, lows, cores, pieces, near_ref, far_ref)
-    clear_spare((xhigh, xlow))
-    for source, target in ((highs, xhigh), (lows, xlow)):
-
-        def shifted(tap, lines):
-            start = LANES - HALF + tap
-            return source[lines, start : start + wide]
-
-        def put(place, values):
-            target[place : place + values.shape[0]] = values
-
-        spread_window(shifted, put)
-
-
-def model_kernel(
-    stripes,
-    normal_ref,
-    xhigh,
-    xlow,
-    far_ref,
-    near_ref,
-    science_ref,
-    good_ref,
-    base_ref,
-    out_ref,
-    coef_ref,
-):
+    region_bases(highs, lows, high_ref, low_ref, 0, out_ref, xhigh, xlow)
+
+
+def next_bases_kernel(first, highs, lows, high_ref, low_ref, after_ref, out_ref, xhigh, xlow):
+    region_bases(highs, lows, high_ref, low_ref, first, out_ref, xhigh, xlow)
+
+
+def add_kernel(mine_ref, other_ref, after_ref, out_ref):
+    out_ref[...] = mine_ref[...] + other_ref[...]
+
+
+def model_kernel(stripes, normal_ref, *refs):
+    far_ref, near_ref, science_ref, good_ref, out_ref, coef_ref = refs[-6:]
+    parts = refs[:-6]
     rows = science_ref.shape[1]
     wide = science_ref.shape[2]
     top, bottom = edges_of(near_ref, far_ref)
@@ -651,77 +717,63 @@
     flat = jnp.sum(jnp.where(row_id(FIT_ROWS) == home, coef, 0.0), axis=0, keepdims=True)
     coef_ref[...] = flat[:, : coef_ref.shape[1]]
 
-    line = row_id(BASE_PAD)
-    lane = lane_id(BASE_PAD)
-    spot = lax.rem(lane, GROUP)
-    shift = jnp.where(line == rows + 1, -2, line - 1)
-    tap = spot - shift
-    inside = (tap >= 0) & (tap < TAPS)
-    corner = lax.rem(lane, 4)
-    blocks = []
-    for term in range(3):
-        share = coef[term * BASE_PAD : (term + 1) * BASE_PAD]
-        parts = []
-        for tile in range(MAIN_TILES + 2):
-            mixed = base_ref[:, tile * LANES : (tile + 1) * LANES] * share
-            parts.append(jnp.broadcast_to(jnp.sum(mixed, axis=0, keepdims=True), (BASE_PAD, LANES)))
-        wanted = []
-        for tile in range(MAIN_TILES):
-            moved = jnp.concatenate(
-                [
-                    pltpu.roll(
-                        pltpu.roll(parts[tile][:8], (start - 1) % LANES, 1), 0, 1, stride=1, stride_axis=0
-                    )
-                    for start in range(0, BASE_PAD, 8)
-                ],
-                axis=0,
+    def share(spot, height):
+        return jnp.broadcast_to(coef[spot : spot + 1], (height, LANES))
+
+    first_row = lax.axis_index("stripe") * rows
+    vert = position(first_row + row_id(rows), rows * stripes)
+    halo_vert = [
+        position(jnp.full((8, LANES), first_row + line, jnp.int32), rows * stripes)
+        for line in (rows, -1)
+    ]
+    slopes = [share(2 * BASE_PAD + b, rows) * vert for b in range(BASES)]
+    halo_slopes = [
+        coef[2 * BASE_PAD : 3 * BASE_PAD] * jnp.concatenate([line] * 3, axis=0) for line in halo_vert
+    ]
+    level = [share(3 * BASE_PAD + m, 8) for m in range(BACK)]
+
+    def ground(here, horiz):
+        square = 0.5 * (3.0 * here * here - 1.0)
+        horiz_square = 0.5 * (3.0 * horiz * horiz - 1.0)
+        steady = level[0] + level[1] * horiz + level[4] * horiz_square
+        sloped = level[2] + level[3] * horiz
+        curved = level[5] + level[6] * horiz
+        if here.shape[0] > 8:
+            steady, sloped, curved = (
+                jnp.concatenate([part] * (here.shape[0] // 8), axis=0)
+                for part in (steady, sloped, curved)
             )
-            moved = jnp.where(line == rows + 1, pltpu.roll(parts[tile], LANES - 2, 1), moved)
-            wanted.append(jnp.where(inside, moved, 0.0))
-        outer, inner = parts[MAIN_TILES], parts[MAIN_TILES + 1]
-        spare = jnp.where((line == rows + 1) & (corner < 2), outer, 0.0)
-        spare = jnp.where((line == 0) & (corner < 2), inner, spare)
-        spare = jnp.where((line == rows - 1) & (corner >= 2), inner, spare)
-        spare = jnp.where((line == rows) & (corner >= 2), outer, spare)
-        wanted.append(spare)
-        blocks.append(jnp.concatenate(wanted, axis=1))
-    blocks.append(jnp.zeros((8, DEPTH), F32))
-    kernel_high, kernel_low = split_two(jnp.concatenate(blocks, axis=0))
-    kernel_gap = kernel_high.shape[0]
-    kernel_both = jnp.concatenate([kernel_high, kernel_low], axis=0)
-    level = [coef[3 * BASE_PAD + m : 3 * BASE_PAD + m + 1, 0:1] for m in range(BACK)]
-    first_row = lax.axis_index("stripe") * rows
-    vert_line = jnp.where(line == rows + 1, -1, line)
-    vert = position(first_row + vert_line, rows * stripes)[:, 0:1]
-    vert_square = 0.5 * (3.0 * vert * vert - 1.0)
-    chunk = min(4 * LANES, wide)
-    outs = []
-    for start in range(0, wide, chunk):
-        span = slice(start, start + chunk)
-        both = jnp.dot(kernel_both, xhigh[:, span], preferred_element_type=F32)
-        lower = jnp.dot(kernel_high, xlow[:, span], preferred_element_type=F32)
-        sums = both[: 3 * BASE_PAD] + (both[kernel_gap : kernel_gap + 3 * BASE_PAD] + lower[: 3 * BASE_PAD])
-        horiz = position(start + lax.broadcasted_iota(jnp.int32, (1, chunk), 1), wide)
-        horiz_square = 0.5 * (3.0 * horiz * horiz - 1.0)
-        model = (
-            sums[:BASE_PAD]
-            + horiz * sums[BASE_PAD : 2 * BASE_PAD]
-            + vert * sums[2 * BASE_PAD :]
-            + (level[0] + level[1] * horiz + level[4] * horiz_square)
-            + vert * (level[2] + level[3] * horiz)
-            + vert_square * (level[5] + level[6] * horiz)
-        )
-        outs.append(model)
-    model = jnp.concatenate(outs, axis=1)
-    own = good_ref[0] * (science_ref[0] - model[:rows])
-
-    def halo(edge, spot):
+        return steady + here * sloped + square * curved
+
+    models, halos = [], [[], []]
+    for part in parts:
+        for start in range(0, part.shape[1], LANES):
+            span = slice(start, start + LANES)
+            begin = len(models) * LANES
+            horiz = position(begin + lane_id(8), wide)
+            total = ground(vert, horiz)
+            for b in range(BASES):
+                steady = share(b, 8) + share(BASE_PAD + b, 8) * horiz
+                scale = jnp.concatenate([steady] * (rows // 8), axis=0) + slopes[b]
+                total = total + part[b * rows : (b + 1) * rows, span] * scale
+            models.append(total)
+            steady = coef[:BASE_PAD] + coef[BASE_PAD : 2 * BASE_PAD] * horiz[0:1]
+            for side in range(2):
+                place = BASES * rows + side * BASE_PAD
+                values = part[place : place + BASE_PAD, span] * (steady + halo_slopes[side])
+                values = jnp.sum(values, axis=0, keepdims=True)
+                halos[side].append(values + ground(halo_vert[side], horiz)[0:1])
+    model = jnp.concatenate(models, axis=1)
+    below_model, above_model = (jnp.concatenate(side, axis=1) for side in halos)
+    own = good_ref[0] * (science_ref[0] - model)
+
+    def halo(edge, values):
         science = jnp.concatenate([edge[20:21], edge[21:22]], axis=1)
         good = jnp.concatenate([edge[22:23], edge[23:24]], axis=1)
-        return good * (science - model[spot : spot + 1])
-
-    above_row = halo(top, rows + 1)
-    below_row = halo(bottom, rows)
+        return good * (science - values)
+
+    above_row = halo(top, above_model)
+    below_row = halo(bottom, below_model)
     lines = lax.broadcasted_iota(jnp.int32, (rows, wide), 0)
     spots = lax.broadcasted_iota(jnp.int32, (rows, wide), 1)
     above = jnp.where(lines == 0, above_row, pltpu.roll(own, 1, 0))
@@ -735,14 +787,34 @@
     return [pl.BlockSpec(memory_space=pltpu.VMEM)] * count
 
 
-def summed(values, axis):
+def add(values, other, after, params):
+    return pl.pallas_call(
+        add_kernel,
+        out_shape=jax.ShapeDtypeStruct(values.shape, values.dtype),
+        in_specs=whole_vmem(3),
+        out_specs=pl.BlockSpec(memory_space=pltpu.VMEM),
+        compiler_params=params,
+        name="add",
+    )(values, other, after)
+
+
+def summed(values, axis, beside, params):
     count = lax.axis_size(axis)
     if count & (count - 1):
+        for work in beside:
+            work(values)
         return lax.psum(values, axis)
     step = 1
+    waiting = list(beside)
     while step < count:
-        values = values + lax.ppermute(values, axis, [(i, i ^ step) for i in range(count)])
+        other = lax.ppermute(values, axis, [(i, i ^ step) for i in range(count)])
+        if waiting:
+            values = add(values, other, waiting.pop(0)(values), params)
+        else:
+            values = values + other
         step *= 2
+    for work in waiting:
+        work(values)
     return values
 
 
@@ -858,33 +930,65 @@
         compiler_params=params,
         name="late",
     )(far, odd, late_high, late_low, part, kept, aux)
-    ext_shapes = [
-        pltpu.VMEM((rows + 24, wide + 2 * LANES), F32),
-        pltpu.VMEM((GROUP + 16, wide + 2 * LANES), BF16),
-        pltpu.VMEM((GROUP + 16, wide + 2 * LANES), BF16),
-    ]
-    wide_shape = jax.ShapeDtypeStruct((DEPTH, wide), BF16)
-    xhigh, xlow = pl.pallas_call(
-        functools.partial(spread_kernel, cores),
-        out_shape=(wide_shape, wide_shape),
-        in_specs=whole_vmem(cores + 3),
-        out_specs=tuple(whole_vmem(2)),
-        scratch_shapes=ext_shapes,
-        compiler_params=params,
-        name="spread",
-    )(*pieces, far, near, normal)
-    normal = summed(normal, "stripe")
+    region_rows = BASES * rows + 2 * BASE_PAD
+    blocks = wide // (2 * LANES)
+    cuts = [blocks * cut // 8 * 2 * LANES for cut in (0, 2, 5, 8)]
+    weight_shape = jax.ShapeDtypeStruct((region_rows, DEPTH), BF16)
+    source_shape = jax.ShapeDtypeStruct((GROUP + 16, reach), BF16)
+    parts, shared = [], []
+
+    def shift_scratch(size):
+        return [pltpu.VMEM((DEPTH, size), BF16)] * 2
+
+    def first_bases(after):
+        size = cuts[1]
+        *made, part = pl.pallas_call(
+            functools.partial(first_bases_kernel, cores),
+            out_shape=(
+                weight_shape,
+                weight_shape,
+                source_shape,
+                source_shape,
+                jax.ShapeDtypeStruct((region_rows, size), F32),
+            ),
+            in_specs=whole_vmem(cores + 4),
+            out_specs=tuple(whole_vmem(5)),
+            scratch_shapes=[pltpu.VMEM((rows + 24, reach), F32)] + shift_scratch(size),
+            compiler_params=params,
+            name="bases",
+        )(*pieces, far, near, base, after)
+        shared.extend(made)
+        parts.append(part)
+        return part
+
+    def next_bases(cut, after):
+        size = cuts[cut + 1] - cuts[cut]
+        high, low, highs, lows = shared
+        part = pl.pallas_call(
+            functools.partial(next_bases_kernel, cuts[cut]),
+            out_shape=jax.ShapeDtypeStruct((region_rows, size), F32),
+            in_specs=whole_vmem(5),
+            out_specs=pl.BlockSpec(memory_space=pltpu.VMEM),
+            scratch_shapes=shift_scratch(size),
+            compiler_params=params,
+            name="bases",
+        )(highs, lows, high, low, after)
+        parts.append(part)
+        return part
+
+    beside = [first_bases, functools.partial(next_bases, 1), functools.partial(next_bases, 2)]
+    normal = summed(normal, "stripe", beside, params)
     filtered, coef = pl.pallas_call(
         functools.partial(model_kernel, stripes),
         out_shape=(
             jax.ShapeDtypeStruct(exposure.shape, F32),
             jax.ShapeDtypeStruct((1, 3 * BASES + BACK), F32),
         ),
-        in_specs=whole_vmem(8),
+        in_specs=whole_vmem(1 + len(parts) + 4),
         out_specs=tuple(whole_vmem(2)),
         compiler_params=params,
         name="model",
-    )(normal, xhigh, xlow, far, near, science, good, base)
+    )(normal, *parts, far, near, science, good)
     return filtered, coef
 
 

time: 33.1 us -> 31.2 us (0.943)
  waiting for transfers between devices: 5.83 us -> 2.63 us
  Pallas kernels: 14.1 us -> 15.8 us
  starting transfers between devices: 12.3 us -> 11.9 us
    pallas_call x1 -> x6, Pallas kernels: 1.73 us -> 4.94 us  [the longest x2 3.24 us: next_bases(): pl.pallas_call(functools.partial(next_bases_kernel, cuts[cut]), out_shape...]
    ppermute x3, waiting for transfers between devices: 4.22 us -> 1.02 us  [summed(): other = lax.ppermute(values, axis, [(i, i ^ step) for i in range(count)])]
    pallas_call x1, Pallas kernels: 5.14 us -> 3.59 us  [shards(): pl.pallas_call(functools.partial(model_kernel, stripes), out_shape=(jax.S...]
    ppermute x3, starting transfers between devices: 8.16 us -> 7.81 us  [summed(): other = lax.ppermute(values, axis, [(i, i ^ step) for i in range(count)])]
  transfers between devices with their start and end apart: 6 -> 6, of which waited for: 4 -> 4; matrix products, arithmetic and copies ran while one was open for 0% -> 0% of each run, Pallas kernels for 21% -> 32%
where the time goes in v3:
time: 31.2 us; the launch traced here: 31 us
  Pallas kernels  15.8 us (51%)
  starting transfers between devices  11.9 us (38%)
  waiting for transfers between devices  2.63 us (8%)
  between operations  0.71 us (2%)
    ppermute x3, starting transfers between devices, summed(): other = lax.ppermute(values, axis, [(i, i ^ step) for i in range(count)])  7.81 us
    pallas_call x1, Pallas kernels, shards(): pl.pallas_call(functools.partial(model_kernel, stripes), out_shape=(jax.S...  3.59 us
    ppermute x2, starting transfers between devices, swapped(): lax.ppermute(values, 'stripe', couples + [(b, a) for a, b in couples])  3.57 us
    pallas_call x2, Pallas kernels, next_bases(): pl.pallas_call(functools.partial(next_bases_kernel, cuts[cut]), out_shape...  3.24 us
    pallas_call x1, Pallas kernels, shards(): pl.pallas_call(functools.partial(early_kernel, cores, stripes), out_shape...  3.2 us
    pallas_call x1, Pallas kernels, shards(): pl.pallas_call(functools.partial(late_kernel, stripes, rows), out_shape=n...  2.04 us
    pallas_call x1, Pallas kernels, first_bases(): pl.pallas_call(functools.partial(first_bases_kernel, cores), out_shape=(w...  1.68 us
    ppermute x2, waiting for transfers between devices, swapped(): lax.ppermute(values, 'stripe', couples + [(b, a) for a, b in couples])  1.57 us
  transfers between devices with their start and end apart: 6, of which 4 were waited for; matrix products, arithmetic and copies ran while one was open for 0% of the time, Pallas kernels for 32%

profile of v3, /device:TPU:0, one launch (start us, length us, event | category | flops | bytes accessed | tf_op | source)
XLA Modules:
  0.0 31.0 jit_solution(5772302844793539651)
XLA Ops:
  0.6 0.5 %collective-permute-start = (f32[16,1024]{1,0:T(8,128)}, f32[16,1024]{1,0:T(8,128)S(1)}, u32[]{:S(2)}, u32[]{:S(2)}) collective-permute-start(f32[16,1024]{1,0:T(8,128)} %template_hbm.1), channel_id=1, source_target_pairs={{1,0},{0,1},{3,2},{2,3},{5,4},{4,5},{7,6},{6,7},{9,8},{8,9},{11,10... | collective-permute-start | bytes 196616 | tf_op jit(solution)/shard_map/ppermute | solution.py:829
  1.1 1.1 %load.1 = (f32[16,1024]{1,0:T(8,128)S(1)}, f32[1,16,2048]{2,1,0:T(8,128)S(1)}, f32[1,16,2048]{2,1,0:T(8,128)S(1)}, f32[19,19]{1,0:T(8,128)S(1)}, f32[19,19]{1,0:T(8,128)S(1)}, /*index=5*/s32[16,128]{1,0:T(8,128)S(1)}) custom-call(f32[16,1024]{1,0:T(8,128)} %template_hbm.1, f32[1,16,2048]{2,1,0:T(8,128)} %science_hbm.1, s32[1,16,2048]{2,1,0:T(8,128)} %good_hbm.1, ...), custom_call_target="tpu_custom_call" | custom-call | tf_op jit(solution)/shard_map/load/pallas_call | solution.py:833
  2.2 0.0 collective-permute-done.refs_1_
  2.3 0.1 edges.3
  2.3 2.9 %collective-permute-start.2 = (f32[24,1024]{1,0:T(8,128)S(1)}, f32[24,1024]{1,0:T(8,128)S(1)}, u32[]{:S(2)}, u32[]{:S(2)}) collective-permute-start(f32[24,1024]{1,0:T(8,128)S(1)} %edges.3), channel_id=1, source_target_pairs={{0,2},{4,6},{8,10},{12,14},{2,0},{6,4},{10,8},{14,12},{1,3},{5,7},... | collective-permute-start | bytes 294920 | tf_op jit(solution)/shard_map/ppermute | solution.py:873
  5.2 0.1 edges.2
  5.3 0.7 %collective-permute-start.1 = (f32[24,1024]{1,0:T(8,128)S(1)}, f32[24,1024]{1,0:T(8,128)S(1)}, u32[]{:S(2)}, u32[]{:S(2)}) collective-permute-start(f32[24,1024]{1,0:T(8,128)S(1)} %edges.2), channel_id=1, source_target_pairs={{2,4},{6,8},{10,12},{4,2},{8,6},{12,10},{3,5},{7,9},{11,13},{5,3},... | collective-permute-start | bytes 294920 | tf_op jit(solution)/shard_map/ppermute | solution.py:873
  6.0 0.8 %weights.1 = (bf16[384,512]{1,0:T(8,128)(2,1)S(1)}, bf16[384,512]{1,0:T(8,128)(2,1)S(1)}, bf16[224,256]{1,0:T(8,128)(2,1)S(1)}, bf16[224,256]{1,0:T(8,128)(2,1)S(1)}, f32[24,896]{1,0:T(8,128)S(1)}) custom-call(f32[19,19]{1,0:T(8,128)S(1)} %get-tuple-element.25.row_ref, f32[19,19]{1,0:T(8,128)S(1)} %get-tuple-element.26.col_ref), custom_call_target="tpu_custom_call" | custom-call | tf_op jit(solution)/shard_map/weights/pallas_call | solution.py:879
  6.8 1.6 %collective-permute-done.2.refs_2_.refs_3_.refs_4_ = f32[24,1024]{1,0:T(8,128)S(1)} collective-permute-done((f32[24,1024]{1,0:T(8,128)S(1)}, f32[24,1024]{1,0:T(8,128)S(1)}, u32[]{:S(2)}, u32[]{:S(2)}) %collective-permute-start.2) | collective-permute-done | bytes 98336 | tf_op jit(solution)/shard_map/ppermute | solution.py:873
  8.4 3.2 %early.1 = (f32[80,128]{1,0:T(8,128)S(1)}, f32[216,1024]{1,0:T(8,128)S(1)}, f32[40,1024]{1,0:T(8,128)S(1)}) custom-call(f32[16,1024]{1,0:T(8,128)S(1)} %get-tuple-element.21.refs_0_, f32[16,1024]{1,0:T(8,128)S(1)} %collective-permute-done.refs_1_, f32[24,1024]{1,0:T(8,128)S(1)} %collective-permute-done.2.refs_2_.refs_3_.refs_4_, ...), custom_call_target="tpu_custom_call" | custom-call | tf_op jit(solution)/shard_map/early/pallas_call | solution.py:897
  11.6 0.0 collective-permute-done.1.refs_0_.refs_2_.refs_3_
  11.6 2.0 %late.1.refs_5_.mine_ref = f32[80,128]{1,0:T(8,128)S(1)} custom-call(f32[24,1024]{1,0:T(8,128)S(1)} %collective-permute-done.1.refs_0_.refs_2_.refs_3_, s32[16,128]{1,0:T(8,128)S(1)} %get-tuple-element.24.refs_5_.refs_1_, bf16[224,256]{1,0:T(8,128)(2,1)S(1)} %get-tuple-element.27.refs_2_, bf16[224,256]{1,0:T(8,128)(2,1)S(1)} %get-tuple-element.28.refs_3_, ...), custom_call_target="tpu_custom_call" | custom-call | tf_op jit(solution)/shard_map/late/pallas_call | solution.py:917
  13.6 2.8 %collective-permute-start.3 = (f32[80,128]{1,0:T(8,128)S(1)}, f32[80,128]{1,0:T(8,128)S(1)}, u32[]{:S(2)}, u32[]{:S(2)}) collective-permute-start(f32[80,128]{1,0:T(8,128)S(1)} %late.1.refs_5_.mine_ref), channel_id=1, source_target_pairs={{0,2},{2,0},{4,6},{6,4},{8,10},{10,8},{12,14},{14,12},{1,3},{3,1},... | collective-permute-start | bytes 122888 | tf_op jit(solution)/shard_map/ppermute | solution.py:810
  16.4 1.7 %bases.3 = (bf16[352,768]{1,0:T(8,128)(2,1)S(1)}, bf16[352,768]{1,0:T(8,128)(2,1)S(1)}, bf16[48,2304]{1,0:T(8,128)(2,1)S(1)}, bf16[48,2304]{1,0:T(8,128)(2,1)S(1)}, f32[352,512]{1,0:T(8,128)S(1)}) custom-call(f32[16,1024]{1,0:T(8,128)S(1)} %get-tuple-element.21.refs_0_, f32[16,1024]{1,0:T(8,128)S(1)} %collective-permute-done.refs_1_, ...), custom_call_target="tpu_custom_call" | custom-call | tf_op jit(solution)/shard_map/bases/pallas_call | solution.py:945
  18.1 0.3 collective-permute-done.3.other_ref
  18.4 2.0 %collective-permute-start.4 = (f32[80,128]{1,0:T(8,128)S(1)}, f32[80,128]{1,0:T(8,128)S(1)}, u32[]{:S(2)}, u32[]{:S(2)}) collective-permute-start(f32[80,128]{1,0:T(8,128)S(1)} %add.3.after_ref.mine_ref), channel_id=1, source_target_pairs={{0,4},{2,6},{4,0},{6,2},{8,12},{10,14},{12,8},{14,10},{1,5},{3,7},... | collective-permute-start | bytes 122888 | tf_op jit(solution)/shard_map/ppermute | solution.py:810
  20.4 1.6 %bases.4.after_ref.refs_1_ = f32[352,768]{1,0:T(8,128)S(1)} custom-call(bf16[48,2304]{1,0:T(8,128)(2,1)S(1)} %get-tuple-element.36.highs, bf16[48,2304]{1,0:T(8,128)(2,1)S(1)} %get-tuple-element.37.lows, bf16[352,768]{1,0:T(8,128)(2,1)S(1)} %get-tuple-element.38.high_ref, bf16[352,768]{1,0:T(8,128)(2,1)S(1)} %get-tuple-element.39.low_ref, ...), custom_call_target="tpu_custom_call" | custom-call | tf_op jit(solution)/shard_map/bases/pallas_call | solution.py:967
  22.0 0.4 %collective-permute-done.4.other_ref = f32[80,128]{1,0:T(8,128)S(1)} collective-permute-done((f32[80,128]{1,0:T(8,128)S(1)}, f32[80,128]{1,0:T(8,128)S(1)}, u32[]{:S(2)}, u32[]{:S(2)}) %collective-permute-start.4) | collective-permute-done | bytes 40992 | tf_op jit(solution)/shard_map/ppermute | solution.py:810
  22.4 3.0 %collective-permute-start.5 = (f32[80,128]{1,0:T(8,128)S(1)}, f32[80,128]{1,0:T(8,128)S(1)}, u32[]{:S(2)}, u32[]{:S(2)}) collective-permute-start(f32[80,128]{1,0:T(8,128)S(1)} %add.4.after_ref.mine_ref), channel_id=1, source_target_pairs={{0,8},{2,10},{4,12},{6,14},{8,0},{10,2},{12,4},{14,6},{1,9},{3,11}... | collective-permute-start | bytes 122888 | tf_op jit(solution)/shard_map/ppermute | solution.py:810
  25.4 1.6 %bases.5.after_ref.refs_2_ = f32[352,768]{1,0:T(8,128)S(1)} custom-call(bf16[48,2304]{1,0:T(8,128)(2,1)S(1)} %get-tuple-element.36.highs, bf16[48,2304]{1,0:T(8,128)(2,1)S(1)} %get-tuple-element.37.lows, bf16[352,768]{1,0:T(8,128)(2,1)S(1)} %get-tuple-element.38.high_ref, bf16[352,768]{1,0:T(8,128)(2,1)S(1)} %get-tuple-element.39.low_ref, ...), custom_call_target="tpu_custom_call" | custom-call | tf_op jit(solution)/shard_map/bases/pallas_call | solution.py:967
  27.1 0.4 %collective-permute-done.5.other_ref = f32[80,128]{1,0:T(8,128)S(1)} collective-permute-done((f32[80,128]{1,0:T(8,128)S(1)}, f32[80,128]{1,0:T(8,128)S(1)}, u32[]{:S(2)}, u32[]{:S(2)}) %collective-permute-start.5) | collective-permute-done | bytes 40992 | tf_op jit(solution)/shard_map/ppermute | solution.py:810
  27.4 3.6 %model.1 = (f32[1,16,2048]{2,1,0:T(8,128)}, f32[1,64]{1,0:T(1,128)}) custom-call(f32[80,128]{1,0:T(8,128)S(1)} %add.5.normal_ref, f32[352,512]{1,0:T(8,128)S(1)} %get-tuple-element.35.after_ref.refs_0_, f32[352,768]{1,0:T(8,128)S(1)} %bases.4.after_ref.refs_1_, f32[352,768]{1,0:T(8,128)S(1)} %bases.5.after_ref.refs_2_, ...), custom_call_target="tpu_custom_call" | custom-call | tf_op jit(solution)/shard_map/model/pallas_call | solution.py:981
  (3 shorter events, 0.0 us)
Async XLA Ops:
  0.6 1.6 %collective-permute-start = (f32[16,1024]{1,0:T(8,128)}, f32[16,1024]{1,0:T(8,128)S(1)}, u32[]{:S(2)}, u32[]{:S(2)}) collective-permute-start(f32[16,1024]{1,0:T(8,128)} %template_hbm.1), channel_id=1, source_target_pairs={{1,0},{0,1},{3,2},{2,3},{5,4},{4,5},{7,6},{6,7},{9,8},{8,9},{11,10... | collective-permute-start | bytes 196616 | tf_op jit(solution)/shard_map/ppermute | solution.py:829
  2.3 6.0 %collective-permute-start.2 = (f32[24,1024]{1,0:T(8,128)S(1)}, f32[24,1024]{1,0:T(8,128)S(1)}, u32[]{:S(2)}, u32[]{:S(2)}) collective-permute-start(f32[24,1024]{1,0:T(8,128)S(1)} %edges.3), channel_id=1, source_target_pairs={{0,2},{4,6},{8,10},{12,14},{2,0},{6,4},{10,8},{14,12},{1,3},{5,7},... | collective-permute-start | bytes 294920 | tf_op jit(solution)/shard_map/ppermute | solution.py:873
  5.3 6.3 %collective-permute-start.1 = (f32[24,1024]{1,0:T(8,128)S(1)}, f32[24,1024]{1,0:T(8,128)S(1)}, u32[]{:S(2)}, u32[]{:S(2)}) collective-permute-start(f32[24,1024]{1,0:T(8,128)S(1)} %edges.2), channel_id=1, source_target_pairs={{2,4},{6,8},{10,12},{4,2},{8,6},{12,10},{3,5},{7,9},{11,13},{5,3},... | collective-permute-start | bytes 294920 | tf_op jit(solution)/shard_map/ppermute | solution.py:873
  13.6 4.8 %collective-permute-start.3 = (f32[80,128]{1,0:T(8,128)S(1)}, f32[80,128]{1,0:T(8,128)S(1)}, u32[]{:S(2)}, u32[]{:S(2)}) collective-permute-start(f32[80,128]{1,0:T(8,128)S(1)} %late.1.refs_5_.mine_ref), channel_id=1, source_target_pairs={{0,2},{2,0},{4,6},{6,4},{8,10},{10,8},{12,14},{14,12},{1,3},{3,1},... | collective-permute-start | bytes 122888 | tf_op jit(solution)/shard_map/ppermute | solution.py:810
  18.4 4.0 %collective-permute-start.4 = (f32[80,128]{1,0:T(8,128)S(1)}, f32[80,128]{1,0:T(8,128)S(1)}, u32[]{:S(2)}, u32[]{:S(2)}) collective-permute-start(f32[80,128]{1,0:T(8,128)S(1)} %add.3.after_ref.mine_ref), channel_id=1, source_target_pairs={{0,4},{2,6},{4,0},{6,2},{8,12},{10,14},{12,8},{14,10},{1,5},{3,7},... | collective-permute-start | bytes 122888 | tf_op jit(solution)/shard_map/ppermute | solution.py:810
  22.4 5.0 %collective-permute-start.5 = (f32[80,128]{1,0:T(8,128)S(1)}, f32[80,128]{1,0:T(8,128)S(1)}, u32[]{:S(2)}, u32[]{:S(2)}) collective-permute-start(f32[80,128]{1,0:T(8,128)S(1)} %add.4.after_ref.mine_ref), channel_id=1, source_target_pairs={{0,8},{2,10},{4,12},{6,14},{8,0},{10,2},{12,4},{14,6},{1,9},{3,11}... | collective-permute-start | bytes 122888 | tf_op jit(solution)/shard_map/ppermute | solution.py:810

commit v4 on v3

--- a/solution.py
+++ b/solution.py
@@ -14,7 +14,10 @@
 LANES = 128
 BASE_PAD = 24
 BACK = 7
-FIT_ROWS = 3 * BASE_PAD + BACK + 1
+FIT_ROWS = 3 * BASE_PAD
+BACK_FIRST = BASE_PAD - BASES
+TARGET = BASE_PAD + BASES + BACK - BACK_FIRST
+PACKED = 2 * BASE_PAD
 REACH = HALF + 1
 GROUP = 32
 GROUPS_TILE = LANES // GROUP
@@ -386,6 +389,22 @@
             )
 
 
+def stamp_values(sources, odd_ref, pair, moves):
+    out = []
+    for source in sources:
+        first = stamp_window(source, odd_ref, 2 * pair, 0)
+        second = stamp_window(source, odd_ref, 2 * pair + 1, STAMP_W)
+        tiles = []
+        for tile, move in moves:
+            a, b = first[16 * tile : 16 * tile + 16], second[16 * tile : 16 * tile + 16]
+            if move:
+                a = pltpu.roll(a, LANES - move, 1)
+                b = pltpu.roll(b, LANES - move, 1)
+            tiles.append(jnp.where(lane_id(16) < STAMP_W, a, b))
+        out.append(jnp.concatenate(tiles, axis=0))
+    return out
+
+
 def three_products(high, low, xhigh, xlow):
     return (
         jnp.dot(high, xhigh, preferred_element_type=F32)
@@ -394,18 +413,31 @@
     )
 
 
-def design_line(bases, keep, target, horiz, profile, row, region_rows):
+def back_rows(rows):
+    empty = jnp.zeros_like(rows[0])
+    lead = [empty] * (8 - BACK_FIRST)
+    second = lead + rows[BACK_FIRST:]
+    second += [empty] * (8 - len(second))
+    return [jnp.concatenate(part, axis=0) for part in (lead + rows[:BACK_FIRST], second)]
+
+
+def design_line(bases, keep, target, horiz, profiles, row, region_rows):
     own = bases * keep
     vert = position(jnp.full(horiz.shape, row, jnp.int32), region_rows)
     square = 0.5 * (3.0 * vert * vert - 1.0)
     steady = jnp.ones_like(vert)
-    scale = jnp.concatenate([steady, steady, vert, vert, steady, square, square], axis=0)
+    scales = back_rows([steady, steady, vert, vert, steady, square, square])
+    first, second = (profile * scale * keep for profile, scale in zip(profiles, scales))
+    spot = lax.broadcasted_iota(jnp.int32, second.shape, 0)
+    second = jnp.where(spot == TARGET % 8, target, second)
+    sloped = own * horiz
     return jnp.concatenate(
-        [own, own * horiz, own * vert, profile * scale * keep, target], axis=0
-    ).astype(BF16)
-
-
-def gram(design):
+        [own[:16], own[16:] + first, sloped[:16], sloped[16:] + second, own * vert], axis=0
+    )
+
+
+def gram(lines):
+    design = jnp.concatenate([line.astype(BF16) for line in lines], axis=1)
     return lax.dot_general(design, design, (((1,), (1,)), ((), ())), preferred_element_type=F32)
 
 
@@ -477,13 +509,13 @@
         late_ref[:, span] = values[:split]
         bases[:, span] = values[split:]
     horiz = aux_ref[2 * rows : 2 * rows + 1]
-    profile = jnp.concatenate(back_profile(horiz), axis=0)
+    profile = back_rows(back_profile(horiz))
     first_line = jnp.where(even_stripe(), HALF, 0)
     first_row = lax.axis_index("stripe") * rows
-    total = jnp.zeros((FIT_ROWS, FIT_ROWS), F32)
+    designs = []
     for spot in range(rows - HALF):
         line = first_line + spot
-        design = design_line(
+        designs.append(design_line(
             bases[spot * BASE_PAD : (spot + 1) * BASE_PAD],
             aux_ref[pl.ds(line, 1), :],
             aux_ref[pl.ds(rows + line, 1), :],
@@ -491,8 +523,8 @@
             profile,
             first_row + line,
             rows * stripes,
-        )
-        total = total + gram(design)
+        ))
+    total = gram(designs)
     total_ref[...] = jnp.concatenate(
         [total, jnp.zeros((FIT_ROWS, LANES - FIT_ROWS), F32)], axis=1
     )
@@ -511,8 +543,6 @@
         ext,
         highs,
         lows,
-        xhigh,
-        xlow,
         bases,
     ) = refs
     width = early_ref.shape[1]
@@ -524,88 +554,135 @@
     highs[...], lows[...] = split_two(lines)
     moves = [(0, 2 * step) for step in range(10)] + [(1, 8 * step) for step in range(3)]
     used = 16 * len(moves)
-    for ref in (xhigh, xlow):
-        ref[used:] = jnp.zeros((LATE - used, width), BF16)
     split = HALF * BASE_PAD
-    chunk = 2 * LANES
+    chunk = 4 * LANES
     for start in range(0, width, chunk):
         span = slice(start, start + chunk)
-        for pair in range(start // LANES, (start + chunk) // LANES):
-            stamp_shifts((highs, lows), (xhigh, xlow), odd_ref, pair, moves)
-        values = three_products(high_ref[...], low_ref[...], xhigh[:, span], xlow[:, span])
+        made = [
+            stamp_values((highs, lows), odd_ref, pair, moves)
+            for pair in range(start // LANES, (start + chunk) // LANES)
+        ]
+        spare = jnp.zeros((LATE - used, chunk), BF16)
+        xh, xl = (
+            jnp.concatenate([jnp.concatenate([one[side] for one in made], axis=1), spare], axis=0)
+            for side in range(2)
+        )
+        values = three_products(high_ref[...], low_ref[...], xh, xl)
         bases[:, span] = early_ref[:, span] + values[:split]
     horiz = aux_ref[2 * rows : 2 * rows + 1]
-    profile = jnp.concatenate(back_profile(horiz), axis=0)
+    profile = back_rows(back_profile(horiz))
     first_line = jnp.where(even_stripe(), 0, rows - HALF)
     first_row = lax.axis_index("stripe") * rows
-    stack = 3
-    total = jnp.zeros((stack * FIT_ROWS, stack * FIT_ROWS), F32)
-    for begin in range(0, HALF, stack):
-        designs = []
-        for spot in range(begin, begin + stack):
-            line = first_line + spot
-            designs.append(
-                design_line(
-                    bases[spot * BASE_PAD : (spot + 1) * BASE_PAD],
-                    aux_ref[pl.ds(line, 1), :],
-                    aux_ref[pl.ds(rows + line, 1), :],
-                    horiz,
-                    profile,
-                    first_row + line,
-                    rows * stripes,
-                )
+    designs = []
+    for spot in range(HALF):
+        line = first_line + spot
+        designs.append(
+            design_line(
+                bases[spot * BASE_PAD : (spot + 1) * BASE_PAD],
+                aux_ref[pl.ds(line, 1), :],
+                aux_ref[pl.ds(rows + line, 1), :],
+                horiz,
+                profile,
+                first_row + line,
+                rows * stripes,
             )
-        total = total + gram(jnp.concatenate(designs, axis=0))
-    own = total_ref[:, :FIT_ROWS]
-    for spot in range(stack):
-        where = slice(spot * FIT_ROWS, (spot + 1) * FIT_ROWS)
-        own = own + total[where, where]
-    out_ref[...] = jnp.concatenate([own, jnp.zeros((FIT_ROWS, LANES - FIT_ROWS), F32)], axis=1)
+        )
+    own = total_ref[:, :FIT_ROWS] + gram(designs)
+    out_ref[...] = packed_normal(own)
+
+
+def packed_normal(normal):
+    room = LANES - FIT_ROWS
+    last = normal[PACKED:]
+    spare = jnp.zeros((BASE_PAD, 2 * room - FIT_ROWS), F32)
+    return jnp.concatenate(
+        [
+            jnp.concatenate([normal[:BASE_PAD], last[:, :room]], axis=1),
+            jnp.concatenate([normal[BASE_PAD:PACKED], last[:, room:], spare], axis=1),
+        ],
+        axis=0,
+    )
+
+
+def unpacked_normal(packed):
+    room = LANES - FIT_ROWS
+    lane = lane_id(BASE_PAD)
+    last = jnp.where(
+        lane < room,
+        pltpu.roll(packed[:BASE_PAD], room, 1),
+        pltpu.roll(packed[BASE_PAD:], 2 * room, 1),
+    )
+    values = jnp.concatenate([packed, last], axis=0)
+    return jnp.where(lane_id(FIT_ROWS) < FIT_ROWS, values, 0.0)
 
 
 def panels():
     out = []
-    for term in range(3):
-        start = term * BASE_PAD
-        out += [(start, 8), (start + 8, 8), (start + 16, BASES - 16)]
-    return out + [(3 * BASE_PAD, BACK)]
+    for term, used in enumerate((BASE_PAD, BASES + BACK - BACK_FIRST, BASES)):
+        for start in range(0, used, 8):
+            out.append((term * BASE_PAD + start, min(8, used - start)))
+    return out
+
+
+def tree_sum(values):
+    while len(values) > 1:
+        values = [sum(values[spot : spot + 2][1:], values[spot]) for spot in range(0, len(values), 2)]
+    return values[0]
 
 
 def solve_rows(matrix):
     sub = row_id(8)
     tiles = [matrix[start : start + 8] for start in range(0, FIT_ROWS, 8)]
+    order = panels()
 
     def spread(tile, spot):
         return jnp.broadcast_to(tile[spot : spot + 1], (8, LANES))
 
-    for start, size in panels():
+    def column(tile, spot):
+        return jnp.broadcast_to(tile[:, spot : spot + 1], (8, LANES))
+
+    start, size = order[0]
+    corner = [column(tiles[start // 8], start + j) for j in range(size)]
+    for step, (start, size) in enumerate(order):
         home = start // 8
         columns = [
-            [jnp.broadcast_to(tile[:, start + j : start + j + 1], (8, LANES)) for tile in tiles]
+            [None if place == home else column(tile, start + j) for place, tile in enumerate(tiles)]
             for j in range(size)
         ]
-        corner = [column[home] for column in columns]
         rows = tiles[home]
+        following = order[step + 1] if step + 1 < len(order) else (0, 0)
+        next_home = following[0] // 8
+        ahead = [column(rows, following[0] + j) for j in range(following[1])]
+        below = [column(tiles[next_home], following[0] + j) for j in range(following[1])]
         for spot in range(size):
             keep = sub == spot
             inverse = 1.0 / spread(corner[spot], spot)
             others = jnp.where(keep, 0.0, corner[spot])
-            scaled = spread(rows, spot) * inverse
-            rows = jnp.where(keep, scaled, rows - others * scaled)
-            for j in range(spot + 1, size):
-                scaled = spread(corner[j], spot) * inverse
-                corner[j] = jnp.where(keep, scaled, corner[j] - others * scaled)
+
+            def eliminated(values):
+                scaled = spread(values, spot) * inverse
+                return jnp.where(keep, scaled, values - others * scaled)
+
+            corner = [
+                eliminated(values) if j > spot else values for j, values in enumerate(corner)
+            ]
+            ahead = [eliminated(values) for values in ahead]
+            rows = eliminated(rows)
+        if following[1]:
+            corner = [
+                values - tree_sum([columns[i][next_home] * spread(ahead[j], i) for i in range(size)])
+                for j, values in enumerate(below)
+            ]
         for place in range(len(tiles)):
             if place == home:
                 tiles[place] = rows
-                continue
-            change = columns[0][place] * spread(rows, 0)
-            for j in range(1, size):
-                change = change + columns[j][place] * spread(rows, j)
-            tiles[place] = tiles[place] - change
+            else:
+                tiles[place] = tiles[place] - tree_sum(
+                    [columns[i][place] * spread(rows, i) for i in range(size)]
+                )
     line = row_id(FIT_ROWS)
-    used = (line >= 3 * BASE_PAD) | (lax.rem(line, BASE_PAD) < BASES)
-    right = jnp.concatenate(tiles, axis=0)[:, FIT_ROWS - 1 : FIT_ROWS]
+    used = (line < TARGET) | ((line >= PACKED) & (line < PACKED + BASES))
+    right = jnp.concatenate(tiles, axis=0)[:, TARGET : TARGET + 1]
     return jnp.where(used, jnp.broadcast_to(right, (FIT_ROWS, LANES)), 0.0)
 
 
@@ -709,11 +786,10 @@
     rows = science_ref.shape[1]
     wide = science_ref.shape[2]
     top, bottom = edges_of(near_ref, far_ref)
-    coef = solve_rows(normal_ref[...])
+    coef = solve_rows(unpacked_normal(normal_ref[...]))
     lane = lane_id(FIT_ROWS)
-    home = jnp.where(
-        lane < 3 * BASES, lax.rem(lane, 3) * BASE_PAD + lane // 3, lane + 3 * (BASE_PAD - BASES)
-    )
+    home = lane - 3 * BASES + jnp.where(lane < 3 * BASES + BACK_FIRST, BASES, BASE_PAD + BASES - BACK_FIRST)
+    home = jnp.where(lane < 3 * BASES, lax.rem(lane, 3) * BASE_PAD + lane // 3, home)
     flat = jnp.sum(jnp.where(row_id(FIT_ROWS) == home, coef, 0.0), axis=0, keepdims=True)
     coef_ref[...] = flat[:, : coef_ref.shape[1]]
 
@@ -730,7 +806,9 @@
     halo_slopes = [
         coef[2 * BASE_PAD : 3 * BASE_PAD] * jnp.concatenate([line] * 3, axis=0) for line in halo_vert
     ]
-    level = [share(3 * BASE_PAD + m, 8) for m in range(BACK)]
+    level = [
+        share(BASES + m + (0 if m < BACK_FIRST else BASE_PAD - BACK_FIRST), 8) for m in range(BACK)
+    ]
 
     def ground(here, horiz):
         square = 0.5 * (3.0 * here * here - 1.0)
@@ -916,15 +994,13 @@
     )(*pieces, near, science, good, odd, high, low)
     normal = pl.pallas_call(
         functools.partial(late_kernel, stripes, rows),
-        out_shape=normal_shape,
+        out_shape=jax.ShapeDtypeStruct((PACKED, LANES), F32),
         in_specs=whole_vmem(7),
         out_specs=pl.BlockSpec(memory_space=pltpu.VMEM),
         scratch_shapes=[
             pltpu.VMEM((16, reach), F32),
             pltpu.VMEM((32, reach), BF16),
             pltpu.VMEM((32, reach), BF16),
-            pltpu.VMEM((LATE, width), BF16),
-            pltpu.VMEM((LATE, width), BF16),
             pltpu.VMEM((HALF * BASE_PAD, width), F32),
         ],
         compiler_params=params,

time: 31.2 us -> 30.1 us (0.965)
  Pallas kernels: 15.8 us -> 15.3 us
  waiting for transfers between devices: 2.63 us -> 2.14 us
    ppermute x3, waiting for transfers between devices: 1.02 us -> 0.53 us  [summed(): other = lax.ppermute(values, axis, [(i, i ^ step) for i in range(count)])]
  transfers between devices with their start and end apart: 6 -> 6, of which waited for: 4 -> 4; matrix products, arithmetic and copies ran while one was open for 0% -> 0% of each run, Pallas kernels for 32% -> 34%
where the time goes in v4:
time: 30.1 us; the launch traced here: 29.9 us
  Pallas kernels  15.3 us (51%)
  starting transfers between devices  11.8 us (39%)
  waiting for transfers between devices  2.14 us (7%)
  between operations  0.71 us (2%)
    ppermute x3, starting transfers between devices, summed(): other = lax.ppermute(values, axis, [(i, i ^ step) for i in range(count)])  7.71 us
    ppermute x2, starting transfers between devices, swapped(): lax.ppermute(values, 'stripe', couples + [(b, a) for a, b in couples])  3.57 us
    pallas_call x1, Pallas kernels, shards(): pl.pallas_call(functools.partial(model_kernel, stripes), out_shape=(jax.S...  3.31 us
    pallas_call x2, Pallas kernels, next_bases(): pl.pallas_call(functools.partial(next_bases_kernel, cuts[cut]), out_shape...  3.24 us
    pallas_call x1, Pallas kernels, shards(): pl.pallas_call(functools.partial(early_kernel, cores, stripes), out_shape...  3.24 us
    pallas_call x1, Pallas kernels, shards(): pl.pallas_call(functools.partial(late_kernel, stripes, rows), out_shape=j...  1.79 us
    pallas_call x1, Pallas kernels, first_bases(): pl.pallas_call(functools.partial(first_bases_kernel, cores), out_shape=(w...  1.68 us
    ppermute x2, waiting for transfers between devices, swapped(): lax.ppermute(values, 'stripe', couples + [(b, a) for a, b in couples])  1.57 us
  transfers between devices with their start and end apart: 6, of which 4 were waited for; matrix products, arithmetic and copies ran while one was open for 0% of the time, Pallas kernels for 34%

profile of v4, /device:TPU:0, one launch (start us, length us, event | category | flops | bytes accessed | tf_op | source)
XLA Modules:
  0.0 29.9 jit_solution(2745446646018956358)
XLA Ops:
  0.6 0.5 %collective-permute-start = (f32[16,1024]{1,0:T(8,128)}, f32[16,1024]{1,0:T(8,128)S(1)}, u32[]{:S(2)}, u32[]{:S(2)}) collective-permute-start(f32[16,1024]{1,0:T(8,128)} %template_hbm.1), channel_id=1, source_target_pairs={{1,0},{0,1},{3,2},{2,3},{5,4},{4,5},{7,6},{6,7},{9,8},{8,9},{11,10... | collective-permute-start | bytes 196616 | tf_op jit(solution)/shard_map/ppermute | solution.py:907
  1.1 1.1 %load.1 = (f32[16,1024]{1,0:T(8,128)S(1)}, f32[1,16,2048]{2,1,0:T(8,128)S(1)}, f32[1,16,2048]{2,1,0:T(8,128)S(1)}, f32[19,19]{1,0:T(8,128)S(1)}, f32[19,19]{1,0:T(8,128)S(1)}, /*index=5*/s32[16,128]{1,0:T(8,128)S(1)}) custom-call(f32[16,1024]{1,0:T(8,128)} %template_hbm.1, f32[1,16,2048]{2,1,0:T(8,128)} %science_hbm.1, s32[1,16,2048]{2,1,0:T(8,128)} %good_hbm.1, ...), custom_call_target="tpu_custom_call" | custom-call | tf_op jit(solution)/shard_map/load/pallas_call | solution.py:911
  2.2 0.0 collective-permute-done.refs_1_
  2.3 0.1 edges.3
  2.3 2.9 %collective-permute-start.2 = (f32[24,1024]{1,0:T(8,128)S(1)}, f32[24,1024]{1,0:T(8,128)S(1)}, u32[]{:S(2)}, u32[]{:S(2)}) collective-permute-start(f32[24,1024]{1,0:T(8,128)S(1)} %edges.3), channel_id=1, source_target_pairs={{0,2},{4,6},{8,10},{12,14},{2,0},{6,4},{10,8},{14,12},{1,3},{5,7},... | collective-permute-start | bytes 294920 | tf_op jit(solution)/shard_map/ppermute | solution.py:951
  5.2 0.1 edges.2
  5.3 0.7 %collective-permute-start.1 = (f32[24,1024]{1,0:T(8,128)S(1)}, f32[24,1024]{1,0:T(8,128)S(1)}, u32[]{:S(2)}, u32[]{:S(2)}) collective-permute-start(f32[24,1024]{1,0:T(8,128)S(1)} %edges.2), channel_id=1, source_target_pairs={{2,4},{6,8},{10,12},{4,2},{8,6},{12,10},{3,5},{7,9},{11,13},{5,3},... | collective-permute-start | bytes 294920 | tf_op jit(solution)/shard_map/ppermute | solution.py:951
  6.0 0.8 %weights.1 = (bf16[384,512]{1,0:T(8,128)(2,1)S(1)}, bf16[384,512]{1,0:T(8,128)(2,1)S(1)}, bf16[224,256]{1,0:T(8,128)(2,1)S(1)}, bf16[224,256]{1,0:T(8,128)(2,1)S(1)}, f32[24,896]{1,0:T(8,128)S(1)}) custom-call(f32[19,19]{1,0:T(8,128)S(1)} %get-tuple-element.25.row_ref, f32[19,19]{1,0:T(8,128)S(1)} %get-tuple-element.26.col_ref), custom_call_target="tpu_custom_call" | custom-call | tf_op jit(solution)/shard_map/weights/pallas_call | solution.py:957
  6.8 1.6 %collective-permute-done.2.refs_2_.refs_3_.refs_4_ = f32[24,1024]{1,0:T(8,128)S(1)} collective-permute-done((f32[24,1024]{1,0:T(8,128)S(1)}, f32[24,1024]{1,0:T(8,128)S(1)}, u32[]{:S(2)}, u32[]{:S(2)}) %collective-permute-start.2) | collective-permute-done | bytes 98336 | tf_op jit(solution)/shard_map/ppermute | solution.py:951
  8.4 3.2 %early.1 = (f32[72,128]{1,0:T(8,128)S(1)}, f32[216,1024]{1,0:T(8,128)S(1)}, f32[40,1024]{1,0:T(8,128)S(1)}) custom-call(f32[16,1024]{1,0:T(8,128)S(1)} %get-tuple-element.21.refs_0_, f32[16,1024]{1,0:T(8,128)S(1)} %collective-permute-done.refs_1_, f32[24,1024]{1,0:T(8,128)S(1)} %collective-permute-done.2.refs_2_.refs_3_.refs_4_, ...), custom_call_target="tpu_custom_call" | custom-call | tf_op jit(solution)/shard_map/early/pallas_call | solution.py:975
  11.6 0.0 collective-permute-done.1.refs_0_.refs_2_.refs_3_
  11.6 1.8 %late.1.refs_5_.mine_ref = f32[48,128]{1,0:T(8,128)S(1)} custom-call(f32[24,1024]{1,0:T(8,128)S(1)} %collective-permute-done.1.refs_0_.refs_2_.refs_3_, s32[16,128]{1,0:T(8,128)S(1)} %get-tuple-element.24.refs_5_.refs_1_, bf16[224,256]{1,0:T(8,128)(2,1)S(1)} %get-tuple-element.27.refs_2_, bf16[224,256]{1,0:T(8,128)(2,1)S(1)} %get-tuple-element.28.refs_3_, ...), custom_call_target="tpu_custom_call" | custom-call | tf_op jit(solution)/shard_map/late/pallas_call | solution.py:995
  13.4 2.8 %collective-permute-start.3 = (f32[48,128]{1,0:T(8,128)S(1)}, f32[48,128]{1,0:T(8,128)S(1)}, u32[]{:S(2)}, u32[]{:S(2)}) collective-permute-start(f32[48,128]{1,0:T(8,128)S(1)} %late.1.refs_5_.mine_ref), channel_id=1, source_target_pairs={{0,2},{2,0},{4,6},{6,4},{8,10},{10,8},{12,14},{14,12},{1,3},{3,1},... | collective-permute-start | bytes 73736 | tf_op jit(solution)/shard_map/ppermute | solution.py:888
  16.2 1.7 %bases.3 = (bf16[352,768]{1,0:T(8,128)(2,1)S(1)}, bf16[352,768]{1,0:T(8,128)(2,1)S(1)}, bf16[48,2304]{1,0:T(8,128)(2,1)S(1)}, bf16[48,2304]{1,0:T(8,128)(2,1)S(1)}, f32[352,512]{1,0:T(8,128)S(1)}) custom-call(f32[16,1024]{1,0:T(8,128)S(1)} %get-tuple-element.21.refs_0_, f32[16,1024]{1,0:T(8,128)S(1)} %collective-permute-done.refs_1_, ...), custom_call_target="tpu_custom_call" | custom-call | tf_op jit(solution)/shard_map/bases/pallas_call | solution.py:1021
  17.8 0.1 collective-permute-done.3.other_ref
  18.0 2.0 %collective-permute-start.4 = (f32[48,128]{1,0:T(8,128)S(1)}, f32[48,128]{1,0:T(8,128)S(1)}, u32[]{:S(2)}, u32[]{:S(2)}) collective-permute-start(f32[48,128]{1,0:T(8,128)S(1)} %add.3.after_ref.mine_ref), channel_id=1, source_target_pairs={{0,4},{2,6},{4,0},{6,2},{8,12},{10,14},{12,8},{14,10},{1,5},{3,7},... | collective-permute-start | bytes 73736 | tf_op jit(solution)/shard_map/ppermute | solution.py:888
  19.9 1.6 %bases.4.after_ref.refs_1_ = f32[352,768]{1,0:T(8,128)S(1)} custom-call(bf16[48,2304]{1,0:T(8,128)(2,1)S(1)} %get-tuple-element.36.highs, bf16[48,2304]{1,0:T(8,128)(2,1)S(1)} %get-tuple-element.37.lows, bf16[352,768]{1,0:T(8,128)(2,1)S(1)} %get-tuple-element.38.high_ref, bf16[352,768]{1,0:T(8,128)(2,1)S(1)} %get-tuple-element.39.low_ref, ...), custom_call_target="tpu_custom_call" | custom-call | tf_op jit(solution)/shard_map/bases/pallas_call | solution.py:1043
  21.6 0.2 collective-permute-done.4.other_ref
  21.8 3.0 %collective-permute-start.5 = (f32[48,128]{1,0:T(8,128)S(1)}, f32[48,128]{1,0:T(8,128)S(1)}, u32[]{:S(2)}, u32[]{:S(2)}) collective-permute-start(f32[48,128]{1,0:T(8,128)S(1)} %add.4.after_ref.mine_ref), channel_id=1, source_target_pairs={{0,8},{2,10},{4,12},{6,14},{8,0},{10,2},{12,4},{14,6},{1,9},{3,11}... | collective-permute-start | bytes 73736 | tf_op jit(solution)/shard_map/ppermute | solution.py:888
  24.8 1.6 %bases.5.after_ref.refs_2_ = f32[352,768]{1,0:T(8,128)S(1)} custom-call(bf16[48,2304]{1,0:T(8,128)(2,1)S(1)} %get-tuple-element.36.highs, bf16[48,2304]{1,0:T(8,128)(2,1)S(1)} %get-tuple-element.37.lows, bf16[352,768]{1,0:T(8,128)(2,1)S(1)} %get-tuple-element.38.high_ref, bf16[352,768]{1,0:T(8,128)(2,1)S(1)} %get-tuple-element.39.low_ref, ...), custom_call_target="tpu_custom_call" | custom-call | tf_op jit(solution)/shard_map/bases/pallas_call | solution.py:1043
  26.4 0.2 collective-permute-done.5.other_ref
  26.6 3.3 %model.1 = (f32[1,16,2048]{2,1,0:T(8,128)}, f32[1,64]{1,0:T(1,128)}) custom-call(f32[48,128]{1,0:T(8,128)S(1)} %add.5.normal_ref, f32[352,512]{1,0:T(8,128)S(1)} %get-tuple-element.35.after_ref.refs_0_, f32[352,768]{1,0:T(8,128)S(1)} %bases.4.after_ref.refs_1_, f32[352,768]{1,0:T(8,128)S(1)} %bases.5.after_ref.refs_2_, ...), custom_call_target="tpu_custom_call" | custom-call | tf_op jit(solution)/shard_map/model/pallas_call | solution.py:1057
  (3 shorter events, 0.0 us)
Async XLA Ops:
  0.6 1.6 %collective-permute-start = (f32[16,1024]{1,0:T(8,128)}, f32[16,1024]{1,0:T(8,128)S(1)}, u32[]{:S(2)}, u32[]{:S(2)}) collective-permute-start(f32[16,1024]{1,0:T(8,128)} %template_hbm.1), channel_id=1, source_target_pairs={{1,0},{0,1},{3,2},{2,3},{5,4},{4,5},{7,6},{6,7},{9,8},{8,9},{11,10... | collective-permute-start | bytes 196616 | tf_op jit(solution)/shard_map/ppermute | solution.py:907
  2.3 6.0 %collective-permute-start.2 = (f32[24,1024]{1,0:T(8,128)S(1)}, f32[24,1024]{1,0:T(8,128)S(1)}, u32[]{:S(2)}, u32[]{:S(2)}) collective-permute-start(f32[24,1024]{1,0:T(8,128)S(1)} %edges.3), channel_id=1, source_target_pairs={{0,2},{4,6},{8,10},{12,14},{2,0},{6,4},{10,8},{14,12},{1,3},{5,7},... | collective-permute-start | bytes 294920 | tf_op jit(solution)/shard_map/ppermute | solution.py:951
  5.3 6.3 %collective-permute-start.1 = (f32[24,1024]{1,0:T(8,128)S(1)}, f32[24,1024]{1,0:T(8,128)S(1)}, u32[]{:S(2)}, u32[]{:S(2)}) collective-permute-start(f32[24,1024]{1,0:T(8,128)S(1)} %edges.2), channel_id=1, source_target_pairs={{2,4},{6,8},{10,12},{4,2},{8,6},{12,10},{3,5},{7,9},{11,13},{5,3},... | collective-permute-start | bytes 294920 | tf_op jit(solution)/shard_map/ppermute | solution.py:951
  13.4 4.6 %collective-permute-start.3 = (f32[48,128]{1,0:T(8,128)S(1)}, f32[48,128]{1,0:T(8,128)S(1)}, u32[]{:S(2)}, u32[]{:S(2)}) collective-permute-start(f32[48,128]{1,0:T(8,128)S(1)} %late.1.refs_5_.mine_ref), channel_id=1, source_target_pairs={{0,2},{2,0},{4,6},{6,4},{8,10},{10,8},{12,14},{14,12},{1,3},{3,1},... | collective-permute-start | bytes 73736 | tf_op jit(solution)/shard_map/ppermute | solution.py:888
  18.0 3.8 %collective-permute-start.4 = (f32[48,128]{1,0:T(8,128)S(1)}, f32[48,128]{1,0:T(8,128)S(1)}, u32[]{:S(2)}, u32[]{:S(2)}) collective-permute-start(f32[48,128]{1,0:T(8,128)S(1)} %add.3.after_ref.mine_ref), channel_id=1, source_target_pairs={{0,4},{2,6},{4,0},{6,2},{8,12},{10,14},{12,8},{14,10},{1,5},{3,7},... | collective-permute-start | bytes 73736 | tf_op jit(solution)/shard_map/ppermute | solution.py:888
  21.8 4.8 %collective-permute-start.5 = (f32[48,128]{1,0:T(8,128)S(1)}, f32[48,128]{1,0:T(8,128)S(1)}, u32[]{:S(2)}, u32[]{:S(2)}) collective-permute-start(f32[48,128]{1,0:T(8,128)S(1)} %add.4.after_ref.mine_ref), channel_id=1, source_target_pairs={{0,8},{2,10},{4,12},{6,14},{8,0},{10,2},{12,4},{14,6},{1,9},{3,11}... | collective-permute-start | bytes 73736 | tf_op jit(solution)/shard_map/ppermute | solution.py:888

commit v5 on v4

--- a/solution.py
+++ b/solution.py
@@ -47,6 +47,12 @@
     high = values.astype(BF16)
     low = (values - high.astype(F32)).astype(BF16)
     return high, low
+
+
+def put_split(target, start, values):
+    size = values.shape[0]
+    gap = target.shape[0] // 2
+    target[start : start + size], target[gap + start : gap + start + size] = split_two(values)
 
 
 def position(index, total):
@@ -131,7 +137,7 @@
 
 
 def weight_kernel(
-    row_ref, col_ref, high_ref, low_ref, late_high_ref, late_low_ref, base_ref, pad
+    row_ref, col_ref, weight_ref, late_ref, base_ref, pad
 ):
     pad[...] = jnp.zeros_like(pad)
     pad[0, 0:BASES, 0:TAPS] = row_ref[...]
@@ -174,7 +180,7 @@
         base_ref[:, tile * LANES : (tile + 1) * LANES] = mains[tile]
     base_ref[:, MAIN : MAIN + LANES] = outer
     base_ref[:, MAIN + LANES :] = inner
-    rows = high_ref.shape[0] // BASE_PAD
+    rows = weight_ref.shape[0] // (2 * BASE_PAD)
     even = even_stripe()
     first_tap, last_tap = tap_at(0), tap_at(TAPS - 1)
 
@@ -266,13 +272,10 @@
                 jnp.concatenate([mine * tile for mine, tile in zip(tiles, late_tiles)], axis=1)
             )
     for spot in range(0, rows, 2):
-        where = pl.ds(spot * BASE_PAD, 2 * BASE_PAD)
-        high_ref[where, :], low_ref[where, :] = split_two(
-            jnp.concatenate(early_rows[spot : spot + 2], axis=0)
-        )
-    spare = late_high_ref.shape[0] - HALF * BASE_PAD
+        put_split(weight_ref, spot * BASE_PAD, jnp.concatenate(early_rows[spot : spot + 2], axis=0))
+    spare = late_ref.shape[0] // 2 - HALF * BASE_PAD
     late_rows.append(jnp.zeros((spare, LATE), F32))
-    late_high_ref[...], late_low_ref[...] = split_two(jnp.concatenate(late_rows, axis=0))
+    put_split(late_ref, 0, jnp.concatenate(late_rows, axis=0))
 
 
 def edges_of(near_ref, far_ref):
@@ -405,11 +408,11 @@
     return out
 
 
-def three_products(high, low, xhigh, xlow):
-    return (
-        jnp.dot(high, xhigh, preferred_element_type=F32)
-        + jnp.dot(low, xhigh, preferred_element_type=F32)
-        + jnp.dot(high, xlow, preferred_element_type=F32)
+def three_products(weights, xhigh, xlow):
+    rows = weights.shape[0] // 2
+    both = jnp.dot(weights, xhigh, preferred_element_type=F32)
+    return both[:rows] + (
+        both[rows:] + jnp.dot(weights[:rows], xlow, preferred_element_type=F32)
     )
 
 
@@ -448,8 +451,7 @@
         science_ref,
         good_ref,
         odd_ref,
-        high_ref,
-        low_ref,
+        weight_ref,
         total_ref,
         late_ref,
         aux_ref,
@@ -505,7 +507,7 @@
     chunk = 2 * LANES
     for start in range(0, wide // 2, chunk):
         span = slice(start, start + chunk)
-        values = three_products(high_ref[...], low_ref[...], xhigh[:, span], xlow[:, span])
+        values = three_products(weight_ref[...], xhigh[:, span], xlow[:, span])
         late_ref[:, span] = values[:split]
         bases[:, span] = values[split:]
     horiz = aux_ref[2 * rows : 2 * rows + 1]
@@ -534,8 +536,7 @@
     (
         far_ref,
         odd_ref,
-        high_ref,
-        low_ref,
+        weight_ref,
         total_ref,
         early_ref,
         aux_ref,
@@ -567,7 +568,7 @@
             jnp.concatenate([jnp.concatenate([one[side] for one in made], axis=1), spare], axis=0)
             for side in range(2)
         )
-        values = three_products(high_ref[...], low_ref[...], xh, xl)
+        values = three_products(weight_ref[...], xh, xl)
         bases[:, span] = early_ref[:, span] + values[:split]
     horiz = aux_ref[2 * rows : 2 * rows + 1]
     profile = back_rows(back_profile(horiz))
@@ -686,7 +687,7 @@
     return jnp.where(used, jnp.broadcast_to(right, (FIT_ROWS, LANES)), 0.0)
 
 
-def region_weights(base_ref, high_ref, low_ref, rows):
+def region_weights(base_ref, weight_ref, rows):
     lane = lane_id(8)
     spot = lax.rem(lane, GROUP)
     corner = lax.rem(lane, 4)
@@ -715,8 +716,7 @@
                 extra = jnp.where((line == 7) & (corner >= 2), mine, extra)
             blocks[b].append(jnp.concatenate(tiles + [extra], axis=1))
     for b in range(BASES):
-        where = pl.ds(b * rows, rows)
-        high_ref[where, :], low_ref[where, :] = split_two(jnp.concatenate(blocks[b], axis=0))
+        put_split(weight_ref, b * rows, jnp.concatenate(blocks[b], axis=0))
     lane = lane_id(BASE_PAD)
     spot = lax.rem(lane, GROUP)
     corner = lax.rem(lane, 4)
@@ -726,11 +726,10 @@
         inside = (tap >= 0) & (tap < TAPS)
         tiles = [jnp.where(inside, pltpu.roll(main, shift % LANES, 1), 0.0) for main in mains]
         halos.append(jnp.concatenate(tiles + [jnp.where(extra, outer, 0.0)], axis=1))
-    where = pl.ds(BASES * rows, 2 * BASE_PAD)
-    high_ref[where, :], low_ref[where, :] = split_two(jnp.concatenate(halos, axis=0))
-
-
-def region_bases(highs, lows, high_ref, low_ref, first, out_ref, xhigh, xlow):
+    put_split(weight_ref, BASES * rows, jnp.concatenate(halos, axis=0))
+
+
+def region_bases(highs, lows, weight_ref, first, out_ref, xhigh, xlow):
     clear_spare((xhigh, xlow))
     wide = out_ref.shape[1]
     chunk = 2 * LANES
@@ -746,9 +745,7 @@
                 target[place : place + values.shape[0], span] = values
 
             spread_window(shifted, put)
-        out_ref[:, span] = three_products(
-            high_ref[...], low_ref[...], xhigh[:, span], xlow[:, span]
-        )
+        out_ref[:, span] = three_products(weight_ref[...], xhigh[:, span], xlow[:, span])
 
 
 def first_bases_kernel(cores, *refs):
@@ -758,8 +755,7 @@
         near_ref,
         base_ref,
         after_ref,
-        high_ref,
-        low_ref,
+        weight_ref,
         highs,
         lows,
         out_ref,
@@ -767,17 +763,21 @@
         xhigh,
         xlow,
     ) = refs[cores:]
-    region_weights(base_ref, high_ref, low_ref, pieces[0].shape[0])
+    region_weights(base_ref, weight_ref, pieces[0].shape[0])
     fill_extended(ext, highs, lows, cores, pieces, near_ref, far_ref)
-    region_bases(highs, lows, high_ref, low_ref, 0, out_ref, xhigh, xlow)
-
-
-def next_bases_kernel(first, highs, lows, high_ref, low_ref, after_ref, out_ref, xhigh, xlow):
-    region_bases(highs, lows, high_ref, low_ref, first, out_ref, xhigh, xlow)
-
-
-def add_kernel(mine_ref, other_ref, after_ref, out_ref):
-    out_ref[...] = mine_ref[...] + other_ref[...]
+    region_bases(highs, lows, weight_ref, 0, out_ref, xhigh, xlow)
+
+
+def next_bases_kernel(first, highs, lows, weight_ref, after_ref, out_ref, xhigh, xlow):
+    region_bases(highs, lows, weight_ref, first, out_ref, xhigh, xlow)
+
+
+def add_kernel(count, *refs):
+    values = [ref[...] for ref in refs[:count]]
+    if count == 4:
+        order = (1, 2, 0)
+        values = [values[0]] + [values[1 + order.index(k)] for k in range(3)]
+    refs[-1][...] = tree_sum(values)
 
 
 def model_kernel(stripes, normal_ref, *refs):
@@ -865,34 +865,39 @@
     return [pl.BlockSpec(memory_space=pltpu.VMEM)] * count
 
 
-def add(values, other, after, params):
+def add(values, after, params):
     return pl.pallas_call(
-        add_kernel,
-        out_shape=jax.ShapeDtypeStruct(values.shape, values.dtype),
-        in_specs=whole_vmem(3),
+        functools.partial(add_kernel, len(values)),
+        out_shape=jax.ShapeDtypeStruct(values[0].shape, values[0].dtype),
+        in_specs=whole_vmem(len(values) + len(after)),
         out_specs=pl.BlockSpec(memory_space=pltpu.VMEM),
         compiler_params=params,
         name="add",
-    )(values, other, after)
+    )(*values, *after)
 
 
 def summed(values, axis, beside, params):
     count = lax.axis_size(axis)
     if count & (count - 1):
-        for work in beside:
-            work(values)
+        for works in beside:
+            for work in works:
+                work(values)
         return lax.psum(values, axis)
-    step = 1
-    waiting = list(beside)
+    rounds = [(1, 2, 3)] if count >= 4 else []
+    step = 4 if rounds else 1
     while step < count:
-        other = lax.ppermute(values, axis, [(i, i ^ step) for i in range(count)])
-        if waiting:
-            values = add(values, other, waiting.pop(0)(values), params)
-        else:
-            values = values + other
+        rounds.append((step,))
         step *= 2
-    for work in waiting:
-        work(values)
+    rounds += [()] * (len(beside) - len(rounds))
+    for spot, steps in enumerate(rounds):
+        others = [
+            lax.ppermute(values, axis, [(i, i ^ step) for i in range(count)]) for step in steps
+        ]
+        after = [work(values) for work in beside[spot]] if spot < len(beside) else []
+        if steps:
+            if len(others) == 3:
+                others = [others[k] for k in (1, 2, 0)]
+            values = add([values] + others, after, params)
     return values
 
 
@@ -952,19 +957,17 @@
 
     far = swapped(far, far_pairs)
     near = swapped(near, near_pairs)
-    early_shape = jax.ShapeDtypeStruct((rows * BASE_PAD, EARLY), BF16)
-    late_shape = jax.ShapeDtypeStruct((LATE_ROWS, LATE), BF16)
-    high, low, late_high, late_low, base = pl.pallas_call(
+    early_shape = jax.ShapeDtypeStruct((2 * rows * BASE_PAD, EARLY), BF16)
+    late_shape = jax.ShapeDtypeStruct((2 * LATE_ROWS, LATE), BF16)
+    early_weights, late_weights, base = pl.pallas_call(
         weight_kernel,
         out_shape=(
             early_shape,
-            early_shape,
-            late_shape,
             late_shape,
             jax.ShapeDtypeStruct((BASE_PAD, DEPTH + LANES), F32),
         ),
         in_specs=whole_vmem(2),
-        out_specs=tuple(whole_vmem(5)),
+        out_specs=tuple(whole_vmem(3)),
         scratch_shapes=[pltpu.VMEM((2, BASE_PAD, LANES), F32)],
         compiler_params=params,
         name="weights",
@@ -979,7 +982,7 @@
             jax.ShapeDtypeStruct((HALF * BASE_PAD, width), F32),
             jax.ShapeDtypeStruct((2 * rows + 8, width), F32),
         ),
-        in_specs=whole_vmem(cores + 6),
+        in_specs=whole_vmem(cores + 5),
         out_specs=tuple(whole_vmem(3)),
         scratch_shapes=[
             pltpu.VMEM((rows + 16, reach), F32),
@@ -991,11 +994,11 @@
         ],
         compiler_params=params,
         name="early",
-    )(*pieces, near, science, good, odd, high, low)
+    )(*pieces, near, science, good, odd, early_weights)
     normal = pl.pallas_call(
         functools.partial(late_kernel, stripes, rows),
         out_shape=jax.ShapeDtypeStruct((PACKED, LANES), F32),
-        in_specs=whole_vmem(7),
+        in_specs=whole_vmem(6),
         out_specs=pl.BlockSpec(memory_space=pltpu.VMEM),
         scratch_shapes=[
             pltpu.VMEM((16, reach), F32),
@@ -1005,11 +1008,11 @@
         ],
         compiler_params=params,
         name="late",
-    )(far, odd, late_high, late_low, part, kept, aux)
+    )(far, odd, late_weights, part, kept, aux)
     region_rows = BASES * rows + 2 * BASE_PAD
     blocks = wide // (2 * LANES)
     cuts = [blocks * cut // 8 * 2 * LANES for cut in (0, 2, 5, 8)]
-    weight_shape = jax.ShapeDtypeStruct((region_rows, DEPTH), BF16)
+    weight_shape = jax.ShapeDtypeStruct((2 * region_rows, DEPTH), BF16)
     source_shape = jax.ShapeDtypeStruct((GROUP + 16, reach), BF16)
     parts, shared = [], []
 
@@ -1022,13 +1025,12 @@
             functools.partial(first_bases_kernel, cores),
             out_shape=(
                 weight_shape,
-                weight_shape,
                 source_shape,
                 source_shape,
                 jax.ShapeDtypeStruct((region_rows, size), F32),
             ),
             in_specs=whole_vmem(cores + 4),
-            out_specs=tuple(whole_vmem(5)),
+            out_specs=tuple(whole_vmem(4)),
             scratch_shapes=[pltpu.VMEM((rows + 24, reach), F32)] + shift_scratch(size),
             compiler_params=params,
             name="bases",
@@ -1039,20 +1041,20 @@
 
     def next_bases(cut, after):
         size = cuts[cut + 1] - cuts[cut]
-        high, low, highs, lows = shared
+        region_weight, highs, lows = shared
         part = pl.pallas_call(
             functools.partial(next_bases_kernel, cuts[cut]),
             out_shape=jax.ShapeDtypeStruct((region_rows, size), F32),
-            in_specs=whole_vmem(5),
+            in_specs=whole_vmem(4),
             out_specs=pl.BlockSpec(memory_space=pltpu.VMEM),
             scratch_shapes=shift_scratch(size),
             compiler_params=params,
             name="bases",
-        )(highs, lows, high, low, after)
+        )(highs, lows, region_weight, after)
         parts.append(part)
         return part
 
-    beside = [first_bases, functools.partial(next_bases, 1), functools.partial(next_bases, 2)]
+    beside = [[first_bases, functools.partial(next_bases, 1)], [functools.partial(next_bases, 2)]]
     normal = summed(normal, "stripe", beside, params)
     filtered, coef = pl.pallas_call(
         functools.partial(model_kernel, stripes),

time: 30.1 us -> 29.7 us (0.987)
  starting transfers between devices: 11.8 us -> 11.1 us
    ppermute x3 -> x4, starting transfers between devices: 7.71 us -> 6.99 us  [summed(): lax.ppermute(values, axis, [(i, i ^ step) for i in range(count)])]
    ppermute x3 -> x4, waiting for transfers between devices: 0.53 us -> 0.78 us  [summed(): lax.ppermute(values, axis, [(i, i ^ step) for i in range(count)])]
    pallas_call x4 -> x3, Pallas kernels: 0.81 us -> 0.81 us  [the longest x1 0.8 us: shards(): pl.pallas_call(weight_kernel, out_shape=(early_shape, late_shape, jax.Sha...]
  transfers between devices with their start and end apart: 6 -> 7, of which waited for: 4 -> 3; matrix products, arithmetic and copies ran while one was open for 0% -> 0% of each run, Pallas kernels for 34% -> 34%
where the time goes in v5:
time: 29.7 us; the launch traced here: 29.5 us
  Pallas kernels  15.3 us (52%)
  starting transfers between devices  11.1 us (37%)
  waiting for transfers between devices  2.39 us (8%)
  between operations  0.73 us (2%)
    ppermute x4, starting transfers between devices, summed(): lax.ppermute(values, axis, [(i, i ^ step) for i in range(count)])  6.99 us
    ppermute x2, starting transfers between devices, swapped(): lax.ppermute(values, 'stripe', couples + [(b, a) for a, b in couples])  3.57 us
    pallas_call x1, Pallas kernels, shards(): pl.pallas_call(functools.partial(early_kernel, cores, stripes), out_shape...  3.36 us
    pallas_call x1, Pallas kernels, shards(): pl.pallas_call(functools.partial(model_kernel, stripes), out_shape=(jax.S...  3.31 us
    pallas_call x2, Pallas kernels, next_bases(): pl.pallas_call(functools.partial(next_bases_kernel, cuts[cut]), out_shape...  3.19 us
    pallas_call x1, Pallas kernels, shards(): pl.pallas_call(functools.partial(late_kernel, stripes, rows), out_shape=j...  1.78 us
    pallas_call x1, Pallas kernels, first_bases(): pl.pallas_call(functools.partial(first_bases_kernel, cores), out_shape=(w...  1.67 us
    ppermute x2, waiting for transfers between devices, swapped(): lax.ppermute(values, 'stripe', couples + [(b, a) for a, b in couples])  1.57 us
  transfers between devices with their start and end apart: 7, of which 3 were waited for; matrix products, arithmetic and copies ran while one was open for 0% of the time, Pallas kernels for 34%

profile of v5, /device:TPU:0, one launch (start us, length us, event | category | flops | bytes accessed | tf_op | source)
XLA Modules:
  0.0 29.5 jit_solution(11120604388437068588)
XLA Ops:
  0.6 0.5 %collective-permute-start = (f32[16,1024]{1,0:T(8,128)}, f32[16,1024]{1,0:T(8,128)S(1)}, u32[]{:S(2)}, u32[]{:S(2)}) collective-permute-start(f32[16,1024]{1,0:T(8,128)} %template_hbm.1), channel_id=1, source_target_pairs={{1,0},{0,1},{3,2},{2,3},{5,4},{4,5},{7,6},{6,7},{9,8},{8,9},{11,10... | collective-permute-start | bytes 196616 | tf_op jit(solution)/shard_map/ppermute | solution.py:912
  1.1 1.1 %load.1 = (f32[16,1024]{1,0:T(8,128)S(1)}, f32[1,16,2048]{2,1,0:T(8,128)S(1)}, f32[1,16,2048]{2,1,0:T(8,128)S(1)}, f32[19,19]{1,0:T(8,128)S(1)}, f32[19,19]{1,0:T(8,128)S(1)}, /*index=5*/s32[16,128]{1,0:T(8,128)S(1)}) custom-call(f32[16,1024]{1,0:T(8,128)} %template_hbm.1, f32[1,16,2048]{2,1,0:T(8,128)} %science_hbm.1, s32[1,16,2048]{2,1,0:T(8,128)} %good_hbm.1, ...), custom_call_target="tpu_custom_call" | custom-call | tf_op jit(solution)/shard_map/load/pallas_call | solution.py:916
  2.2 0.0 collective-permute-done.refs_1_
  2.3 0.1 edges.3
  2.3 2.9 %collective-permute-start.2 = (f32[24,1024]{1,0:T(8,128)S(1)}, f32[24,1024]{1,0:T(8,128)S(1)}, u32[]{:S(2)}, u32[]{:S(2)}) collective-permute-start(f32[24,1024]{1,0:T(8,128)S(1)} %edges.3), channel_id=1, source_target_pairs={{0,2},{4,6},{8,10},{12,14},{2,0},{6,4},{10,8},{14,12},{1,3},{5,7},... | collective-permute-start | bytes 294920 | tf_op jit(solution)/shard_map/ppermute | solution.py:956
  5.2 0.1 edges.2
  5.3 0.7 %collective-permute-start.1 = (f32[24,1024]{1,0:T(8,128)S(1)}, f32[24,1024]{1,0:T(8,128)S(1)}, u32[]{:S(2)}, u32[]{:S(2)}) collective-permute-start(f32[24,1024]{1,0:T(8,128)S(1)} %edges.2), channel_id=1, source_target_pairs={{2,4},{6,8},{10,12},{4,2},{8,6},{12,10},{3,5},{7,9},{11,13},{5,3},... | collective-permute-start | bytes 294920 | tf_op jit(solution)/shard_map/ppermute | solution.py:956
  6.0 0.8 %weights.1 = (bf16[768,512]{1,0:T(8,128)(2,1)S(1)}, bf16[448,256]{1,0:T(8,128)(2,1)S(1)}, f32[24,896]{1,0:T(8,128)S(1)}) custom-call(f32[19,19]{1,0:T(8,128)S(1)} %get-tuple-element.22.row_ref, f32[19,19]{1,0:T(8,128)S(1)} %get-tuple-element.23.col_ref), custom_call_target="tpu_custom_call" | custom-call | tf_op jit(solution)/shard_map/weights/pallas_call | solution.py:962
  6.8 1.6 %collective-permute-done.2.refs_2_.refs_3_.refs_4_ = f32[24,1024]{1,0:T(8,128)S(1)} collective-permute-done((f32[24,1024]{1,0:T(8,128)S(1)}, f32[24,1024]{1,0:T(8,128)S(1)}, u32[]{:S(2)}, u32[]{:S(2)}) %collective-permute-start.2) | collective-permute-done | bytes 98336 | tf_op jit(solution)/shard_map/ppermute | solution.py:956
  8.4 3.4 %early.1 = (f32[72,128]{1,0:T(8,128)S(1)}, f32[216,1024]{1,0:T(8,128)S(1)}, f32[40,1024]{1,0:T(8,128)S(1)}) custom-call(f32[16,1024]{1,0:T(8,128)S(1)} %get-tuple-element.18.refs_0_, f32[16,1024]{1,0:T(8,128)S(1)} %collective-permute-done.refs_1_, f32[24,1024]{1,0:T(8,128)S(1)} %collective-permute-done.2.refs_2_.refs_3_.refs_4_, ...), custom_call_target="tpu_custom_call" | custom-call | tf_op jit(solution)/shard_map/early/pallas_call | solution.py:978
  11.7 0.0 collective-permute-done.1.refs_0_.refs_2_.refs_3_
  11.7 1.8 %late.1.refs_5_.after_ref.refs_0_ = f32[48,128]{1,0:T(8,128)S(1)} custom-call(f32[24,1024]{1,0:T(8,128)S(1)} %collective-permute-done.1.refs_0_.refs_2_.refs_3_, s32[16,128]{1,0:T(8,128)S(1)} %get-tuple-element.21.refs_5_.refs_1_, bf16[448,256]{1,0:T(8,128)(2,1)S(1)} %get-tuple-element.24.refs_2_, f32[72,128]{1,0:T(8,128)S(1)} %get-tuple-element.26.refs_3_, ...), custom_call_target="tpu_custom_call" | custom-call | tf_op jit(solution)/shard_map/late/pallas_call | solution.py:998
  13.5 2.8 %collective-permute-start.5 = (f32[48,128]{1,0:T(8,128)S(1)}, f32[48,128]{1,0:T(8,128)S(1)}, u32[]{:S(2)}, u32[]{:S(2)}) collective-permute-start(f32[48,128]{1,0:T(8,128)S(1)} %late.1.refs_5_.after_ref.refs_0_), channel_id=1, source_target_pairs={{0,2},{2,0},{4,6},{6,4},{8,10},{10,8},{12,14},{14,12},{1,3},{3,1},... | collective-permute-start | bytes 73736 | tf_op jit(solution)/shard_map/ppermute | solution.py:894
  16.3 1.3 %collective-permute-start.4 = (f32[48,128]{1,0:T(8,128)S(1)}, f32[48,128]{1,0:T(8,128)S(1)}, u32[]{:S(2)}, u32[]{:S(2)}) collective-permute-start(f32[48,128]{1,0:T(8,128)S(1)} %late.1.refs_5_.after_ref.refs_0_), channel_id=1, source_target_pairs={{0,6},{2,4},{4,2},{6,0},{8,14},{10,12},{12,10},{14,8},{1,7},{3,5},... | collective-permute-start | bytes 73736 | tf_op jit(solution)/shard_map/ppermute | solution.py:894
  17.6 0.3 collective-permute-start.3
  17.8 1.7 %bases.3 = (bf16[704,768]{1,0:T(8,128)(2,1)S(1)}, bf16[48,2304]{1,0:T(8,128)(2,1)S(1)}, bf16[48,2304]{1,0:T(8,128)(2,1)S(1)}, f32[352,512]{1,0:T(8,128)S(1)}) custom-call(f32[16,1024]{1,0:T(8,128)S(1)} %get-tuple-element.18.refs_0_, f32[16,1024]{1,0:T(8,128)S(1)} %collective-permute-done.refs_1_, ...), custom_call_target="tpu_custom_call" | custom-call | tf_op jit(solution)/shard_map/bases/pallas_call | solution.py:1024
  19.5 1.6 %bases.4.refs_5_.refs_1_ = f32[352,768]{1,0:T(8,128)S(1)} custom-call(bf16[48,2304]{1,0:T(8,128)(2,1)S(1)} %get-tuple-element.31.highs, bf16[48,2304]{1,0:T(8,128)(2,1)S(1)} %get-tuple-element.32.lows, bf16[704,768]{1,0:T(8,128)(2,1)S(1)} %get-tuple-element.33.weight_ref, f32[48,128]{1,0:T(8,128)S(1)} %late.1.refs_5_.after_ref.refs_0_), custom_call_target="tpu_custom_call" | custom-call | tf_op jit(solution)/shard_map/bases/pallas_call | solution.py:1045
  21.1 0.0 collective-permute-done.5.refs_3_
  21.1 0.0 collective-permute-done.4.refs_2_
  21.1 0.2 collective-permute-done.3.refs_1_
  21.4 2.7 %collective-permute-start.6 = (f32[48,128]{1,0:T(8,128)S(1)}, f32[48,128]{1,0:T(8,128)S(1)}, u32[]{:S(2)}, u32[]{:S(2)}) collective-permute-start(f32[48,128]{1,0:T(8,128)S(1)} %add.2.after_ref.refs_0_), channel_id=1, source_target_pairs={{0,8},{2,10},{4,12},{6,14},{8,0},{10,2},{12,4},{14,6},{1,9},{3,11}... | collective-permute-start | bytes 73736 | tf_op jit(solution)/shard_map/ppermute | solution.py:894
  24.1 1.6 %bases.5.refs_2_ = f32[352,768]{1,0:T(8,128)S(1)} custom-call(bf16[48,2304]{1,0:T(8,128)(2,1)S(1)} %get-tuple-element.31.highs, bf16[48,2304]{1,0:T(8,128)(2,1)S(1)} %get-tuple-element.32.lows, bf16[704,768]{1,0:T(8,128)(2,1)S(1)} %get-tuple-element.33.weight_ref, f32[48,128]{1,0:T(8,128)S(1)} %add.2.after_ref.refs_0_), custom_call_target="tpu_custom_call" | custom-call | tf_op jit(solution)/shard_map/bases/pallas_call | solution.py:1045
  25.7 0.5 %collective-permute-done.6.refs_1_ = f32[48,128]{1,0:T(8,128)S(1)} collective-permute-done((f32[48,128]{1,0:T(8,128)S(1)}, f32[48,128]{1,0:T(8,128)S(1)}, u32[]{:S(2)}, u32[]{:S(2)}) %collective-permute-start.6) | collective-permute-done | bytes 24608 | tf_op jit(solution)/shard_map/ppermute | solution.py:894
  26.2 3.3 %model.1 = (f32[1,16,2048]{2,1,0:T(8,128)}, f32[1,64]{1,0:T(1,128)}) custom-call(f32[48,128]{1,0:T(8,128)S(1)} %add.3.normal_ref, f32[352,512]{1,0:T(8,128)S(1)} %get-tuple-element.30.refs_4_.refs_0_, f32[352,768]{1,0:T(8,128)S(1)} %bases.4.refs_5_.refs_1_, f32[352,768]{1,0:T(8,128)S(1)} %bases.5.refs_2_, ...), custom_call_target="tpu_custom_call" | custom-call | tf_op jit(solution)/shard_map/model/pallas_call | solution.py:1059
  (2 shorter events, 0.0 us)
Async XLA Ops:
  0.6 1.6 %collective-permute-start = (f32[16,1024]{1,0:T(8,128)}, f32[16,1024]{1,0:T(8,128)S(1)}, u32[]{:S(2)}, u32[]{:S(2)}) collective-permute-start(f32[16,1024]{1,0:T(8,128)} %template_hbm.1), channel_id=1, source_target_pairs={{1,0},{0,1},{3,2},{2,3},{5,4},{4,5},{7,6},{6,7},{9,8},{8,9},{11,10... | collective-permute-start | bytes 196616 | tf_op jit(solution)/shard_map/ppermute | solution.py:912
  2.3 6.0 %collective-permute-start.2 = (f32[24,1024]{1,0:T(8,128)S(1)}, f32[24,1024]{1,0:T(8,128)S(1)}, u32[]{:S(2)}, u32[]{:S(2)}) collective-permute-start(f32[24,1024]{1,0:T(8,128)S(1)} %edges.3), channel_id=1, source_target_pairs={{0,2},{4,6},{8,10},{12,14},{2,0},{6,4},{10,8},{14,12},{1,3},{5,7},... | collective-permute-start | bytes 294920 | tf_op jit(solution)/shard_map/ppermute | solution.py:956
  5.3 6.4 %collective-permute-start.1 = (f32[24,1024]{1,0:T(8,128)S(1)}, f32[24,1024]{1,0:T(8,128)S(1)}, u32[]{:S(2)}, u32[]{:S(2)}) collective-permute-start(f32[24,1024]{1,0:T(8,128)S(1)} %edges.2), channel_id=1, source_target_pairs={{2,4},{6,8},{10,12},{4,2},{8,6},{12,10},{3,5},{7,9},{11,13},{5,3},... | collective-permute-start | bytes 294920 | tf_op jit(solution)/shard_map/ppermute | solution.py:956
  13.5 7.6 %collective-permute-start.5 = (f32[48,128]{1,0:T(8,128)S(1)}, f32[48,128]{1,0:T(8,128)S(1)}, u32[]{:S(2)}, u32[]{:S(2)}) collective-permute-start(f32[48,128]{1,0:T(8,128)S(1)} %late.1.refs_5_.after_ref.refs_0_), channel_id=1, source_target_pairs={{0,2},{2,0},{4,6},{6,4},{8,10},{10,8},{12,14},{14,12},{1,3},{3,1},... | collective-permute-start | bytes 73736 | tf_op jit(solution)/shard_map/ppermute | solution.py:894
  16.3 4.9 %collective-permute-start.4 = (f32[48,128]{1,0:T(8,128)S(1)}, f32[48,128]{1,0:T(8,128)S(1)}, u32[]{:S(2)}, u32[]{:S(2)}) collective-permute-start(f32[48,128]{1,0:T(8,128)S(1)} %late.1.refs_5_.after_ref.refs_0_), channel_id=1, source_target_pairs={{0,6},{2,4},{4,2},{6,0},{8,14},{10,12},{12,10},{14,8},{1,7},{3,5},... | collective-permute-start | bytes 73736 | tf_op jit(solution)/shard_map/ppermute | solution.py:894
  17.6 3.8 %collective-permute-start.3 = (f32[48,128]{1,0:T(8,128)S(1)}, f32[48,128]{1,0:T(8,128)S(1)}, u32[]{:S(2)}, u32[]{:S(2)}) collective-permute-start(f32[48,128]{1,0:T(8,128)S(1)} %late.1.refs_5_.after_ref.refs_0_), channel_id=1, source_target_pairs={{0,4},{2,6},{4,0},{6,2},{8,12},{10,14},{12,8},{14,10},{1,5},{3,7},... | collective-permute-start | bytes 73736 | tf_op jit(solution)/shard_map/ppermute | solution.py:894
  21.4 4.8 %collective-permute-start.6 = (f32[48,128]{1,0:T(8,128)S(1)}, f32[48,128]{1,0:T(8,128)S(1)}, u32[]{:S(2)}, u32[]{:S(2)}) collective-permute-start(f32[48,128]{1,0:T(8,128)S(1)} %add.2.after_ref.refs_0_), channel_id=1, source_target_pairs={{0,8},{2,10},{4,12},{6,14},{8,0},{10,2},{12,4},{14,6},{1,9},{3,11}... | collective-permute-start | bytes 73736 | tf_op jit(solution)/shard_map/ppermute | solution.py:894

commit v6 on v5

--- a/solution.py
+++ b/solution.py
@@ -14,10 +14,12 @@
 LANES = 128
 BASE_PAD = 24
 BACK = 7
-FIT_ROWS = 3 * BASE_PAD
 BACK_FIRST = BASE_PAD - BASES
-TARGET = BASE_PAD + BASES + BACK - BACK_FIRST
-PACKED = 2 * BASE_PAD
+ALIGNED = BASES // 8 * 8
+SPILL = BASES - ALIGNED
+SPILL_AT = BASE_PAD - SPILL
+UNKNOWNS = 2 * BASE_PAD + ALIGNED
+FIT_ROWS = UNKNOWNS + 8
 REACH = HALF + 1
 GROUP = 32
 GROUPS_TILE = LANES // GROUP
@@ -63,33 +65,50 @@
     return lax.rem(lax.axis_index("stripe"), 2) == 0
 
 
-def edge_kernel(cores, toward_near, *refs):
+def edge_lines(rows, toward_near):
+    last = (rows - 8, rows - REACH, rows - 1)
+    first = (0, 8, 0)
+    return (last, first) if toward_near else (first, last)
+
+
+def sides_of(line, cores):
+    fold = line.shape[1] // cores
+    return [line[:, side * fold : (side + 1) * fold] for side in range(cores)]
+
+
+def near_kernel(cores, template_ref, science_ref, good_ref, edge_ref):
+    rows = template_ref.shape[0]
+
+    def edge(main, extra, outer):
+        parts = [template_ref[main : main + 8], template_ref[extra : extra + 2]]
+        for source in (science_ref, good_ref):
+            parts += sides_of(source[0, outer : outer + 1, :], cores)
+        spare = edge_ref.shape[0] - REACH - 2 * cores
+        return jnp.concatenate(parts + [jnp.zeros((spare, edge_ref.shape[1]), F32)], axis=0)
+
+    if_even, if_odd = (edge(*lines) for lines in edge_lines(rows, True))
+    edge_ref[...] = jnp.where(even_stripe(), if_even, if_odd)
+
+
+def far_kernel(cores, *refs):
     pieces = refs[:cores]
-    science_ref, good_ref = refs[cores : cores + 2]
-    edge_ref, ext = refs[-2:]
+    science_ref, good_ref, edge_ref, ext = refs[cores:]
     rows, half = pieces[0].shape
-    wide = science_ref.shape[2]
     me = lax.axis_index("exp")
     for step in range(cores):
         start = lax.rem(me + step, cores) * half
         ext[:, pl.ds(pl.multiple_of(start, LANES), half)] = pieces[step][...]
-    fold = wide // 2
-    low_first = rows - 8
-
-    def edge(first, extra, outer):
-        parts = [ext[first : first + 8, :fold], ext[first : first + 8, fold:]]
-        tail = []
+
+    def edge(main, extra, outer):
+        parts = sides_of(ext[main : main + 8], cores)
         for line in (extra, extra + 1):
-            tail += [ext[line : line + 1, :fold], ext[line : line + 1, fold:]]
-        science = science_ref[0, outer : outer + 1, :]
-        good = good_ref[0, outer : outer + 1, :]
-        for line in (science, good):
-            tail += [line[:, :fold], line[:, fold:]]
-        return jnp.concatenate(parts + tail, axis=0)
-
-    bottom = edge(low_first, rows - REACH, rows - 1)
-    top = edge(0, 8, 0)
-    edge_ref[...] = jnp.where(even_stripe() == toward_near, bottom, top)
+            parts += sides_of(ext[line : line + 1], cores)
+        for source in (science_ref, good_ref):
+            parts += sides_of(source[0, outer : outer + 1, :], cores)
+        return jnp.concatenate(parts, axis=0)
+
+    if_even, if_odd = (edge(*lines) for lines in edge_lines(rows, False))
+    edge_ref[...] = jnp.where(even_stripe(), if_even, if_odd)
 
 
 def load_kernel(
@@ -140,8 +159,9 @@
     row_ref, col_ref, weight_ref, late_ref, base_ref, pad
 ):
     pad[...] = jnp.zeros_like(pad)
-    pad[0, 0:BASES, 0:TAPS] = row_ref[...]
-    pad[1, 0:BASES, 0:TAPS] = col_ref[...]
+    for spot, source in enumerate((row_ref, col_ref)):
+        pad[spot, 0:BASES, 0:TAPS] = source[...]
+        pad[spot, SPILL_AT:BASE_PAD, 0:TAPS] = source[ALIGNED:BASES]
     row = pad[0]
     lane = lane_id(BASE_PAD)
     group = lane // GROUP
@@ -176,10 +196,10 @@
     inner = jnp.where(corner == 1, tap_at(0), jnp.where(corner == 2, tap_at(TAPS - 1), 0.0))
     outer = outer * spread
     inner = inner * spread
-    for tile in range(MAIN_TILES):
-        base_ref[:, tile * LANES : (tile + 1) * LANES] = mains[tile]
-    base_ref[:, MAIN : MAIN + LANES] = outer
-    base_ref[:, MAIN + LANES :] = inner
+    for tile, values in enumerate(mains + [outer, inner]):
+        base_ref[:, tile * LANES : (tile + 1) * LANES] = jnp.where(
+            row_id(BASE_PAD) < BASES, values, 0.0
+        )
     rows = weight_ref.shape[0] // (2 * BASE_PAD)
     even = even_stripe()
     first_tap, last_tap = tap_at(0), tap_at(TAPS - 1)
@@ -288,7 +308,6 @@
 def fill_extended(ext, highs, lows, cores, pieces, near_ref, far_ref):
     rows, half = pieces[0].shape
     wide = half * cores
-    fold = wide // 2
     ext[:, 0:LANES] = jnp.zeros((ext.shape[0], LANES), F32)
     ext[:, LANES + wide :] = jnp.zeros((ext.shape[0], LANES), F32)
     me = lax.axis_index("exp")
@@ -296,16 +315,12 @@
         start = lax.rem(me + step, cores) * half + LANES
         ext[8 : 8 + rows, pl.ds(pl.multiple_of(start, LANES), half)] = pieces[step][...]
     top, bottom = edges_of(near_ref, far_ref)
-    for side in range(2):
-        where = pl.ds(LANES + side * fold, fold)
+    for side in range(cores):
+        where = pl.ds(LANES + side * half, half)
         ext[0:8, where] = top[8 * side : 8 * side + 8]
         ext[8 + rows : 16 + rows, where] = bottom[8 * side : 8 * side + 8]
-        spare = [
-            top[16 + side : 17 + side],
-            top[18 + side : 19 + side],
-            bottom[16 + side : 17 + side],
-            bottom[18 + side : 19 + side],
-        ]
+        spots = [8 * cores + side, 9 * cores + side]
+        spare = [edge[spot : spot + 1] for edge in (top, bottom) for spot in spots]
         ext[16 + rows : 24 + rows, where] = jnp.concatenate(spare + spare, axis=0)
     main = slice(0, GROUP)
     highs[main], lows[main] = split_two(ext[main])
@@ -339,14 +354,15 @@
     return [steady, horiz, steady, horiz, square, steady, horiz]
 
 
-def put_halves(target, edge_ref, rows, first):
+def put_sides(target, edge_ref):
     fold = edge_ref.shape[1]
-    for side in range(2):
+    cores = edge_ref.shape[0] // (REACH + 2)
+    for side in range(cores):
         where = pl.ds(LANES + side * fold, fold)
-        target[first : first + 8, where] = edge_ref[8 * side : 8 * side + 8]
+        target[0:8, where] = edge_ref[8 * side : 8 * side + 8]
         for line in range(2):
-            spot = 16 + 2 * line + side
-            target[rows + line : rows + line + 1, where] = edge_ref[spot : spot + 1]
+            spot = (8 + line) * cores + side
+            target[8 + line : 9 + line, where] = edge_ref[spot : spot + 1]
 
 
 def paired(values):
@@ -375,21 +391,6 @@
     odd = pltpu.roll(odd, (HALF + STAMP_W + offset) % LANES, 1)
     even = pltpu.roll(even, HALF + offset, 1)
     return jnp.where(odd_rows(odd_ref, stamp, height), odd, even)
-
-
-def stamp_shifts(sources, targets, odd_ref, pair, moves):
-    columns = slice(pair * LANES, (pair + 1) * LANES)
-    for source, target in zip(sources, targets):
-        first = stamp_window(source, odd_ref, 2 * pair, 0)
-        second = stamp_window(source, odd_ref, 2 * pair + 1, STAMP_W)
-        for spot, (tile, move) in enumerate(moves):
-            a, b = first[16 * tile : 16 * tile + 16], second[16 * tile : 16 * tile + 16]
-            if move:
-                a = pltpu.roll(a, LANES - move, 1)
-                b = pltpu.roll(b, LANES - move, 1)
-            target[16 * spot : 16 * spot + 16, columns] = jnp.where(
-                lane_id(16) < STAMP_W, a, b
-            )
 
 
 def stamp_values(sources, odd_ref, pair, moves):
@@ -432,10 +433,19 @@
     scales = back_rows([steady, steady, vert, vert, steady, square, square])
     first, second = (profile * scale * keep for profile, scale in zip(profiles, scales))
     spot = lax.broadcasted_iota(jnp.int32, second.shape, 0)
-    second = jnp.where(spot == TARGET % 8, target, second)
     sloped = own * horiz
+    tilted = own * vert
+    mixed = jnp.where(spot < SPILL_AT - ALIGNED, second, tilted[ALIGNED:])
     return jnp.concatenate(
-        [own[:16], own[16:] + first, sloped[:16], sloped[16:] + second, own * vert], axis=0
+        [
+            own[:ALIGNED],
+            jnp.where(spot < SPILL, own[ALIGNED:], first),
+            sloped[:ALIGNED],
+            jnp.where(spot < SPILL, sloped[ALIGNED:], mixed),
+            tilted[:ALIGNED],
+            jnp.where(spot == 0, target, 0.0),
+        ],
+        axis=0,
     )
 
 
@@ -446,8 +456,8 @@
 
 def early_kernel(cores, stripes, *refs):
     pieces = refs[:cores]
+    near_pieces = refs[cores : 2 * cores]
     (
-        near_ref,
         science_ref,
         good_ref,
         odd_ref,
@@ -455,13 +465,12 @@
         total_ref,
         late_ref,
         aux_ref,
+        near_ref,
         ext,
         highs,
         lows,
-        xhigh,
-        xlow,
         bases,
-    ) = refs[cores:]
+    ) = refs[2 * cores :]
     rows, half = pieces[0].shape
     wide = science_ref.shape[2]
     pairs = wide // (4 * STAMP_W)
@@ -469,9 +478,15 @@
     ext[:, 0:LANES] = jnp.zeros((ext.shape[0], LANES), F32)
     ext[:, LANES + wide :] = jnp.zeros((ext.shape[0], LANES), F32)
     for step in range(cores):
-        start = lax.rem(me + step, cores) * half + LANES
-        ext[0:rows, pl.ds(pl.multiple_of(start, LANES), half)] = pieces[step][...]
-    put_halves(ext, near_ref, rows + 8, rows)
+        side = lax.rem(me + step, cores)
+        where = pl.ds(pl.multiple_of(side * half + LANES, LANES), half)
+        ext[0:rows, where] = pieces[step][...]
+        edge = near_pieces[step][...]
+        ext[rows : rows + REACH, where] = edge[:REACH]
+        near_ref[pl.ds(pl.multiple_of(8 * side, 8), 8), :] = edge[:8]
+        for line in range(2):
+            near_ref[pl.ds((8 + line) * cores + side, 1), :] = edge[8 + line : 9 + line]
+    near_ref[REACH * cores :] = near_pieces[0][REACH : REACH + 2 * cores]
     lines = jnp.concatenate(
         [ext[0:rows], paired(ext[rows : rows + 8]), corner_block(ext[rows + 8 : rows + 10])], axis=0
     )
@@ -482,7 +497,6 @@
     lane = lane_id(1)
     for pair in range(pairs):
         columns = slice(pair * LANES, (pair + 1) * LANES)
-        stamp_shifts((highs, lows), (xhigh, xlow), odd_ref, pair, moves)
         odd = jnp.where(
             lane < STAMP_W,
             odd_ref[2 * pair : 2 * pair + 1],
@@ -507,7 +521,14 @@
     chunk = 2 * LANES
     for start in range(0, wide // 2, chunk):
         span = slice(start, start + chunk)
-        values = three_products(weight_ref[...], xhigh[:, span], xlow[:, span])
+        made = [
+            stamp_values((highs, lows), odd_ref, pair, moves)
+            for pair in range(start // LANES, (start + chunk) // LANES)
+        ]
+        values = three_products(
+            weight_ref[...],
+            *(jnp.concatenate([one[side] for one in made], axis=1) for side in range(2)),
+        )
         late_ref[:, span] = values[:split]
         bases[:, span] = values[split:]
     horiz = aux_ref[2 * rows : 2 * rows + 1]
@@ -550,7 +571,7 @@
     pairs = width // LANES
     ext[:, 0:LANES] = jnp.zeros((ext.shape[0], LANES), F32)
     ext[:, ext.shape[1] - LANES :] = jnp.zeros((ext.shape[0], LANES), F32)
-    put_halves(ext, far_ref, 8, 0)
+    put_sides(ext, far_ref)
     lines = jnp.concatenate([paired(ext[0:8]), corner_block(ext[8:10])], axis=0)
     highs[...], lows[...] = split_two(lines)
     moves = [(0, 2 * step) for step in range(10)] + [(1, 8 * step) for step in range(3)]
@@ -593,36 +614,28 @@
 
 
 def packed_normal(normal):
-    room = LANES - FIT_ROWS
-    last = normal[PACKED:]
-    spare = jnp.zeros((BASE_PAD, 2 * room - FIT_ROWS), F32)
-    return jnp.concatenate(
+    half = UNKNOWNS // 2
+    lane = lane_id(8)
+    right = jnp.zeros((8, LANES), F32)
+    for tile in range(UNKNOWNS // 8):
+        column = normal[8 * tile : 8 * tile + 8, UNKNOWNS : UNKNOWNS + 1]
+        right = jnp.where(lane == tile, jnp.broadcast_to(column, (8, LANES)), right)
+    both = [normal[:half, :UNKNOWNS], normal[half:UNKNOWNS, :UNKNOWNS]]
+    return jnp.concatenate([jnp.concatenate(both, axis=1), right], axis=0)
+
+
+def unpacked_normal(packed):
+    half = UNKNOWNS // 2
+    lane = lane_id(UNKNOWNS)
+    values = jnp.concatenate([packed[:half], pltpu.roll(packed[:half], UNKNOWNS, 1)], axis=0)
+    right = jnp.concatenate(
         [
-            jnp.concatenate([normal[:BASE_PAD], last[:, :room]], axis=1),
-            jnp.concatenate([normal[BASE_PAD:PACKED], last[:, room:], spare], axis=1),
+            jnp.broadcast_to(packed[half:, tile : tile + 1], (8, LANES))
+            for tile in range(UNKNOWNS // 8)
         ],
         axis=0,
     )
-
-
-def unpacked_normal(packed):
-    room = LANES - FIT_ROWS
-    lane = lane_id(BASE_PAD)
-    last = jnp.where(
-        lane < room,
-        pltpu.roll(packed[:BASE_PAD], room, 1),
-        pltpu.roll(packed[BASE_PAD:], 2 * room, 1),
-    )
-    values = jnp.concatenate([packed, last], axis=0)
-    return jnp.where(lane_id(FIT_ROWS) < FIT_ROWS, values, 0.0)
-
-
-def panels():
-    out = []
-    for term, used in enumerate((BASE_PAD, BASES + BACK - BACK_FIRST, BASES)):
-        for start in range(0, used, 8):
-            out.append((term * BASE_PAD + start, min(8, used - start)))
-    return out
+    return jnp.where(lane < UNKNOWNS, values, jnp.where(lane == UNKNOWNS, right, 0.0))
 
 
 def tree_sum(values):
@@ -633,8 +646,8 @@
 
 def solve_rows(matrix):
     sub = row_id(8)
-    tiles = [matrix[start : start + 8] for start in range(0, FIT_ROWS, 8)]
-    order = panels()
+    tiles = [matrix[start : start + 8] for start in range(0, UNKNOWNS, 8)]
+    order = [(start, 8) for start in range(0, UNKNOWNS, 8)]
 
     def spread(tile, spot):
         return jnp.broadcast_to(tile[spot : spot + 1], (8, LANES))
@@ -681,10 +694,8 @@
                 tiles[place] = tiles[place] - tree_sum(
                     [columns[i][place] * spread(rows, i) for i in range(size)]
                 )
-    line = row_id(FIT_ROWS)
-    used = (line < TARGET) | ((line >= PACKED) & (line < PACKED + BASES))
-    right = jnp.concatenate(tiles, axis=0)[:, TARGET : TARGET + 1]
-    return jnp.where(used, jnp.broadcast_to(right, (FIT_ROWS, LANES)), 0.0)
+    right = jnp.concatenate(tiles, axis=0)[:, UNKNOWNS : UNKNOWNS + 1]
+    return jnp.broadcast_to(right, (UNKNOWNS, LANES))
 
 
 def region_weights(base_ref, weight_ref, rows):
@@ -729,23 +740,25 @@
     put_split(weight_ref, BASES * rows, jnp.concatenate(halos, axis=0))
 
 
-def region_bases(highs, lows, weight_ref, first, out_ref, xhigh, xlow):
-    clear_spare((xhigh, xlow))
+def region_bases(highs, lows, weight_ref, first, out_ref, scratch):
     wide = out_ref.shape[1]
-    chunk = 2 * LANES
-    for start in range(0, wide, chunk):
-        span = slice(start, start + chunk)
-        for source, target in ((highs, xhigh), (lows, xlow)):
+    chunk = scratch[0].shape[1]
+    for spot, start in enumerate(range(0, wide, chunk)):
+        targets = scratch[2 * spot : 2 * spot + 2]
+        clear_spare(targets)
+        for source, target in zip((highs, lows), targets):
 
             def shifted(tap, lines):
                 begin = first + start + LANES - HALF + tap
                 return source[lines, begin : begin + chunk]
 
             def put(place, values):
-                target[place : place + values.shape[0], span] = values
+                target[place : place + values.shape[0]] = values
 
             spread_window(shifted, put)
-        out_ref[:, span] = three_products(weight_ref[...], xhigh[:, span], xlow[:, span])
+        out_ref[:, start : start + chunk] = three_products(
+            weight_ref[...], targets[0][...], targets[1][...]
+        )
 
 
 def first_bases_kernel(cores, *refs):
@@ -760,16 +773,15 @@
         lows,
         out_ref,
         ext,
-        xhigh,
-        xlow,
+        *scratch,
     ) = refs[cores:]
     region_weights(base_ref, weight_ref, pieces[0].shape[0])
     fill_extended(ext, highs, lows, cores, pieces, near_ref, far_ref)
-    region_bases(highs, lows, weight_ref, 0, out_ref, xhigh, xlow)
-
-
-def next_bases_kernel(first, highs, lows, weight_ref, after_ref, out_ref, xhigh, xlow):
-    region_bases(highs, lows, weight_ref, first, out_ref, xhigh, xlow)
+    region_bases(highs, lows, weight_ref, 0, out_ref, scratch)
+
+
+def next_bases_kernel(first, highs, lows, weight_ref, after_ref, out_ref, *scratch):
+    region_bases(highs, lows, weight_ref, first, out_ref, scratch)
 
 
 def add_kernel(count, *refs):
@@ -787,10 +799,12 @@
     wide = science_ref.shape[2]
     top, bottom = edges_of(near_ref, far_ref)
     coef = solve_rows(unpacked_normal(normal_ref[...]))
-    lane = lane_id(FIT_ROWS)
+    lane = lane_id(UNKNOWNS)
+    base, term = lane // 3, lax.rem(lane, 3)
+    tilt = jnp.where(base < ALIGNED, 2 * BASE_PAD, BASE_PAD + SPILL_AT - ALIGNED) + base
     home = lane - 3 * BASES + jnp.where(lane < 3 * BASES + BACK_FIRST, BASES, BASE_PAD + BASES - BACK_FIRST)
-    home = jnp.where(lane < 3 * BASES, lax.rem(lane, 3) * BASE_PAD + lane // 3, home)
-    flat = jnp.sum(jnp.where(row_id(FIT_ROWS) == home, coef, 0.0), axis=0, keepdims=True)
+    home = jnp.where(lane < 3 * BASES, jnp.where(term == 2, tilt, term * BASE_PAD + base), home)
+    flat = jnp.sum(jnp.where(row_id(UNKNOWNS) == home, coef, 0.0), axis=0, keepdims=True)
     coef_ref[...] = flat[:, : coef_ref.shape[1]]
 
     def share(spot, height):
@@ -802,10 +816,19 @@
         position(jnp.full((8, LANES), first_row + line, jnp.int32), rows * stripes)
         for line in (rows, -1)
     ]
-    slopes = [share(2 * BASE_PAD + b, rows) * vert for b in range(BASES)]
-    halo_slopes = [
-        coef[2 * BASE_PAD : 3 * BASE_PAD] * jnp.concatenate([line] * 3, axis=0) for line in halo_vert
+    tilts = [
+        2 * BASE_PAD + b if b < ALIGNED else BASE_PAD + SPILL_AT + b - ALIGNED for b in range(BASES)
     ]
+    slopes = [share(spot, rows) * vert for spot in tilts]
+    tilted = jnp.concatenate(
+        [
+            coef[2 * BASE_PAD :],
+            coef[BASE_PAD + SPILL_AT : 2 * BASE_PAD],
+            jnp.zeros((BACK_FIRST, LANES), F32),
+        ],
+        axis=0,
+    )
+    halo_slopes = [tilted * jnp.concatenate([line] * 3, axis=0) for line in halo_vert]
     level = [
         share(BASES + m + (0 if m < BACK_FIRST else BASE_PAD - BACK_FIRST), 8) for m in range(BACK)
     ]
@@ -846,8 +869,13 @@
     own = good_ref[0] * (science_ref[0] - model)
 
     def halo(edge, values):
-        science = jnp.concatenate([edge[20:21], edge[21:22]], axis=1)
-        good = jnp.concatenate([edge[22:23], edge[23:24]], axis=1)
+        cores = edge.shape[0] // (REACH + 2)
+        science, good = (
+            jnp.concatenate(
+                [edge[spot : spot + 1] for spot in range(start * cores, (start + 1) * cores)], axis=1
+            )
+            for start in (REACH, REACH + 1)
+        )
         return good * (science - values)
 
     above_row = halo(top, above_model)
@@ -901,6 +929,13 @@
     return values
 
 
+def shared_pieces(values, cores):
+    return [
+        lax.ppermute(values, "exp", [((i + step) % cores, i) for i in range(cores)])
+        for step in range(1, cores)
+    ]
+
+
 def shards(template, exposure, cosmic_mask, stamp_blocks, row_filters, col_filters):
     arguments = (template, exposure, cosmic_mask, row_filters, col_filters, stamp_blocks)
     rows, half = template.shape
@@ -908,10 +943,7 @@
     cores = lax.axis_size("exp")
     stripes = lax.axis_size("stripe")
     params = pltpu.CompilerParams(vmem_limit_bytes=24 * 1024 * 1024)
-    pieces = [template] + [
-        lax.ppermute(template, "exp", [((i + step) % cores, i) for i in range(cores)])
-        for step in range(1, cores)
-    ]
+    pieces = [template] + shared_pieces(template, cores)
     stamps = stamp_blocks.shape[1]
     template_in, science, good, row_in, col_in, odd = pl.pallas_call(
         load_kernel,
@@ -934,29 +966,33 @@
         name="load",
     )(*[pltpu.with_memory_space_constraint(array, pltpu.HBM) for array in arguments])
     pieces = [template_in] + pieces[1:]
-    edge_shape = jax.ShapeDtypeStruct((24, wide // 2), F32)
-
-    def edge(toward_near, *others):
-        return pl.pallas_call(
-            functools.partial(edge_kernel, cores, toward_near),
-            out_shape=edge_shape,
-            in_specs=whole_vmem(cores + 2 + len(others)),
-            out_specs=pl.BlockSpec(memory_space=pltpu.VMEM),
-            scratch_shapes=[pltpu.VMEM((rows, wide), F32)],
-            compiler_params=params,
-            name="edges",
-        )(*pieces, science, good, *others)
-
-    far = edge(False)
-    near = edge(True)
     near_pairs = [(i, i + 1) for i in range(0, stripes - 1, 2)]
     far_pairs = [(i, i + 1) for i in range(1, stripes - 1, 2)]
 
     def swapped(values, couples):
         return lax.ppermute(values, "stripe", couples + [(b, a) for a, b in couples])
 
+    near = pl.pallas_call(
+        functools.partial(near_kernel, cores),
+        out_shape=jax.ShapeDtypeStruct((-(-(REACH + 2 * cores) // 8) * 8, half), F32),
+        in_specs=whole_vmem(3),
+        out_specs=pl.BlockSpec(memory_space=pltpu.VMEM),
+        compiler_params=params,
+        name="near",
+    )(template_in, science, good)
+    near = swapped(near, near_pairs)
+    near_pieces = [near] + shared_pieces(near, cores)
+    edge_shape = jax.ShapeDtypeStruct(((REACH + 2) * cores, half), F32)
+    far = pl.pallas_call(
+        functools.partial(far_kernel, cores),
+        out_shape=edge_shape,
+        in_specs=whole_vmem(cores + 2),
+        out_specs=pl.BlockSpec(memory_space=pltpu.VMEM),
+        scratch_shapes=[pltpu.VMEM((rows, wide), F32)],
+        compiler_params=params,
+        name="far",
+    )(*pieces, science, good)
     far = swapped(far, far_pairs)
-    near = swapped(near, near_pairs)
     early_shape = jax.ShapeDtypeStruct((2 * rows * BASE_PAD, EARLY), BF16)
     late_shape = jax.ShapeDtypeStruct((2 * LATE_ROWS, LATE), BF16)
     early_weights, late_weights, base = pl.pallas_call(
@@ -975,29 +1011,28 @@
     width = wide // 2
     reach = wide + 2 * LANES
     normal_shape = jax.ShapeDtypeStruct((FIT_ROWS, LANES), F32)
-    part, kept, aux = pl.pallas_call(
+    part, kept, aux, near = pl.pallas_call(
         functools.partial(early_kernel, cores, stripes),
         out_shape=(
             normal_shape,
             jax.ShapeDtypeStruct((HALF * BASE_PAD, width), F32),
             jax.ShapeDtypeStruct((2 * rows + 8, width), F32),
+            edge_shape,
         ),
-        in_specs=whole_vmem(cores + 5),
-        out_specs=tuple(whole_vmem(3)),
+        in_specs=whole_vmem(2 * cores + 4),
+        out_specs=tuple(whole_vmem(4)),
         scratch_shapes=[
             pltpu.VMEM((rows + 16, reach), F32),
             pltpu.VMEM((rows + 32, reach), BF16),
             pltpu.VMEM((rows + 32, reach), BF16),
-            pltpu.VMEM((EARLY, width), BF16),
-            pltpu.VMEM((EARLY, width), BF16),
             pltpu.VMEM(((rows - HALF) * BASE_PAD, width), F32),
         ],
         compiler_params=params,
         name="early",
-    )(*pieces, near, science, good, odd, early_weights)
+    )(*pieces, *near_pieces, science, good, odd, early_weights)
     normal = pl.pallas_call(
         functools.partial(late_kernel, stripes, rows),
-        out_shape=jax.ShapeDtypeStruct((PACKED, LANES), F32),
+        out_shape=jax.ShapeDtypeStruct((UNKNOWNS // 2 + 8, LANES), F32),
         in_specs=whole_vmem(6),
         out_specs=pl.BlockSpec(memory_space=pltpu.VMEM),
         scratch_shapes=[
@@ -1011,13 +1046,14 @@
     )(far, odd, late_weights, part, kept, aux)
     region_rows = BASES * rows + 2 * BASE_PAD
     blocks = wide // (2 * LANES)
-    cuts = [blocks * cut // 8 * 2 * LANES for cut in (0, 2, 5, 8)]
+    cuts = [blocks * cut // 8 * 2 * LANES for cut in (0, 2, 4, 8)]
     weight_shape = jax.ShapeDtypeStruct((2 * region_rows, DEPTH), BF16)
     source_shape = jax.ShapeDtypeStruct((GROUP + 16, reach), BF16)
     parts, shared = [], []
 
     def shift_scratch(size):
-        return [pltpu.VMEM((DEPTH, size), BF16)] * 2
+        chunk = 2 * LANES
+        return [pltpu.VMEM((DEPTH, chunk), BF16)] * (2 * (size // chunk))
 
     def first_bases(after):
         size = cuts[1]

time: 29.7 us -> 29.5 us (level)
  waiting for transfers between devices: 2.39 us -> 3.31 us
  starting transfers between devices: 11.1 us -> 10.4 us
  Pallas kernels: 15.3 us -> 14.9 us
    ppermute x2, waiting for transfers between devices: 1.57 us -> 2.01 us  [swapped(): lax.ppermute(values, 'stripe', couples + [(b, a) for a, b in couples])]
    ppermute x1 -> x2, waiting for transfers between devices: 0.04 us -> 0.45 us  [shared_pieces(): lax.ppermute(values, 'exp', [((i + step) % cores, i) for i in range(cores)])]
    pallas_call x1, Pallas kernels: 3.36 us -> 2.97 us  [shards(): pl.pallas_call(functools.partial(early_kernel, cores, stripes), out_shape...]
    ppermute x4, starting transfers between devices: 6.99 us -> 6.63 us  [summed(): lax.ppermute(values, axis, [(i, i ^ step) for i in range(count)])]
    ppermute x2, starting transfers between devices: 3.57 us -> 3.23 us  [swapped(): lax.ppermute(values, 'stripe', couples + [(b, a) for a, b in couples])]
  transfers between devices with their start and end apart: 7 -> 8, of which waited for: 3 -> 5; matrix products, arithmetic and copies ran while one was open for 0% -> 0% of each run, Pallas kernels for 34% -> 34%
where the time goes in v6:
time: 29.5 us; the launch traced here: 29.3 us
  Pallas kernels  14.9 us (51%)
  starting transfers between devices  10.4 us (35%)
  waiting for transfers between devices  3.31 us (11%)
  between operations  0.73 us (2%)
    ppermute x4, starting transfers between devices, summed(): lax.ppermute(values, axis, [(i, i ^ step) for i in range(count)])  6.63 us
    pallas_call x1, Pallas kernels, shards(): pl.pallas_call(functools.partial(model_kernel, stripes), out_shape=(jax.S...  3.3 us
    ppermute x2, starting transfers between devices, swapped(): lax.ppermute(values, 'stripe', couples + [(b, a) for a, b in couples])  3.23 us
    pallas_call x2, Pallas kernels, next_bases(): pl.pallas_call(functools.partial(next_bases_kernel, cuts[cut]), out_shape...  3.22 us
    pallas_call x1, Pallas kernels, shards(): pl.pallas_call(functools.partial(early_kernel, cores, stripes), out_shape...  2.97 us
    ppermute x2, waiting for transfers between devices, swapped(): lax.ppermute(values, 'stripe', couples + [(b, a) for a, b in couples])  2.01 us
    pallas_call x1, Pallas kernels, shards(): pl.pallas_call(functools.partial(late_kernel, stripes, rows), out_shape=j...  1.78 us
    pallas_call x1, Pallas kernels, first_bases(): pl.pallas_call(functools.partial(first_bases_kernel, cores), out_shape=(w...  1.68 us
  transfers between devices with their start and end apart: 8, of which 5 were waited for; matrix products, arithmetic and copies ran while one was open for 0% of the time, Pallas kernels for 34%

profile of v6, /device:TPU:0, one launch (start us, length us, event | category | flops | bytes accessed | tf_op | source)
XLA Modules:
  0.0 29.3 jit_solution(14062624000153396431)
XLA Ops:
  0.6 0.5 %collective-permute-start = (f32[16,1024]{1,0:T(8,128)}, f32[16,1024]{1,0:T(8,128)S(1)}, u32[]{:S(2)}, u32[]{:S(2)}) collective-permute-start(f32[16,1024]{1,0:T(8,128)} %template_hbm.1), channel_id=1, source_target_pairs={{1,0},{0,1},{3,2},{2,3},{5,4},{4,5},{7,6},{6,7},{9,8},{8,9},{11,10... | collective-permute-start | bytes 196616 | tf_op jit(solution)/shard_map/ppermute | solution.py:934
  1.1 1.1 %load.1 = (f32[16,1024]{1,0:T(8,128)S(1)}, f32[1,16,2048]{2,1,0:T(8,128)S(1)}, f32[1,16,2048]{2,1,0:T(8,128)S(1)}, f32[19,19]{1,0:T(8,128)S(1)}, f32[19,19]{1,0:T(8,128)S(1)}, /*index=5*/s32[16,128]{1,0:T(8,128)S(1)}) custom-call(f32[16,1024]{1,0:T(8,128)} %template_hbm.1, f32[1,16,2048]{2,1,0:T(8,128)} %science_hbm.1, s32[1,16,2048]{2,1,0:T(8,128)} %good_hbm.1, ...), custom_call_target="tpu_custom_call" | custom-call | tf_op jit(solution)/shard_map/load/pallas_call | solution.py:948
  2.3 2.6 %collective-permute-start.2 = (f32[16,1024]{1,0:T(8,128)S(1)}, f32[16,1024]{1,0:T(8,128)S(1)}, u32[]{:S(2)}, u32[]{:S(2)}) collective-permute-start(f32[16,1024]{1,0:T(8,128)S(1)} %near.1), channel_id=1, source_target_pairs={{0,2},{4,6},{8,10},{12,14},{2,0},{6,4},{10,8},{14,12},{1,3},{5,7},... | collective-permute-start | bytes 196616 | tf_op jit(solution)/shard_map/ppermute | solution.py:973
  4.8 0.0 collective-permute-done.refs_1_
  4.8 0.1 far.1
  4.9 0.7 %collective-permute-start.1 = (f32[24,1024]{1,0:T(8,128)S(1)}, f32[24,1024]{1,0:T(8,128)S(1)}, u32[]{:S(2)}, u32[]{:S(2)}) collective-permute-start(f32[24,1024]{1,0:T(8,128)S(1)} %far.1), channel_id=1, source_target_pairs={{2,4},{6,8},{10,12},{4,2},{8,6},{12,10},{3,5},{7,9},{11,13},{5,3},... | collective-permute-start | bytes 294920 | tf_op jit(solution)/shard_map/ppermute | solution.py:973
  5.6 2.0 %collective-permute-done.2.refs_2_ = f32[16,1024]{1,0:T(8,128)S(1)} collective-permute-done((f32[16,1024]{1,0:T(8,128)S(1)}, f32[16,1024]{1,0:T(8,128)S(1)}, u32[]{:S(2)}, u32[]{:S(2)}) %collective-permute-start.2) | collective-permute-done | bytes 65568 | tf_op jit(solution)/shard_map/ppermute | solution.py:973
  7.6 0.0 collective-permute-start.3
  7.6 0.8 %weights.1 = (bf16[768,512]{1,0:T(8,128)(2,1)S(1)}, bf16[448,256]{1,0:T(8,128)(2,1)S(1)}, f32[24,896]{1,0:T(8,128)S(1)}) custom-call(f32[19,19]{1,0:T(8,128)S(1)} %get-tuple-element.23.row_ref, f32[19,19]{1,0:T(8,128)S(1)} %get-tuple-element.24.col_ref), custom_call_target="tpu_custom_call" | custom-call | tf_op jit(solution)/shard_map/weights/pallas_call | solution.py:998
  8.4 0.4 %collective-permute-done.3.refs_3_ = f32[16,1024]{1,0:T(8,128)S(1)} collective-permute-done((f32[16,1024]{1,0:T(8,128)S(1)}, f32[16,1024]{1,0:T(8,128)S(1)}, u32[]{:S(2)}, u32[]{:S(2)}) %collective-permute-start.3) | collective-permute-done | bytes 65568 | tf_op jit(solution)/shard_map/ppermute | solution.py:934
  8.8 3.0 %early.1 = (f32[72,128]{1,0:T(8,128)S(1)}, f32[216,1024]{1,0:T(8,128)S(1)}, f32[40,1024]{1,0:T(8,128)S(1)}, f32[24,1024]{1,0:T(8,128)S(1)}) custom-call(f32[16,1024]{1,0:T(8,128)S(1)} %get-tuple-element.19.refs_0_.template_ref, f32[16,1024]{1,0:T(8,128)S(1)} %collective-permute-done.refs_1_, f32[16,1024]{1,0:T(8,128)S(1)} %collective-permute-done.2.refs_2_, ...), custom_call_target="tpu_custom_call" | custom-call | tf_op jit(solution)/shard_map/early/pallas_call | solution.py:1014
  11.8 0.0 collective-permute-done.1.refs_0_.refs_2_.refs_3_
  11.8 1.8 %late.1.refs_5_.after_ref.refs_0_ = f32[40,128]{1,0:T(8,128)S(1)} custom-call(f32[24,1024]{1,0:T(8,128)S(1)} %collective-permute-done.1.refs_0_.refs_2_.refs_3_, s32[16,128]{1,0:T(8,128)S(1)} %get-tuple-element.22.refs_6_.refs_1_, bf16[448,256]{1,0:T(8,128)(2,1)S(1)} %get-tuple-element.25.refs_2_, f32[72,128]{1,0:T(8,128)S(1)} %get-tuple-element.27.refs_3_, ...), custom_call_target="tpu_custom_call" | custom-call | tf_op jit(solution)/shard_map/late/pallas_call | solution.py:1033
  13.6 2.4 %collective-permute-start.6 = (f32[40,128]{1,0:T(8,128)S(1)}, f32[40,128]{1,0:T(8,128)S(1)}, u32[]{:S(2)}, u32[]{:S(2)}) collective-permute-start(f32[40,128]{1,0:T(8,128)S(1)} %late.1.refs_5_.after_ref.refs_0_), channel_id=1, source_target_pairs={{0,2},{2,0},{4,6},{6,4},{8,10},{10,8},{12,14},{14,12},{1,3},{3,1},... | collective-permute-start | bytes 61448 | tf_op jit(solution)/shard_map/ppermute | solution.py:922
  16.0 1.5 %collective-permute-start.5 = (f32[40,128]{1,0:T(8,128)S(1)}, f32[40,128]{1,0:T(8,128)S(1)}, u32[]{:S(2)}, u32[]{:S(2)}) collective-permute-start(f32[40,128]{1,0:T(8,128)S(1)} %late.1.refs_5_.after_ref.refs_0_), channel_id=1, source_target_pairs={{0,6},{2,4},{4,2},{6,0},{8,14},{10,12},{12,10},{14,8},{1,7},{3,5},... | collective-permute-start | bytes 61448 | tf_op jit(solution)/shard_map/ppermute | solution.py:922
  17.5 0.1 collective-permute-start.4
  17.6 1.7 %bases.3 = (bf16[704,768]{1,0:T(8,128)(2,1)S(1)}, bf16[48,2304]{1,0:T(8,128)(2,1)S(1)}, bf16[48,2304]{1,0:T(8,128)(2,1)S(1)}, f32[352,512]{1,0:T(8,128)S(1)}) custom-call(f32[16,1024]{1,0:T(8,128)S(1)} %get-tuple-element.19.refs_0_.template_ref, f32[16,1024]{1,0:T(8,128)S(1)} %collective-permute-done.refs_1_, ...), custom_call_target="tpu_custom_call" | custom-call | tf_op jit(solution)/shard_map/bases/pallas_call | solution.py:1060
  19.3 1.2 %bases.4.refs_5_.refs_1_ = f32[352,512]{1,0:T(8,128)S(1)} custom-call(bf16[48,2304]{1,0:T(8,128)(2,1)S(1)} %get-tuple-element.33.highs, bf16[48,2304]{1,0:T(8,128)(2,1)S(1)} %get-tuple-element.34.lows, bf16[704,768]{1,0:T(8,128)(2,1)S(1)} %get-tuple-element.35.weight_ref, f32[40,128]{1,0:T(8,128)S(1)} %late.1.refs_5_.after_ref.refs_0_), custom_call_target="tpu_custom_call" | custom-call | tf_op jit(solution)/shard_map/bases/pallas_call | solution.py:1081
  20.5 0.0 collective-permute-done.6.refs_3_
  20.5 0.2 collective-permute-done.5.refs_2_
  20.7 0.6 %collective-permute-done.4.refs_1_ = f32[40,128]{1,0:T(8,128)S(1)} collective-permute-done((f32[40,128]{1,0:T(8,128)S(1)}, f32[40,128]{1,0:T(8,128)S(1)}, u32[]{:S(2)}, u32[]{:S(2)}) %collective-permute-start.4) | collective-permute-done | bytes 20512 | tf_op jit(solution)/shard_map/ppermute | solution.py:922
  21.3 2.6 %collective-permute-start.7 = (f32[40,128]{1,0:T(8,128)S(1)}, f32[40,128]{1,0:T(8,128)S(1)}, u32[]{:S(2)}, u32[]{:S(2)}) collective-permute-start(f32[40,128]{1,0:T(8,128)S(1)} %add.2.after_ref.refs_0_), channel_id=1, source_target_pairs={{0,8},{2,10},{4,12},{6,14},{8,0},{10,2},{12,4},{14,6},{1,9},{3,11}... | collective-permute-start | bytes 61448 | tf_op jit(solution)/shard_map/ppermute | solution.py:922
  23.9 2.0 %bases.5.refs_2_ = f32[352,1024]{1,0:T(8,128)S(1)} custom-call(bf16[48,2304]{1,0:T(8,128)(2,1)S(1)} %get-tuple-element.33.highs, bf16[48,2304]{1,0:T(8,128)(2,1)S(1)} %get-tuple-element.34.lows, bf16[704,768]{1,0:T(8,128)(2,1)S(1)} %get-tuple-element.35.weight_ref, f32[40,128]{1,0:T(8,128)S(1)} %add.2.after_ref.refs_0_), custom_call_target="tpu_custom_call" | custom-call | tf_op jit(solution)/shard_map/bases/pallas_call | solution.py:1081
  26.0 0.1 collective-permute-done.7.refs_1_
  26.0 3.3 %model.1 = (f32[1,16,2048]{2,1,0:T(8,128)}, f32[1,64]{1,0:T(1,128)}) custom-call(f32[40,128]{1,0:T(8,128)S(1)} %add.3.normal_ref, f32[352,512]{1,0:T(8,128)S(1)} %get-tuple-element.32.refs_4_.refs_0_, f32[352,512]{1,0:T(8,128)S(1)} %bases.4.refs_5_.refs_1_, f32[352,1024]{1,0:T(8,128)S(1)} %bases.5.refs_2_, ...), custom_call_target="tpu_custom_call" | custom-call | tf_op jit(solution)/shard_map/model/pallas_call | solution.py:1095
  (3 shorter events, 0.0 us)
Async XLA Ops:
  0.6 4.2 %collective-permute-start = (f32[16,1024]{1,0:T(8,128)}, f32[16,1024]{1,0:T(8,128)S(1)}, u32[]{:S(2)}, u32[]{:S(2)}) collective-permute-start(f32[16,1024]{1,0:T(8,128)} %template_hbm.1), channel_id=1, source_target_pairs={{1,0},{0,1},{3,2},{2,3},{5,4},{4,5},{7,6},{6,7},{9,8},{8,9},{11,10... | collective-permute-start | bytes 196616 | tf_op jit(solution)/shard_map/ppermute | solution.py:934
  2.3 5.3 %collective-permute-start.2 = (f32[16,1024]{1,0:T(8,128)S(1)}, f32[16,1024]{1,0:T(8,128)S(1)}, u32[]{:S(2)}, u32[]{:S(2)}) collective-permute-start(f32[16,1024]{1,0:T(8,128)S(1)} %near.1), channel_id=1, source_target_pairs={{0,2},{4,6},{8,10},{12,14},{2,0},{6,4},{10,8},{14,12},{1,3},{5,7},... | collective-permute-start | bytes 196616 | tf_op jit(solution)/shard_map/ppermute | solution.py:973
  4.9 6.9 %collective-permute-start.1 = (f32[24,1024]{1,0:T(8,128)S(1)}, f32[24,1024]{1,0:T(8,128)S(1)}, u32[]{:S(2)}, u32[]{:S(2)}) collective-permute-start(f32[24,1024]{1,0:T(8,128)S(1)} %far.1), channel_id=1, source_target_pairs={{2,4},{6,8},{10,12},{4,2},{8,6},{12,10},{3,5},{7,9},{11,13},{5,3},... | collective-permute-start | bytes 294920 | tf_op jit(solution)/shard_map/ppermute | solution.py:973
  7.6 1.3 %collective-permute-start.3 = (f32[16,1024]{1,0:T(8,128)S(1)}, f32[16,1024]{1,0:T(8,128)S(1)}, u32[]{:S(2)}, u32[]{:S(2)}) collective-permute-start(f32[16,1024]{1,0:T(8,128)S(1)} %collective-permute-done.2.refs_2_), channel_id=1, source_target_pairs={{1,0},{0,1},{3,2},{2,3},{5,4},{4,5},{7,6},{6,7},{9,8},{8,9},{11,10... | collective-permute-start | bytes 196616 | tf_op jit(solution)/shard_map/ppermute | solution.py:934
  13.6 6.9 %collective-permute-start.6 = (f32[40,128]{1,0:T(8,128)S(1)}, f32[40,128]{1,0:T(8,128)S(1)}, u32[]{:S(2)}, u32[]{:S(2)}) collective-permute-start(f32[40,128]{1,0:T(8,128)S(1)} %late.1.refs_5_.after_ref.refs_0_), channel_id=1, source_target_pairs={{0,2},{2,0},{4,6},{6,4},{8,10},{10,8},{12,14},{14,12},{1,3},{3,1},... | collective-permute-start | bytes 61448 | tf_op jit(solution)/shard_map/ppermute | solution.py:922
  16.0 4.7 %collective-permute-start.5 = (f32[40,128]{1,0:T(8,128)S(1)}, f32[40,128]{1,0:T(8,128)S(1)}, u32[]{:S(2)}, u32[]{:S(2)}) collective-permute-start(f32[40,128]{1,0:T(8,128)S(1)} %late.1.refs_5_.after_ref.refs_0_), channel_id=1, source_target_pairs={{0,6},{2,4},{4,2},{6,0},{8,14},{10,12},{12,10},{14,8},{1,7},{3,5},... | collective-permute-start | bytes 61448 | tf_op jit(solution)/shard_map/ppermute | solution.py:922
  17.5 3.8 %collective-permute-start.4 = (f32[40,128]{1,0:T(8,128)S(1)}, f32[40,128]{1,0:T(8,128)S(1)}, u32[]{:S(2)}, u32[]{:S(2)}) collective-permute-start(f32[40,128]{1,0:T(8,128)S(1)} %late.1.refs_5_.after_ref.refs_0_), channel_id=1, source_target_pairs={{0,4},{2,6},{4,0},{6,2},{8,12},{10,14},{12,8},{14,10},{1,5},{3,7},... | collective-permute-start | bytes 61448 | tf_op jit(solution)/shard_map/ppermute | solution.py:922
  21.3 4.7 %collective-permute-start.7 = (f32[40,128]{1,0:T(8,128)S(1)}, f32[40,128]{1,0:T(8,128)S(1)}, u32[]{:S(2)}, u32[]{:S(2)}) collective-permute-start(f32[40,128]{1,0:T(8,128)S(1)} %add.2.after_ref.refs_0_), channel_id=1, source_target_pairs={{0,8},{2,10},{4,12},{6,14},{8,0},{10,2},{12,4},{14,6},{1,9},{3,11}... | collective-permute-start | bytes 61448 | tf_op jit(solution)/shard_map/ppermute | solution.py:922

commit v7 on v6

--- a/solution.py
+++ b/solution.py
@@ -792,13 +792,13 @@
     refs[-1][...] = tree_sum(values)
 
 
-def model_kernel(stripes, normal_ref, *refs):
+def model_kernel(stripes, count, *refs):
     far_ref, near_ref, science_ref, good_ref, out_ref, coef_ref = refs[-6:]
-    parts = refs[:-6]
+    parts = refs[count:-6]
     rows = science_ref.shape[1]
     wide = science_ref.shape[2]
     top, bottom = edges_of(near_ref, far_ref)
-    coef = solve_rows(unpacked_normal(normal_ref[...]))
+    coef = solve_rows(unpacked_normal(tree_sum([ref[...] for ref in refs[:count]])))
     lane = lane_id(UNKNOWNS)
     base, term = lane // 3, lax.rem(lane, 3)
     tilt = jnp.where(base < ALIGNED, 2 * BASE_PAD, BASE_PAD + SPILL_AT - ALIGNED) + base
@@ -846,48 +846,59 @@
             )
         return steady + here * sloped + square * curved
 
-    models, halos = [], [[], []]
+    lane_row = lane_id(rows)
+    line_row = row_id(rows)
+    tiles = wide // LANES
+    edges = []
+    for edge in (top, bottom):
+        cores = edge.shape[0] // (REACH + 2)
+        edges.append(
+            [
+                jnp.concatenate(
+                    [edge[spot : spot + 1] for spot in range(first * cores, (first + 1) * cores)],
+                    axis=1,
+                )
+                for first in (REACH, REACH + 1)
+            ]
+        )
+    owns, aboves, belows = [], [], []
+
+    def put_tile(tile):
+        own = owns[tile]
+        empty = jnp.zeros_like(own)
+        earlier = owns[tile - 1] if tile else empty
+        later = owns[tile + 1] if tile + 1 < tiles else empty
+        above = jnp.where(line_row == 0, aboves[tile], pltpu.roll(own, 1, 0))
+        below = jnp.where(line_row == rows - 1, belows[tile], pltpu.roll(own, rows - 1, 0))
+        before = pltpu.roll(jnp.where(lane_row == LANES - 1, earlier, own), 1, 1)
+        after = pltpu.roll(jnp.where(lane_row == 0, later, own), LANES - 1, 1)
+        span = slice(tile * LANES, (tile + 1) * LANES)
+        out_ref[0, :, span] = 4.0 * own - (below + above + after + before)
+
     for part in parts:
         for start in range(0, part.shape[1], LANES):
             span = slice(start, start + LANES)
-            begin = len(models) * LANES
+            tile = len(owns)
+            begin = tile * LANES
+            place = slice(begin, begin + LANES)
             horiz = position(begin + lane_id(8), wide)
             total = ground(vert, horiz)
             for b in range(BASES):
                 steady = share(b, 8) + share(BASE_PAD + b, 8) * horiz
                 scale = jnp.concatenate([steady] * (rows // 8), axis=0) + slopes[b]
                 total = total + part[b * rows : (b + 1) * rows, span] * scale
-            models.append(total)
+            owns.append(good_ref[0, :, place] * (science_ref[0, :, place] - total))
             steady = coef[:BASE_PAD] + coef[BASE_PAD : 2 * BASE_PAD] * horiz[0:1]
-            for side in range(2):
-                place = BASES * rows + side * BASE_PAD
-                values = part[place : place + BASE_PAD, span] * (steady + halo_slopes[side])
+            for side, kept in enumerate((belows, aboves)):
+                spot = BASES * rows + side * BASE_PAD
+                values = part[spot : spot + BASE_PAD, span] * (steady + halo_slopes[side])
                 values = jnp.sum(values, axis=0, keepdims=True)
-                halos[side].append(values + ground(halo_vert[side], horiz)[0:1])
-    model = jnp.concatenate(models, axis=1)
-    below_model, above_model = (jnp.concatenate(side, axis=1) for side in halos)
-    own = good_ref[0] * (science_ref[0] - model)
-
-    def halo(edge, values):
-        cores = edge.shape[0] // (REACH + 2)
-        science, good = (
-            jnp.concatenate(
-                [edge[spot : spot + 1] for spot in range(start * cores, (start + 1) * cores)], axis=1
-            )
-            for start in (REACH, REACH + 1)
-        )
-        return good * (science - values)
-
-    above_row = halo(top, above_model)
-    below_row = halo(bottom, below_model)
-    lines = lax.broadcasted_iota(jnp.int32, (rows, wide), 0)
-    spots = lax.broadcasted_iota(jnp.int32, (rows, wide), 1)
-    above = jnp.where(lines == 0, above_row, pltpu.roll(own, 1, 0))
-    below = jnp.where(lines == rows - 1, below_row, pltpu.roll(own, rows - 1, 0))
-    before = jnp.where(spots == 0, 0.0, pltpu.roll(own, 1, 1))
-    after = jnp.where(spots == wide - 1, 0.0, pltpu.roll(own, wide - 1, 1))
-    out_ref[0] = 4.0 * own - (below + above + after + before)
-
+                values = values + ground(halo_vert[side], horiz)[0:1]
+                science, good = edges[1 - side]
+                kept.append(good[:, place] * (science[:, place] - values))
+            if tile:
+                put_tile(tile - 1)
+    put_tile(tiles - 1)
 
 def whole_vmem(count):
     return [pl.BlockSpec(memory_space=pltpu.VMEM)] * count
@@ -910,12 +921,13 @@
         for works in beside:
             for work in works:
                 work(values)
-        return lax.psum(values, axis)
+        return [lax.psum(values, axis)]
     rounds = [(1, 2, 3)] if count >= 4 else []
     step = 4 if rounds else 1
     while step < count:
         rounds.append((step,))
         step *= 2
+    last = len(rounds) - 1
     rounds += [()] * (len(beside) - len(rounds))
     for spot, steps in enumerate(rounds):
         others = [
@@ -925,8 +937,13 @@
         if steps:
             if len(others) == 3:
                 others = [others[k] for k in (1, 2, 0)]
+            if spot == last:
+                for works in beside[spot + 1 :]:
+                    for work in works:
+                        work(values)
+                return [values] + others
             values = add([values] + others, after, params)
-    return values
+    return [values]
 
 
 def shared_pieces(values, cores):
@@ -1091,18 +1108,18 @@
         return part
 
     beside = [[first_bases, functools.partial(next_bases, 1)], [functools.partial(next_bases, 2)]]
-    normal = summed(normal, "stripe", beside, params)
+    shares = summed(normal, "stripe", beside, params)
     filtered, coef = pl.pallas_call(
-        functools.partial(model_kernel, stripes),
+        functools.partial(model_kernel, stripes, len(shares)),
         out_shape=(
             jax.ShapeDtypeStruct(exposure.shape, F32),
             jax.ShapeDtypeStruct((1, 3 * BASES + BACK), F32),
         ),
-        in_specs=whole_vmem(1 + len(parts) + 4),
+        in_specs=whole_vmem(len(shares) + len(parts) + 4),
         out_specs=tuple(whole_vmem(2)),
         compiler_params=params,
         name="model",
-    )(normal, *parts, far, near, science, good)
+    )(*shares, *parts, far, near, science, good)
     return filtered, coef
 
 

time: 29.5 us -> 29.6 us (level)
  transfers between devices with their start and end apart: 8 -> 8, of which waited for: 5 -> 4; matrix products, arithmetic and copies ran while one was open for 0% -> 0% of each run, Pallas kernels for 34% -> 33%
where the time goes in v7:
time: 29.6 us; the launch traced here: 29.4 us
  Pallas kernels  15 us (51%)
  starting transfers between devices  10.4 us (35%)
  waiting for transfers between devices  3.29 us (11%)
  between operations  0.73 us (2%)
    ppermute x4, starting transfers between devices, summed(): lax.ppermute(values, axis, [(i, i ^ step) for i in range(count)])  6.63 us
    pallas_call x1, Pallas kernels, shards(): pl.pallas_call(functools.partial(model_kernel, stripes, len(shares)), out...  3.36 us
    ppermute x2, starting transfers between devices, swapped(): lax.ppermute(values, 'stripe', couples + [(b, a) for a, b in couples])  3.23 us
    pallas_call x2, Pallas kernels, next_bases(): pl.pallas_call(functools.partial(next_bases_kernel, cuts[cut]), out_shape...  3.23 us
    pallas_call x1, Pallas kernels, shards(): pl.pallas_call(functools.partial(early_kernel, cores, stripes), out_shape...  2.97 us
    ppermute x2, waiting for transfers between devices, swapped(): lax.ppermute(values, 'stripe', couples + [(b, a) for a, b in couples])  2.01 us
    pallas_call x1, Pallas kernels, shards(): pl.pallas_call(functools.partial(late_kernel, stripes, rows), out_shape=j...  1.78 us
    pallas_call x1, Pallas kernels, first_bases(): pl.pallas_call(functools.partial(first_bases_kernel, cores), out_shape=(w...  1.69 us
  transfers between devices with their start and end apart: 8, of which 4 were waited for; matrix products, arithmetic and copies ran while one was open for 0% of the time, Pallas kernels for 33%

profile of v7, /device:TPU:0, one launch (start us, length us, event | category | flops | bytes accessed | tf_op | source)
XLA Modules:
  0.0 29.4 jit_solution(7531451977914431828)
XLA Ops:
  0.6 0.5 %collective-permute-start = (f32[16,1024]{1,0:T(8,128)}, f32[16,1024]{1,0:T(8,128)S(1)}, u32[]{:S(2)}, u32[]{:S(2)}) collective-permute-start(f32[16,1024]{1,0:T(8,128)} %template_hbm.1), channel_id=1, source_target_pairs={{1,0},{0,1},{3,2},{2,3},{5,4},{4,5},{7,6},{6,7},{9,8},{8,9},{11,10... | collective-permute-start | bytes 196616 | tf_op jit(solution)/shard_map/ppermute | solution.py:951
  1.1 1.1 %load.1 = (f32[16,1024]{1,0:T(8,128)S(1)}, f32[1,16,2048]{2,1,0:T(8,128)S(1)}, f32[1,16,2048]{2,1,0:T(8,128)S(1)}, f32[19,19]{1,0:T(8,128)S(1)}, f32[19,19]{1,0:T(8,128)S(1)}, /*index=5*/s32[16,128]{1,0:T(8,128)S(1)}) custom-call(f32[16,1024]{1,0:T(8,128)} %template_hbm.1, f32[1,16,2048]{2,1,0:T(8,128)} %science_hbm.1, s32[1,16,2048]{2,1,0:T(8,128)} %good_hbm.1, ...), custom_call_target="tpu_custom_call" | custom-call | tf_op jit(solution)/shard_map/load/pallas_call | solution.py:965
  2.3 2.6 %collective-permute-start.2 = (f32[16,1024]{1,0:T(8,128)S(1)}, f32[16,1024]{1,0:T(8,128)S(1)}, u32[]{:S(2)}, u32[]{:S(2)}) collective-permute-start(f32[16,1024]{1,0:T(8,128)S(1)} %near.1), channel_id=1, source_target_pairs={{0,2},{4,6},{8,10},{12,14},{2,0},{6,4},{10,8},{14,12},{1,3},{5,7},... | collective-permute-start | bytes 196616 | tf_op jit(solution)/shard_map/ppermute | solution.py:990
  4.8 0.0 collective-permute-done.refs_1_
  4.8 0.1 far.1
  4.9 0.7 %collective-permute-start.1 = (f32[24,1024]{1,0:T(8,128)S(1)}, f32[24,1024]{1,0:T(8,128)S(1)}, u32[]{:S(2)}, u32[]{:S(2)}) collective-permute-start(f32[24,1024]{1,0:T(8,128)S(1)} %far.1), channel_id=1, source_target_pairs={{2,4},{6,8},{10,12},{4,2},{8,6},{12,10},{3,5},{7,9},{11,13},{5,3},... | collective-permute-start | bytes 294920 | tf_op jit(solution)/shard_map/ppermute | solution.py:990
  5.6 2.0 %collective-permute-done.2.refs_2_ = f32[16,1024]{1,0:T(8,128)S(1)} collective-permute-done((f32[16,1024]{1,0:T(8,128)S(1)}, f32[16,1024]{1,0:T(8,128)S(1)}, u32[]{:S(2)}, u32[]{:S(2)}) %collective-permute-start.2) | collective-permute-done | bytes 65568 | tf_op jit(solution)/shard_map/ppermute | solution.py:990
  7.6 0.0 collective-permute-start.3
  7.6 0.8 %weights.1 = (bf16[768,512]{1,0:T(8,128)(2,1)S(1)}, bf16[448,256]{1,0:T(8,128)(2,1)S(1)}, f32[24,896]{1,0:T(8,128)S(1)}) custom-call(f32[19,19]{1,0:T(8,128)S(1)} %get-tuple-element.23.row_ref, f32[19,19]{1,0:T(8,128)S(1)} %get-tuple-element.24.col_ref), custom_call_target="tpu_custom_call" | custom-call | tf_op jit(solution)/shard_map/weights/pallas_call | solution.py:1015
  8.4 0.4 %collective-permute-done.3.refs_3_ = f32[16,1024]{1,0:T(8,128)S(1)} collective-permute-done((f32[16,1024]{1,0:T(8,128)S(1)}, f32[16,1024]{1,0:T(8,128)S(1)}, u32[]{:S(2)}, u32[]{:S(2)}) %collective-permute-start.3) | collective-permute-done | bytes 65568 | tf_op jit(solution)/shard_map/ppermute | solution.py:951
  8.8 3.0 %early.1 = (f32[72,128]{1,0:T(8,128)S(1)}, f32[216,1024]{1,0:T(8,128)S(1)}, f32[40,1024]{1,0:T(8,128)S(1)}, f32[24,1024]{1,0:T(8,128)S(1)}) custom-call(f32[16,1024]{1,0:T(8,128)S(1)} %get-tuple-element.19.refs_0_.template_ref, f32[16,1024]{1,0:T(8,128)S(1)} %collective-permute-done.refs_1_, f32[16,1024]{1,0:T(8,128)S(1)} %collective-permute-done.2.refs_2_, ...), custom_call_target="tpu_custom_call" | custom-call | tf_op jit(solution)/shard_map/early/pallas_call | solution.py:1031
  11.8 0.0 collective-permute-done.1.refs_0_.refs_2_.refs_5_
  11.8 1.8 %late.1.refs_5_.after_ref.refs_0_ = f32[40,128]{1,0:T(8,128)S(1)} custom-call(f32[24,1024]{1,0:T(8,128)S(1)} %collective-permute-done.1.refs_0_.refs_2_.refs_5_, s32[16,128]{1,0:T(8,128)S(1)} %get-tuple-element.22.refs_6_.refs_1_, bf16[448,256]{1,0:T(8,128)(2,1)S(1)} %get-tuple-element.25.refs_2_, f32[72,128]{1,0:T(8,128)S(1)} %get-tuple-element.27.refs_3_, ...), custom_call_target="tpu_custom_call" | custom-call | tf_op jit(solution)/shard_map/late/pallas_call | solution.py:1050
  13.6 2.4 %collective-permute-start.6 = (f32[40,128]{1,0:T(8,128)S(1)}, f32[40,128]{1,0:T(8,128)S(1)}, u32[]{:S(2)}, u32[]{:S(2)}) collective-permute-start(f32[40,128]{1,0:T(8,128)S(1)} %late.1.refs_5_.after_ref.refs_0_), channel_id=1, source_target_pairs={{0,2},{2,0},{4,6},{6,4},{8,10},{10,8},{12,14},{14,12},{1,3},{3,1},... | collective-permute-start | bytes 61448 | tf_op jit(solution)/shard_map/ppermute | solution.py:934
  16.0 1.5 %collective-permute-start.5 = (f32[40,128]{1,0:T(8,128)S(1)}, f32[40,128]{1,0:T(8,128)S(1)}, u32[]{:S(2)}, u32[]{:S(2)}) collective-permute-start(f32[40,128]{1,0:T(8,128)S(1)} %late.1.refs_5_.after_ref.refs_0_), channel_id=1, source_target_pairs={{0,6},{2,4},{4,2},{6,0},{8,14},{10,12},{12,10},{14,8},{1,7},{3,5},... | collective-permute-start | bytes 61448 | tf_op jit(solution)/shard_map/ppermute | solution.py:934
  17.5 0.1 collective-permute-start.4
  17.6 1.7 %bases.3 = (bf16[704,768]{1,0:T(8,128)(2,1)S(1)}, bf16[48,2304]{1,0:T(8,128)(2,1)S(1)}, bf16[48,2304]{1,0:T(8,128)(2,1)S(1)}, f32[352,512]{1,0:T(8,128)S(1)}) custom-call(f32[16,1024]{1,0:T(8,128)S(1)} %get-tuple-element.19.refs_0_.template_ref, f32[16,1024]{1,0:T(8,128)S(1)} %collective-permute-done.refs_1_, ...), custom_call_target="tpu_custom_call" | custom-call | tf_op jit(solution)/shard_map/bases/pallas_call | solution.py:1077
  19.3 1.2 %bases.4.refs_5_.refs_3_ = f32[352,512]{1,0:T(8,128)S(1)} custom-call(bf16[48,2304]{1,0:T(8,128)(2,1)S(1)} %get-tuple-element.33.highs, bf16[48,2304]{1,0:T(8,128)(2,1)S(1)} %get-tuple-element.34.lows, bf16[704,768]{1,0:T(8,128)(2,1)S(1)} %get-tuple-element.35.weight_ref, f32[40,128]{1,0:T(8,128)S(1)} %late.1.refs_5_.after_ref.refs_0_), custom_call_target="tpu_custom_call" | custom-call | tf_op jit(solution)/shard_map/bases/pallas_call | solution.py:1098
  20.5 0.0 collective-permute-done.6.refs_3_
  20.5 0.2 collective-permute-done.5.refs_2_
  20.7 0.6 %collective-permute-done.4.refs_1_ = f32[40,128]{1,0:T(8,128)S(1)} collective-permute-done((f32[40,128]{1,0:T(8,128)S(1)}, f32[40,128]{1,0:T(8,128)S(1)}, u32[]{:S(2)}, u32[]{:S(2)}) %collective-permute-start.4) | collective-permute-done | bytes 20512 | tf_op jit(solution)/shard_map/ppermute | solution.py:934
  21.3 2.6 %collective-permute-start.7 = (f32[40,128]{1,0:T(8,128)S(1)}, f32[40,128]{1,0:T(8,128)S(1)}, u32[]{:S(2)}, u32[]{:S(2)}) collective-permute-start(f32[40,128]{1,0:T(8,128)S(1)} %add.1.after_ref.refs_0_), channel_id=1, source_target_pairs={{0,8},{2,10},{4,12},{6,14},{8,0},{10,2},{12,4},{14,6},{1,9},{3,11}... | collective-permute-start | bytes 61448 | tf_op jit(solution)/shard_map/ppermute | solution.py:934
  23.9 2.0 %bases.5.refs_4_ = f32[352,1024]{1,0:T(8,128)S(1)} custom-call(bf16[48,2304]{1,0:T(8,128)(2,1)S(1)} %get-tuple-element.33.highs, bf16[48,2304]{1,0:T(8,128)(2,1)S(1)} %get-tuple-element.34.lows, bf16[704,768]{1,0:T(8,128)(2,1)S(1)} %get-tuple-element.35.weight_ref, f32[40,128]{1,0:T(8,128)S(1)} %add.1.after_ref.refs_0_), custom_call_target="tpu_custom_call" | custom-call | tf_op jit(solution)/shard_map/bases/pallas_call | solution.py:1098
  26.0 0.0 collective-permute-done.7.refs_1_
  26.0 3.4 %model.1 = (f32[1,16,2048]{2,1,0:T(8,128)}, f32[1,64]{1,0:T(1,128)}) custom-call(f32[40,128]{1,0:T(8,128)S(1)} %add.1.after_ref.refs_0_, f32[40,128]{1,0:T(8,128)S(1)} %collective-permute-done.7.refs_1_, f32[352,512]{1,0:T(8,128)S(1)} %get-tuple-element.32.refs_4_.refs_2_, f32[352,512]{1,0:T(8,128)S(1)} %bases.4.refs_5_.refs_3_, ...), custom_call_target="tpu_custom_call" | custom-call | tf_op jit(solution)/shard_map/model/pallas_call | solution.py:1112
  (2 shorter events, 0.0 us)
Async XLA Ops:
  0.6 4.2 %collective-permute-start = (f32[16,1024]{1,0:T(8,128)}, f32[16,1024]{1,0:T(8,128)S(1)}, u32[]{:S(2)}, u32[]{:S(2)}) collective-permute-start(f32[16,1024]{1,0:T(8,128)} %template_hbm.1), channel_id=1, source_target_pairs={{1,0},{0,1},{3,2},{2,3},{5,4},{4,5},{7,6},{6,7},{9,8},{8,9},{11,10... | collective-permute-start | bytes 196616 | tf_op jit(solution)/shard_map/ppermute | solution.py:951
  2.3 5.3 %collective-permute-start.2 = (f32[16,1024]{1,0:T(8,128)S(1)}, f32[16,1024]{1,0:T(8,128)S(1)}, u32[]{:S(2)}, u32[]{:S(2)}) collective-permute-start(f32[16,1024]{1,0:T(8,128)S(1)} %near.1), channel_id=1, source_target_pairs={{0,2},{4,6},{8,10},{12,14},{2,0},{6,4},{10,8},{14,12},{1,3},{5,7},... | collective-permute-start | bytes 196616 | tf_op jit(solution)/shard_map/ppermute | solution.py:990
  4.9 6.9 %collective-permute-start.1 = (f32[24,1024]{1,0:T(8,128)S(1)}, f32[24,1024]{1,0:T(8,128)S(1)}, u32[]{:S(2)}, u32[]{:S(2)}) collective-permute-start(f32[24,1024]{1,0:T(8,128)S(1)} %far.1), channel_id=1, source_target_pairs={{2,4},{6,8},{10,12},{4,2},{8,6},{12,10},{3,5},{7,9},{11,13},{5,3},... | collective-permute-start | bytes 294920 | tf_op jit(solution)/shard_map/ppermute | solution.py:990
  7.6 1.3 %collective-permute-start.3 = (f32[16,1024]{1,0:T(8,128)S(1)}, f32[16,1024]{1,0:T(8,128)S(1)}, u32[]{:S(2)}, u32[]{:S(2)}) collective-permute-start(f32[16,1024]{1,0:T(8,128)S(1)} %collective-permute-done.2.refs_2_), channel_id=1, source_target_pairs={{1,0},{0,1},{3,2},{2,3},{5,4},{4,5},{7,6},{6,7},{9,8},{8,9},{11,10... | collective-permute-start | bytes 196616 | tf_op jit(solution)/shard_map/ppermute | solution.py:951
  13.6 6.9 %collective-permute-start.6 = (f32[40,128]{1,0:T(8,128)S(1)}, f32[40,128]{1,0:T(8,128)S(1)}, u32[]{:S(2)}, u32[]{:S(2)}) collective-permute-start(f32[40,128]{1,0:T(8,128)S(1)} %late.1.refs_5_.after_ref.refs_0_), channel_id=1, source_target_pairs={{0,2},{2,0},{4,6},{6,4},{8,10},{10,8},{12,14},{14,12},{1,3},{3,1},... | collective-permute-start | bytes 61448 | tf_op jit(solution)/shard_map/ppermute | solution.py:934
  16.0 4.7 %collective-permute-start.5 = (f32[40,128]{1,0:T(8,128)S(1)}, f32[40,128]{1,0:T(8,128)S(1)}, u32[]{:S(2)}, u32[]{:S(2)}) collective-permute-start(f32[40,128]{1,0:T(8,128)S(1)} %late.1.refs_5_.after_ref.refs_0_), channel_id=1, source_target_pairs={{0,6},{2,4},{4,2},{6,0},{8,14},{10,12},{12,10},{14,8},{1,7},{3,5},... | collective-permute-start | bytes 61448 | tf_op jit(solution)/shard_map/ppermute | solution.py:934
  17.5 3.8 %collective-permute-start.4 = (f32[40,128]{1,0:T(8,128)S(1)}, f32[40,128]{1,0:T(8,128)S(1)}, u32[]{:S(2)}, u32[]{:S(2)}) collective-permute-start(f32[40,128]{1,0:T(8,128)S(1)} %late.1.refs_5_.after_ref.refs_0_), channel_id=1, source_target_pairs={{0,4},{2,6},{4,0},{6,2},{8,12},{10,14},{12,8},{14,10},{1,5},{3,7},... | collective-permute-start | bytes 61448 | tf_op jit(solution)/shard_map/ppermute | solution.py:934
  21.3 4.7 %collective-permute-start.7 = (f32[40,128]{1,0:T(8,128)S(1)}, f32[40,128]{1,0:T(8,128)S(1)}, u32[]{:S(2)}, u32[]{:S(2)}) collective-permute-start(f32[40,128]{1,0:T(8,128)S(1)} %add.1.after_ref.refs_0_), channel_id=1, source_target_pairs={{0,8},{2,10},{4,12},{6,14},{8,0},{10,2},{12,4},{14,6},{1,9},{3,11}... | collective-permute-start | bytes 61448 | tf_op jit(solution)/shard_map/ppermute | solution.py:934

commit v8 on v6

--- a/solution.py
+++ b/solution.py
@@ -609,7 +609,11 @@
                 rows * stripes,
             )
         )
-    own = total_ref[:, :FIT_ROWS] + gram(designs)
+    middle = width // 2
+    own = total_ref[:, :FIT_ROWS] + (
+        gram([design[:, :middle] for design in designs])
+        + gram([design[:, middle:] for design in designs])
+    )
     out_ref[...] = packed_normal(own)
 
 

time: 29.5 us -> 29.5 us (level)
  no operation moved by 1% of the time
where the time goes in v8:
time: 29.5 us; the launch traced here: 29.3 us
  Pallas kernels  14.9 us (51%)
  starting transfers between devices  10.4 us (35%)
  waiting for transfers between devices  3.31 us (11%)
  between operations  0.73 us (2%)
    ppermute x4, starting transfers between devices, summed(): lax.ppermute(values, axis, [(i, i ^ step) for i in range(count)])  6.64 us
    pallas_call x1, Pallas kernels, shards(): pl.pallas_call(functools.partial(model_kernel, stripes), out_shape=(jax.S...  3.3 us
    ppermute x2, starting transfers between devices, swapped(): lax.ppermute(values, 'stripe', couples + [(b, a) for a, b in couples])  3.23 us
    pallas_call x2, Pallas kernels, next_bases(): pl.pallas_call(functools.partial(next_bases_kernel, cuts[cut]), out_shape...  3.21 us
    pallas_call x1, Pallas kernels, shards(): pl.pallas_call(functools.partial(early_kernel, cores, stripes), out_shape...  2.97 us
    ppermute x2, waiting for transfers between devices, swapped(): lax.ppermute(values, 'stripe', couples + [(b, a) for a, b in couples])  2.01 us
    pallas_call x1, Pallas kernels, shards(): pl.pallas_call(functools.partial(late_kernel, stripes, rows), out_shape=j...  1.78 us
    pallas_call x1, Pallas kernels, first_bases(): pl.pallas_call(functools.partial(first_bases_kernel, cores), out_shape=(w...  1.68 us
  transfers between devices with their start and end apart: 8, of which 5 were waited for; matrix products, arithmetic and copies ran while one was open for 0% of the time, Pallas kernels for 34%

profile of v8, /device:TPU:0, one launch (start us, length us, event | category | flops | bytes accessed | tf_op | source)
XLA Modules:
  0.0 29.3 jit_solution(6990331476406900770)
XLA Ops:
  0.6 0.5 %collective-permute-start = (f32[16,1024]{1,0:T(8,128)}, f32[16,1024]{1,0:T(8,128)S(1)}, u32[]{:S(2)}, u32[]{:S(2)}) collective-permute-start(f32[16,1024]{1,0:T(8,128)} %template_hbm.1), channel_id=1, source_target_pairs={{1,0},{0,1},{3,2},{2,3},{5,4},{4,5},{7,6},{6,7},{9,8},{8,9},{11,10... | collective-permute-start | bytes 196616 | tf_op jit(solution)/shard_map/ppermute | solution.py:938
  1.1 1.1 %load.1 = (f32[16,1024]{1,0:T(8,128)S(1)}, f32[1,16,2048]{2,1,0:T(8,128)S(1)}, f32[1,16,2048]{2,1,0:T(8,128)S(1)}, f32[19,19]{1,0:T(8,128)S(1)}, f32[19,19]{1,0:T(8,128)S(1)}, /*index=5*/s32[16,128]{1,0:T(8,128)S(1)}) custom-call(f32[16,1024]{1,0:T(8,128)} %template_hbm.1, f32[1,16,2048]{2,1,0:T(8,128)} %science_hbm.1, s32[1,16,2048]{2,1,0:T(8,128)} %good_hbm.1, ...), custom_call_target="tpu_custom_call" | custom-call | tf_op jit(solution)/shard_map/load/pallas_call | solution.py:952
  2.3 2.6 %collective-permute-start.2 = (f32[16,1024]{1,0:T(8,128)S(1)}, f32[16,1024]{1,0:T(8,128)S(1)}, u32[]{:S(2)}, u32[]{:S(2)}) collective-permute-start(f32[16,1024]{1,0:T(8,128)S(1)} %near.1), channel_id=1, source_target_pairs={{0,2},{4,6},{8,10},{12,14},{2,0},{6,4},{10,8},{14,12},{1,3},{5,7},... | collective-permute-start | bytes 196616 | tf_op jit(solution)/shard_map/ppermute | solution.py:977
  4.8 0.0 collective-permute-done.refs_1_
  4.8 0.1 far.1
  4.9 0.7 %collective-permute-start.1 = (f32[24,1024]{1,0:T(8,128)S(1)}, f32[24,1024]{1,0:T(8,128)S(1)}, u32[]{:S(2)}, u32[]{:S(2)}) collective-permute-start(f32[24,1024]{1,0:T(8,128)S(1)} %far.1), channel_id=1, source_target_pairs={{2,4},{6,8},{10,12},{4,2},{8,6},{12,10},{3,5},{7,9},{11,13},{5,3},... | collective-permute-start | bytes 294920 | tf_op jit(solution)/shard_map/ppermute | solution.py:977
  5.6 2.0 %collective-permute-done.2.refs_2_ = f32[16,1024]{1,0:T(8,128)S(1)} collective-permute-done((f32[16,1024]{1,0:T(8,128)S(1)}, f32[16,1024]{1,0:T(8,128)S(1)}, u32[]{:S(2)}, u32[]{:S(2)}) %collective-permute-start.2) | collective-permute-done | bytes 65568 | tf_op jit(solution)/shard_map/ppermute | solution.py:977
  7.6 0.0 collective-permute-start.3
  7.6 0.8 %weights.1 = (bf16[768,512]{1,0:T(8,128)(2,1)S(1)}, bf16[448,256]{1,0:T(8,128)(2,1)S(1)}, f32[24,896]{1,0:T(8,128)S(1)}) custom-call(f32[19,19]{1,0:T(8,128)S(1)} %get-tuple-element.23.row_ref, f32[19,19]{1,0:T(8,128)S(1)} %get-tuple-element.24.col_ref), custom_call_target="tpu_custom_call" | custom-call | tf_op jit(solution)/shard_map/weights/pallas_call | solution.py:1002
  8.4 0.4 %collective-permute-done.3.refs_3_ = f32[16,1024]{1,0:T(8,128)S(1)} collective-permute-done((f32[16,1024]{1,0:T(8,128)S(1)}, f32[16,1024]{1,0:T(8,128)S(1)}, u32[]{:S(2)}, u32[]{:S(2)}) %collective-permute-start.3) | collective-permute-done | bytes 65568 | tf_op jit(solution)/shard_map/ppermute | solution.py:938
  8.8 3.0 %early.1 = (f32[72,128]{1,0:T(8,128)S(1)}, f32[216,1024]{1,0:T(8,128)S(1)}, f32[40,1024]{1,0:T(8,128)S(1)}, f32[24,1024]{1,0:T(8,128)S(1)}) custom-call(f32[16,1024]{1,0:T(8,128)S(1)} %get-tuple-element.19.refs_0_.template_ref, f32[16,1024]{1,0:T(8,128)S(1)} %collective-permute-done.refs_1_, f32[16,1024]{1,0:T(8,128)S(1)} %collective-permute-done.2.refs_2_, ...), custom_call_target="tpu_custom_call" | custom-call | tf_op jit(solution)/shard_map/early/pallas_call | solution.py:1018
  11.8 0.0 collective-permute-done.1.refs_0_.refs_2_.refs_3_
  11.8 1.8 %late.1.refs_5_.after_ref.refs_0_ = f32[40,128]{1,0:T(8,128)S(1)} custom-call(f32[24,1024]{1,0:T(8,128)S(1)} %collective-permute-done.1.refs_0_.refs_2_.refs_3_, s32[16,128]{1,0:T(8,128)S(1)} %get-tuple-element.22.refs_6_.refs_1_, bf16[448,256]{1,0:T(8,128)(2,1)S(1)} %get-tuple-element.25.refs_2_, f32[72,128]{1,0:T(8,128)S(1)} %get-tuple-element.27.refs_3_, ...), custom_call_target="tpu_custom_call" | custom-call | tf_op jit(solution)/shard_map/late/pallas_call | solution.py:1037
  13.6 2.4 %collective-permute-start.6 = (f32[40,128]{1,0:T(8,128)S(1)}, f32[40,128]{1,0:T(8,128)S(1)}, u32[]{:S(2)}, u32[]{:S(2)}) collective-permute-start(f32[40,128]{1,0:T(8,128)S(1)} %late.1.refs_5_.after_ref.refs_0_), channel_id=1, source_target_pairs={{0,2},{2,0},{4,6},{6,4},{8,10},{10,8},{12,14},{14,12},{1,3},{3,1},... | collective-permute-start | bytes 61448 | tf_op jit(solution)/shard_map/ppermute | solution.py:926
  16.0 1.5 %collective-permute-start.5 = (f32[40,128]{1,0:T(8,128)S(1)}, f32[40,128]{1,0:T(8,128)S(1)}, u32[]{:S(2)}, u32[]{:S(2)}) collective-permute-start(f32[40,128]{1,0:T(8,128)S(1)} %late.1.refs_5_.after_ref.refs_0_), channel_id=1, source_target_pairs={{0,6},{2,4},{4,2},{6,0},{8,14},{10,12},{12,10},{14,8},{1,7},{3,5},... | collective-permute-start | bytes 61448 | tf_op jit(solution)/shard_map/ppermute | solution.py:926
  17.5 0.1 collective-permute-start.4
  17.6 1.7 %bases.3 = (bf16[704,768]{1,0:T(8,128)(2,1)S(1)}, bf16[48,2304]{1,0:T(8,128)(2,1)S(1)}, bf16[48,2304]{1,0:T(8,128)(2,1)S(1)}, f32[352,512]{1,0:T(8,128)S(1)}) custom-call(f32[16,1024]{1,0:T(8,128)S(1)} %get-tuple-element.19.refs_0_.template_ref, f32[16,1024]{1,0:T(8,128)S(1)} %collective-permute-done.refs_1_, ...), custom_call_target="tpu_custom_call" | custom-call | tf_op jit(solution)/shard_map/bases/pallas_call | solution.py:1064
  19.3 1.2 %bases.4.refs_5_.refs_1_ = f32[352,512]{1,0:T(8,128)S(1)} custom-call(bf16[48,2304]{1,0:T(8,128)(2,1)S(1)} %get-tuple-element.33.highs, bf16[48,2304]{1,0:T(8,128)(2,1)S(1)} %get-tuple-element.34.lows, bf16[704,768]{1,0:T(8,128)(2,1)S(1)} %get-tuple-element.35.weight_ref, f32[40,128]{1,0:T(8,128)S(1)} %late.1.refs_5_.after_ref.refs_0_), custom_call_target="tpu_custom_call" | custom-call | tf_op jit(solution)/shard_map/bases/pallas_call | solution.py:1085
  20.5 0.0 collective-permute-done.6.refs_3_
  20.5 0.2 collective-permute-done.5.refs_2_
  20.7 0.6 %collective-permute-done.4.refs_1_ = f32[40,128]{1,0:T(8,128)S(1)} collective-permute-done((f32[40,128]{1,0:T(8,128)S(1)}, f32[40,128]{1,0:T(8,128)S(1)}, u32[]{:S(2)}, u32[]{:S(2)}) %collective-permute-start.4) | collective-permute-done | bytes 20512 | tf_op jit(solution)/shard_map/ppermute | solution.py:926
  21.3 2.6 %collective-permute-start.7 = (f32[40,128]{1,0:T(8,128)S(1)}, f32[40,128]{1,0:T(8,128)S(1)}, u32[]{:S(2)}, u32[]{:S(2)}) collective-permute-start(f32[40,128]{1,0:T(8,128)S(1)} %add.2.after_ref.refs_0_), channel_id=1, source_target_pairs={{0,8},{2,10},{4,12},{6,14},{8,0},{10,2},{12,4},{14,6},{1,9},{3,11}... | collective-permute-start | bytes 61448 | tf_op jit(solution)/shard_map/ppermute | solution.py:926
  23.9 2.0 %bases.5.refs_2_ = f32[352,1024]{1,0:T(8,128)S(1)} custom-call(bf16[48,2304]{1,0:T(8,128)(2,1)S(1)} %get-tuple-element.33.highs, bf16[48,2304]{1,0:T(8,128)(2,1)S(1)} %get-tuple-element.34.lows, bf16[704,768]{1,0:T(8,128)(2,1)S(1)} %get-tuple-element.35.weight_ref, f32[40,128]{1,0:T(8,128)S(1)} %add.2.after_ref.refs_0_), custom_call_target="tpu_custom_call" | custom-call | tf_op jit(solution)/shard_map/bases/pallas_call | solution.py:1085
  26.0 0.1 collective-permute-done.7.refs_1_
  26.0 3.3 %model.1 = (f32[1,16,2048]{2,1,0:T(8,128)}, f32[1,64]{1,0:T(1,128)}) custom-call(f32[40,128]{1,0:T(8,128)S(1)} %add.3.normal_ref, f32[352,512]{1,0:T(8,128)S(1)} %get-tuple-element.32.refs_4_.refs_0_, f32[352,512]{1,0:T(8,128)S(1)} %bases.4.refs_5_.refs_1_, f32[352,1024]{1,0:T(8,128)S(1)} %bases.5.refs_2_, ...), custom_call_target="tpu_custom_call" | custom-call | tf_op jit(solution)/shard_map/model/pallas_call | solution.py:1099
  (3 shorter events, 0.0 us)
Async XLA Ops:
  0.6 4.2 %collective-permute-start = (f32[16,1024]{1,0:T(8,128)}, f32[16,1024]{1,0:T(8,128)S(1)}, u32[]{:S(2)}, u32[]{:S(2)}) collective-permute-start(f32[16,1024]{1,0:T(8,128)} %template_hbm.1), channel_id=1, source_target_pairs={{1,0},{0,1},{3,2},{2,3},{5,4},{4,5},{7,6},{6,7},{9,8},{8,9},{11,10... | collective-permute-start | bytes 196616 | tf_op jit(solution)/shard_map/ppermute | solution.py:938
  2.3 5.3 %collective-permute-start.2 = (f32[16,1024]{1,0:T(8,128)S(1)}, f32[16,1024]{1,0:T(8,128)S(1)}, u32[]{:S(2)}, u32[]{:S(2)}) collective-permute-start(f32[16,1024]{1,0:T(8,128)S(1)} %near.1), channel_id=1, source_target_pairs={{0,2},{4,6},{8,10},{12,14},{2,0},{6,4},{10,8},{14,12},{1,3},{5,7},... | collective-permute-start | bytes 196616 | tf_op jit(solution)/shard_map/ppermute | solution.py:977
  4.9 6.9 %collective-permute-start.1 = (f32[24,1024]{1,0:T(8,128)S(1)}, f32[24,1024]{1,0:T(8,128)S(1)}, u32[]{:S(2)}, u32[]{:S(2)}) collective-permute-start(f32[24,1024]{1,0:T(8,128)S(1)} %far.1), channel_id=1, source_target_pairs={{2,4},{6,8},{10,12},{4,2},{8,6},{12,10},{3,5},{7,9},{11,13},{5,3},... | collective-permute-start | bytes 294920 | tf_op jit(solution)/shard_map/ppermute | solution.py:977
  7.6 1.3 %collective-permute-start.3 = (f32[16,1024]{1,0:T(8,128)S(1)}, f32[16,1024]{1,0:T(8,128)S(1)}, u32[]{:S(2)}, u32[]{:S(2)}) collective-permute-start(f32[16,1024]{1,0:T(8,128)S(1)} %collective-permute-done.2.refs_2_), channel_id=1, source_target_pairs={{1,0},{0,1},{3,2},{2,3},{5,4},{4,5},{7,6},{6,7},{9,8},{8,9},{11,10... | collective-permute-start | bytes 196616 | tf_op jit(solution)/shard_map/ppermute | solution.py:938
  13.6 6.9 %collective-permute-start.6 = (f32[40,128]{1,0:T(8,128)S(1)}, f32[40,128]{1,0:T(8,128)S(1)}, u32[]{:S(2)}, u32[]{:S(2)}) collective-permute-start(f32[40,128]{1,0:T(8,128)S(1)} %late.1.refs_5_.after_ref.refs_0_), channel_id=1, source_target_pairs={{0,2},{2,0},{4,6},{6,4},{8,10},{10,8},{12,14},{14,12},{1,3},{3,1},... | collective-permute-start | bytes 61448 | tf_op jit(solution)/shard_map/ppermute | solution.py:926
  16.0 4.7 %collective-permute-start.5 = (f32[40,128]{1,0:T(8,128)S(1)}, f32[40,128]{1,0:T(8,128)S(1)}, u32[]{:S(2)}, u32[]{:S(2)}) collective-permute-start(f32[40,128]{1,0:T(8,128)S(1)} %late.1.refs_5_.after_ref.refs_0_), channel_id=1, source_target_pairs={{0,6},{2,4},{4,2},{6,0},{8,14},{10,12},{12,10},{14,8},{1,7},{3,5},... | collective-permute-start | bytes 61448 | tf_op jit(solution)/shard_map/ppermute | solution.py:926
  17.5 3.8 %collective-permute-start.4 = (f32[40,128]{1,0:T(8,128)S(1)}, f32[40,128]{1,0:T(8,128)S(1)}, u32[]{:S(2)}, u32[]{:S(2)}) collective-permute-start(f32[40,128]{1,0:T(8,128)S(1)} %late.1.refs_5_.after_ref.refs_0_), channel_id=1, source_target_pairs={{0,4},{2,6},{4,0},{6,2},{8,12},{10,14},{12,8},{14,10},{1,5},{3,7},... | collective-permute-start | bytes 61448 | tf_op jit(solution)/shard_map/ppermute | solution.py:926
  21.3 4.7 %collective-permute-start.7 = (f32[40,128]{1,0:T(8,128)S(1)}, f32[40,128]{1,0:T(8,128)S(1)}, u32[]{:S(2)}, u32[]{:S(2)}) collective-permute-start(f32[40,128]{1,0:T(8,128)S(1)} %add.2.after_ref.refs_0_), channel_id=1, source_target_pairs={{0,8},{2,10},{4,12},{6,14},{8,0},{10,2},{12,4},{14,6},{1,9},{3,11}... | collective-permute-start | bytes 61448 | tf_op jit(solution)/shard_map/ppermute | solution.py:926
